TPU v7x, 32 devices: a whole 2x2x4 slice. The times are simulated.
32 devices in a mesh: row: 2 (over core), col: 16 (over z, y, x).
Axes of the slice: x: 2, y: 2, z: 4, core: 2. Of those that a mesh axis runs over, the one named last changes fastest.
Arguments:
- features: bfloat16 [16384, 128], P(('row', 'col')), may hold values from -6 to 6
- weight: bfloat16 [128, 128], replicated, may hold values from -0.5 to 0.5
- bias: float32 [128], replicated, may hold values from -3 to 3
- cotangent: bfloat16 [16384, 128], P(('row', 'col')), may hold values from -6 to 6
- block_count: int32 [2, 16], P('row', 'col'), may hold values from 64 to 512
- block_rows: int32 [2, 16, 512], P('row', 'col'), may hold values from 0 to 63
- block_cols: int32 [2, 16, 512], P('row', 'col'), may hold values from 0 to 7
- edge_offsets: int32 [2, 16, 512, 128], P('row', 'col'), may hold values from 0 to 16383, as said below
- edge_weight: bfloat16 [2, 16, 512, 128], P('row', 'col'), may hold values from 0.0099487305 to 0.099609375
Outputs:
- output: bfloat16 [16384, 128], P(('row', 'col'))
- grad_features: bfloat16 [16384, 128], P(('row', 'col'))
- grad_weight: float32 [128, 128], replicated
- grad_bias: float32 [128], replicated
Inputs may be any that keep to these rules, and one draw needn't show every extreme that they name: `edge_offsets`: the offsets within one slot are distinct.
All inputs are finite; a program needn't handle non-finite values.
Results may differ from a plain program's by a relative error of at most 0.013.
The roundings to bfloat16 on the way count: a program that leaves them out, or rounds other values in their place, can miss the bound.
Values may be sent and summed in bfloat16 or wider, within the bound.
No kernel may reach another device: no remote copies, remote signals or barrier semaphores. Data moves between devices by JAX's collectives and lax.ppermute only.
A program may use at most 128 MiB of HBM per device.

v0:
```python
import functools
import jax
import jax.numpy as jnp
from jax import lax
from jax.experimental import pallas as pl
from jax.experimental.pallas import tpu as pltpu
from jax.sharding import PartitionSpec as P


def swap(x, axis, bit):
    n = lax.axis_size(axis)
    return lax.ppermute(x, axis, [(i, i ^ bit) for i in range(n)])


def bits_of(axis):
    n = lax.axis_size(axis)
    return [1 << k for k in range(n.bit_length() - 1)]


def scatter_sum(x, axis):
    for bit in bits_of(axis):
        pairs = x.reshape((x.shape[0] // 2, 2) + x.shape[1:])
        x = pairs[:, 0] + swap(pairs[:, 1], axis, bit)
    return x[0]


def gather_relative(x, axis):
    x = x[None]
    for bit in reversed(bits_of(axis)):
        x = jnp.stack([x, swap(x, axis, bit)], axis=1)
        x = x.reshape((x.shape[0] * 2,) + x.shape[2:])
    return x


def total_sum(x, axes):
    for axis in axes:
        for bit in bits_of(axis):
            x = x + swap(x, axis, bit)
    return x


GROUP = 8


def forward_kernel(meta, order, dst, col, offs, wts, panel, totals, dense, dbuf, sems):
    turns = meta[0]
    rows = lax.broadcasted_iota(jnp.int32, (128, 128), 0)
    totals[...] = jnp.zeros_like(totals)

    def out_copy(i, slot):
        return pltpu.make_async_copy(
            dbuf.at[slot], dense.at[pl.ds(i * GROUP, GROUP)], sems.at[slot]
        )

    def turn(i, _):
        slot = lax.rem(i, 2)

        @pl.when(i >= 2)
        def _():
            out_copy(i - 2, slot).wait()

        for u in range(GROUP):
            p = i * GROUP + u
            s = order[p]
            o = offs[pl.ds(s, 1), :]
            w = wts[pl.ds(s, 1), :]
            left = jnp.where(rows == (o >> 7), w, 0.0).astype(jnp.bfloat16)
            right = jnp.where(rows == (o & 127), 1.0, 0.0).astype(jnp.bfloat16)
            block = lax.dot_general(
                left, right, (((1,), (1,)), ((), ())), preferred_element_type=jnp.float32
            ).astype(jnp.bfloat16)
            dbuf[slot, u] = block
            totals[dst[p]] += jnp.dot(block, panel[col[p]], preferred_element_type=jnp.float32)
        out_copy(i, slot).start()
        return 0

    lax.fori_loop(0, turns, turn, 0)

    @pl.when(turns >= 2)
    def _():
        out_copy(turns - 2, lax.rem(turns, 2)).wait()

    @pl.when(turns >= 1)
    def _():
        out_copy(turns - 1, lax.rem(turns + 1, 2)).wait()


def backward_kernel(meta, src, col, grad, dense, acc, dbuf, sems):
    turns = meta[0]
    acc[...] = jnp.zeros_like(acc)

    def in_copy(i, slot):
        return pltpu.make_async_copy(
            dense.at[pl.ds(i * GROUP, GROUP)], dbuf.at[slot], sems.at[slot]
        )

    for k in range(2):

        @pl.when(turns > k)
        def _():
            in_copy(k, k).start()

    def turn(i, _):
        slot = lax.rem(i, 3)

        @pl.when(i + 2 < turns)
        def _():
            in_copy(i + 2, lax.rem(i + 2, 3)).start()

        in_copy(i, slot).wait()
        for u in range(GROUP):
            p = i * GROUP + u
            acc[col[p]] += jnp.dot(
                grad[src[p]], dbuf[slot, u], preferred_element_type=jnp.float32
            )
        return 0

    lax.fori_loop(0, turns, turn, 0)


SMEM = pl.BlockSpec(memory_space=pltpu.SMEM)
VMEM = pl.BlockSpec(memory_space=pltpu.VMEM)
HBM = pl.BlockSpec(memory_space=pl.ANY)
LIMIT = 40 * 1024 * 1024


def run_forward(meta, order, dst, col, offs, wts, panel, row_blocks):
    slots = order.shape[0]
    width = panel.shape[-1]
    return pl.pallas_call(
        forward_kernel,
        out_shape=(
            jax.ShapeDtypeStruct((row_blocks, 128, width), jnp.float32),
            jax.ShapeDtypeStruct((slots, 128, 128), jnp.bfloat16),
        ),
        in_specs=[SMEM, SMEM, SMEM, SMEM, VMEM, VMEM, VMEM],
        out_specs=(VMEM, HBM),
        scratch_shapes=[
            pltpu.VMEM((2, GROUP, 128, 128), jnp.bfloat16),
            pltpu.SemaphoreType.DMA((2,)),
        ],
        compiler_params=pltpu.CompilerParams(vmem_limit_bytes=LIMIT),
    )(meta, order, dst, col, offs, wts, panel)


def run_backward(meta, src, col, grad, dense, col_blocks):
    width = grad.shape[1]
    return pl.pallas_call(
        backward_kernel,
        out_shape=jax.ShapeDtypeStruct((col_blocks, width, 128), jnp.float32),
        in_specs=[SMEM, SMEM, SMEM, VMEM, HBM],
        out_specs=VMEM,
        scratch_shapes=[
            pltpu.VMEM((3, GROUP, 128, 128), jnp.bfloat16),
            pltpu.SemaphoreType.DMA((3,)),
        ],
        compiler_params=pltpu.CompilerParams(vmem_limit_bytes=LIMIT),
    )(meta, src, col, grad, dense)


def shards(
    features,
    weight,
    bias,
    cotangent,
    block_count,
    block_rows,
    block_cols,
    edge_offsets,
    edge_weight,
):
    node_dev, width = features.shape
    n_row = lax.axis_size("row")
    n_col = lax.axis_size("col")
    slots = block_rows.shape[2]
    count = block_count[0, 0]
    mine = lax.axis_index("col")
    per = node_dev // 128
    row_blocks = per * n_col
    col_blocks = per * n_row

    brow = block_rows[0, 0]
    brow = ((brow // per) ^ mine) * per + brow % per
    bcol = block_cols[0, 0]
    ids = jnp.arange(slots, dtype=jnp.int32)
    order = jnp.where(ids < count, ids, slots)
    dst = jnp.where(ids < count, brow, 0)
    col = jnp.where(ids < count, bcol, 0)
    meta = ((count + GROUP - 1) // GROUP).reshape(1)
    offs = jnp.pad(edge_offsets[0, 0], ((0, 8), (0, 0)))
    wts = jnp.pad(edge_weight[0, 0].astype(jnp.float32), ((0, 8), (0, 0)))

    panel_in = lax.all_gather(features, "row", axis=0, tiled=True)
    panel = jnp.dot(panel_in, weight, preferred_element_type=jnp.float32).astype(jnp.bfloat16)
    totals, dense = run_forward(
        meta, order, dst, col, offs, wts, panel.reshape(col_blocks, 128, width), row_blocks
    )
    own = scatter_sum(totals.reshape(n_col, node_dev, width), "col")
    pre = own + bias
    output = jnp.maximum(pre, 0.0).astype(jnp.bfloat16)
    grad_own = jnp.where(pre > 0, cotangent.astype(jnp.float32), 0.0).astype(jnp.bfloat16)
    local_bias = jnp.sum(grad_own.astype(jnp.float32), axis=0)
    turned = jnp.swapaxes(grad_own.reshape(per, 128, width), 1, 2)
    grad = gather_relative(turned, "col").reshape(row_blocks, width, 128)

    acc = run_backward(meta, dst, col, grad, dense, col_blocks)
    back = jnp.swapaxes(acc, 1, 2).reshape(col_blocks * 128, width)
    local_weight = lax.dot_general(
        panel_in,
        back.astype(jnp.bfloat16),
        (((0,), (0,)), ((), ())),
        preferred_element_type=jnp.float32,
    )
    local = jnp.concatenate([local_weight, jnp.tile(local_bias[None], (8, 1))], axis=0)
    total = total_sum(local, ("row", "col"))
    mine_row = lax.axis_index("row")
    grad_proj = scatter_sum(
        jnp.stack(
            [
                lax.dynamic_slice_in_dim(back, (mine_row ^ k) * node_dev, node_dev, 0)
                for k in range(n_row)
            ]
        ),
        "row",
    ).astype(jnp.bfloat16)
    grad_features = lax.dot_general(
        grad_proj, weight, (((1,), (1,)), ((), ())), preferred_element_type=jnp.float32
    ).astype(jnp.bfloat16)
    scale = (node_dev * n_row * n_col) ** (-0.5)
    return (
        output,
        grad_features,
        total[: weight.shape[0]] * scale,
        total[weight.shape[0]] * scale,
    )


def solution(mesh):
    return jax.shard_map(
        shards,
        mesh=mesh,
        in_specs=(
            P(("row", "col"), None),
            P(),
            P(),
            P(("row", "col"), None),
            P("row", "col"),
            P("row", "col", None),
            P("row", "col", None),
            P("row", "col", None, None),
            P("row", "col", None, None),
        ),
        out_specs=(P(("row", "col"), None), P(("row", "col"), None), P(), P()),
        check_vma=False,
    )
```

profile of v0, /device:TPU:0, one launch (start us, length us, event | category | flops | bytes accessed | tf_op | source)
XLA Modules:
  0.0 293.9 jit_solution(18223723324610955519)
XLA Ops:
  1.3 2.3 all_gather.3
  3.6 1.0 pad.10.offs
  4.6 0.9 pad_convert_fusion.wts
  7.1 12.4 %shard_map.120 = (f32[64,128,128]{2,1,0:T(8,128)S(1)}, bf16[512,128,128]{2,1,0:T(8,128)(2,1)}) custom-call(s32[1]{0:T(128)} %bitcast.1.meta, s32[512]{0:T(512)S(1)} %get-tuple-element.16.order, s32[512]{0:T(512)S(1)} %get-tuple-element.15.dst.src, s32[512]{0:T(512)S(1)} %fusion.18.col, s32[520,128]{1,0:T(8,128)S(1)} %pad.10.offs, ...), custom_call_target="tpu_custom_call" | custom-call | tf_op jit(solution)/shard_map/pallas_call | solution.py:130
  19.6 13.7 %collective-permute-start = (f32[8,512,128]{2,1,0:T(8,128)S(1)}, f32[8,512,128]{2,1,0:T(8,128)S(1)}, u32[]{:S(2)}, u32[]{:S(2)}) collective-permute-start(f32[8,512,128]{2,1,0:T(8,128)S(1)} %slice_bitcast_fusion), channel_id=1, source_target_pairs={{0,1},{1,0},{2,3},{3,2},{4,5},{5,4},{6,7},{7,6},{8,9},{9,8},{10,11... | collective-permute-start | bytes 6291464 | tf_op jit(solution)/shard_map/ppermute | solution.py:12
  33.4 27.4 %collective-permute-done = f32[8,512,128]{2,1,0:T(8,128)S(1)} collective-permute-done((f32[8,512,128]{2,1,0:T(8,128)S(1)}, f32[8,512,128]{2,1,0:T(8,128)S(1)}, u32[]{:S(2)}, u32[]{:S(2)}) %collective-permute-start) | collective-permute-done | bytes 2097184 | tf_op jit(solution)/shard_map/ppermute | solution.py:12
  61.6 14.3 %collective-permute-done.1 = f32[4,512,128]{2,1,0:T(8,128)S(1)} collective-permute-done((f32[4,512,128]{2,1,0:T(8,128)S(1)}, f32[4,512,128]{2,1,0:T(8,128)S(1)}, u32[]{:S(2)}, u32[]{:S(2)}) %collective-permute-start.1) | collective-permute-done | bytes 1048608 | tf_op jit(solution)/shard_map/ppermute | solution.py:12
  76.2 72.8 %collective-permute-start.2 = (f32[2,512,128]{2,1,0:T(8,128)S(1)}, f32[2,512,128]{2,1,0:T(8,128)S(1)}, u32[]{:S(2)}, u32[]{:S(2)}) collective-permute-start(f32[2,512,128]{2,1,0:T(8,128)S(1)} %slice_bitcast_fusion.4), channel_id=1, source_target_pairs={{0,4},{1,5},{2,6},{3,7},{4,0},{5,1},{6,2},{7,3},{8,12},{9,13},{10,... | collective-permute-start | bytes 1572872 | tf_op jit(solution)/shard_map/ppermute | solution.py:12
  148.9 11.1 %collective-permute-done.2 = f32[2,512,128]{2,1,0:T(8,128)S(1)} collective-permute-done((f32[2,512,128]{2,1,0:T(8,128)S(1)}, f32[2,512,128]{2,1,0:T(8,128)S(1)}, u32[]{:S(2)}, u32[]{:S(2)}) %collective-permute-start.2) | collective-permute-done | bytes 524320 | tf_op jit(solution)/shard_map/ppermute | solution.py:12
  160.1 25.4 %collective-permute-start.3 = (f32[1,512,128]{2,1,0:T(8,128)S(1)}, f32[1,512,128]{2,1,0:T(8,128)S(1)}, u32[]{:S(2)}, u32[]{:S(2)}) collective-permute-start(f32[1,512,128]{2,1,0:T(8,128)S(1)} %slice_bitcast_fusion.8), channel_id=1, source_target_pairs={{0,8},{1,9},{2,10},{3,11},{4,12},{5,13},{6,14},{7,15},{8,0},{9,1},... | collective-permute-start | bytes 786440 | tf_op jit(solution)/shard_map/ppermute | solution.py:12
  185.5 10.7 %collective-permute-done.3 = f32[1,512,128]{2,1,0:T(8,128)S(1)} collective-permute-done((f32[1,512,128]{2,1,0:T(8,128)S(1)}, f32[1,512,128]{2,1,0:T(8,128)S(1)}, u32[]{:S(2)}, u32[]{:S(2)}) %collective-permute-start.3) | collective-permute-done | bytes 262176 | tf_op jit(solution)/shard_map/ppermute | solution.py:12
  197.2 8.6 %collective-permute-done.4 = bf16[1,4,128,128]{3,2,1,0:T(8,128)(2,1)S(1)} collective-permute-done((bf16[1,4,128,128]{3,2,1,0:T(8,128)(2,1)S(1)}, bf16[1,4,128,128]{3,2,1,0:T(8,128)(2,1)S(1)}, u32[]{:S(2)}, u32[]{:S(2)}) %collective-permute-start.4) | collective-permute-done | bytes 131104 | tf_op jit(solution)/shard_map/ppermute | solution.py:12
  205.9 6.4 %collective-permute-done.5 = bf16[2,4,128,128]{3,2,1,0:T(8,128)(2,1)S(1)} collective-permute-done((bf16[2,4,128,128]{3,2,1,0:T(8,128)(2,1)S(1)}, bf16[2,4,128,128]{3,2,1,0:T(8,128)(2,1)S(1)}, u32[]{:S(2)}, u32[]{:S(2)}) %collective-permute-start.5) | collective-permute-done | bytes 262176 | tf_op jit(solution)/shard_map/ppermute | solution.py:12
  212.3 1.2 collective-permute-start.6
  213.5 8.8 %collective-permute-done.6 = bf16[4,4,128,128]{3,2,1,0:T(8,128)(2,1)S(1)} collective-permute-done((bf16[4,4,128,128]{3,2,1,0:T(8,128)(2,1)S(1)}, bf16[4,4,128,128]{3,2,1,0:T(8,128)(2,1)S(1)}, u32[]{:S(2)}, u32[]{:S(2)}) %collective-permute-start.6) | collective-permute-done | bytes 524320 | tf_op jit(solution)/shard_map/ppermute | solution.py:12
  222.6 20.2 %collective-permute-done.7 = bf16[8,4,128,128]{3,2,1,0:T(8,128)(2,1)S(1)} collective-permute-done((bf16[8,4,128,128]{3,2,1,0:T(8,128)(2,1)S(1)}, bf16[8,4,128,128]{3,2,1,0:T(8,128)(2,1)S(1)}, u32[]{:S(2)}, u32[]{:S(2)}) %collective-permute-start.7) | collective-permute-done | bytes 1048608 | tf_op jit(solution)/shard_map/ppermute | solution.py:12
  243.3 4.5 %shard_map.121 = f32[8,128,128]{2,1,0:T(8,128)S(1)} custom-call(s32[1]{0:T(128)} %bitcast.1.meta, s32[512]{0:T(512)S(1)} %get-tuple-element.15.dst.src, s32[512]{0:T(512)S(1)} %fusion.18.col, bf16[64,128,128]{2,1,0:T(8,128)(2,1)S(1)} %bitcast.118, bf16[512,128,128]{2,1,0:T(8,128)(2,1)} %get-tuple-element.7.dense), custom_call_target="tpu_custom_call" | custom-call | tf_op jit(solution)/shard_map/pallas_call | solution.py:148
  248.3 4.1 %collective-permute-start.9 = (f32[136,128]{1,0:T(8,128)S(1)}, f32[136,128]{1,0:T(8,128)S(1)}, u32[]{:S(2)}, u32[]{:S(2)}) collective-permute-start(f32[136,128]{1,0:T(8,128)S(1)} %pad_maximum_fusion.4), channel_id=1, source_target_pairs={{0,16},{16,0},{1,17},{17,1},{2,18},{18,2},{3,19},{19,3},{4,20},{20... | collective-permute-start | bytes 208904 | tf_op jit(solution)/shard_map/ppermute | solution.py:12
  253.4 4.4 %collective-permute-done.10 = f32[136,128]{1,0:T(8,128)S(1)} collective-permute-done((f32[136,128]{1,0:T(8,128)S(1)}, f32[136,128]{1,0:T(8,128)S(1)}, u32[]{:S(2)}, u32[]{:S(2)}) %collective-permute-start.10) | collective-permute-done | bytes 69664 | tf_op jit(solution)/shard_map/ppermute | solution.py:12
  257.9 4.3 %collective-permute-done.11 = f32[136,128]{1,0:T(8,128)S(1)} collective-permute-done((f32[136,128]{1,0:T(8,128)S(1)}, f32[136,128]{1,0:T(8,128)S(1)}, u32[]{:S(2)}, u32[]{:S(2)}) %collective-permute-start.11) | collective-permute-done | bytes 69664 | tf_op jit(solution)/shard_map/ppermute | solution.py:12
  262.2 22.9 %collective-permute-start.12 = (f32[136,128]{1,0:T(8,128)S(1)}, f32[136,128]{1,0:T(8,128)S(1)}, u32[]{:S(2)}, u32[]{:S(2)}) collective-permute-start(f32[136,128]{1,0:T(8,128)S(1)} %add.76), channel_id=1, source_target_pairs={{0,4},{1,5},{2,6},{3,7},{4,0},{5,1},{6,2},{7,3},{8,12},{9,13},{10,... | collective-permute-start | bytes 208904 | tf_op jit(solution)/shard_map/ppermute | solution.py:12
  285.1 2.3 collective-permute-done.12
  287.5 1.0 collective-permute-start.13
  289.3 3.5 %collective-permute-done.13 = f32[136,128]{1,0:T(8,128)S(1)} collective-permute-done((f32[136,128]{1,0:T(8,128)S(1)}, f32[136,128]{1,0:T(8,128)S(1)}, u32[]{:S(2)}, u32[]{:S(2)}) %collective-permute-start.13) | collective-permute-done | bytes 69664 | tf_op jit(solution)/shard_map/ppermute | solution.py:12
  (48 shorter events, 8.2 us)
Async XLA Ops:
  0.6 5.6 %copy-start = (bf16[128,128]{1,0:T(8,128)(2,1)S(1)}, bf16[128,128]{1,0:T(8,128)(2,1)}, u32[]{:S(2)}) copy-start(bf16[128,128]{1,0:T(8,128)(2,1)} %param.10) | copy-start | bytes 98308
  19.6 41.2 %collective-permute-start = (f32[8,512,128]{2,1,0:T(8,128)S(1)}, f32[8,512,128]{2,1,0:T(8,128)S(1)}, u32[]{:S(2)}, u32[]{:S(2)}) collective-permute-start(f32[8,512,128]{2,1,0:T(8,128)S(1)} %slice_bitcast_fusion), channel_id=1, source_target_pairs={{0,1},{1,0},{2,3},{3,2},{4,5},{5,4},{6,7},{7,6},{8,9},{9,8},{10,11... | collective-permute-start | bytes 6291464 | tf_op jit(solution)/shard_map/ppermute | solution.py:12
  61.1 14.9 %collective-permute-start.1 = (f32[4,512,128]{2,1,0:T(8,128)S(1)}, f32[4,512,128]{2,1,0:T(8,128)S(1)}, u32[]{:S(2)}, u32[]{:S(2)}) collective-permute-start(f32[4,512,128]{2,1,0:T(8,128)S(1)} %slice_bitcast_fusion.2), channel_id=1, source_target_pairs={{0,2},{1,3},{2,0},{3,1},{4,6},{5,7},{6,4},{7,5},{8,10},{9,11},{10,... | collective-permute-start | bytes 3145736 | tf_op jit(solution)/shard_map/ppermute | solution.py:12
  76.1 120.1 %copy-start.1 = (bf16[512,128]{1,0:T(8,128)(2,1)S(1)}, bf16[512,128]{1,0:T(8,128)(2,1)}, u32[]{:S(2)}) copy-start(bf16[512,128]{1,0:T(8,128)(2,1)} %param.12) | copy-start | bytes 393220
  76.1 120.1 %copy-start.2 = (f32[128]{0:T(128)S(1)}, f32[128]{0:T(128)}, u32[]{:S(2)}) copy-start(f32[128]{0:T(128)} %param.11) | copy-start | bytes 1540
  76.2 83.8 %collective-permute-start.2 = (f32[2,512,128]{2,1,0:T(8,128)S(1)}, f32[2,512,128]{2,1,0:T(8,128)S(1)}, u32[]{:S(2)}, u32[]{:S(2)}) collective-permute-start(f32[2,512,128]{2,1,0:T(8,128)S(1)} %slice_bitcast_fusion.4), channel_id=1, source_target_pairs={{0,4},{1,5},{2,6},{3,7},{4,0},{5,1},{6,2},{7,3},{8,12},{9,13},{10,... | collective-permute-start | bytes 1572872 | tf_op jit(solution)/shard_map/ppermute | solution.py:12
  160.1 36.1 %collective-permute-start.3 = (f32[1,512,128]{2,1,0:T(8,128)S(1)}, f32[1,512,128]{2,1,0:T(8,128)S(1)}, u32[]{:S(2)}, u32[]{:S(2)}) collective-permute-start(f32[1,512,128]{2,1,0:T(8,128)S(1)} %slice_bitcast_fusion.8), channel_id=1, source_target_pairs={{0,8},{1,9},{2,10},{3,11},{4,12},{5,13},{6,14},{7,15},{8,0},{9,1},... | collective-permute-start | bytes 786440 | tf_op jit(solution)/shard_map/ppermute | solution.py:12
  197.1 8.7 %collective-permute-start.4 = (bf16[1,4,128,128]{3,2,1,0:T(8,128)(2,1)S(1)}, bf16[1,4,128,128]{3,2,1,0:T(8,128)(2,1)S(1)}, u32[]{:S(2)}, u32[]{:S(2)}) collective-permute-start(bf16[1,4,128,128]{3,2,1,0:T(8,128)(2,1)S(1)} %bitcast.134), channel_id=1, source_target_pairs={{0,8},{1,9},{2,10},{3,11},{4,12},{5,13},{6,14},{7,15},{8,0},{9,1},... | collective-permute-start | bytes 393224 | tf_op jit(solution)/shard_map/ppermute | solution.py:12
  205.8 6.4 %collective-permute-start.5 = (bf16[2,4,128,128]{3,2,1,0:T(8,128)(2,1)S(1)}, bf16[2,4,128,128]{3,2,1,0:T(8,128)(2,1)S(1)}, u32[]{:S(2)}, u32[]{:S(2)}) collective-permute-start(bf16[2,4,128,128]{3,2,1,0:T(8,128)(2,1)S(1)} %get-tuple-element.14), channel_id=1, source_target_pairs={{0,4},{1,5},{2,6},{3,7},{4,0},{5,1},{6,2},{7,3},{8,12},{9,13},{10,... | collective-permute-start | bytes 786440 | tf_op jit(solution)/shard_map/ppermute | solution.py:12
  212.3 10.0 %collective-permute-start.6 = (bf16[4,4,128,128]{3,2,1,0:T(8,128)(2,1)S(1)}, bf16[4,4,128,128]{3,2,1,0:T(8,128)(2,1)S(1)}, u32[]{:S(2)}, u32[]{:S(2)}) collective-permute-start(bf16[4,4,128,128]{3,2,1,0:T(8,128)(2,1)S(1)} %bitcast.131), channel_id=1, source_target_pairs={{0,2},{1,3},{2,0},{3,1},{4,6},{5,7},{6,4},{7,5},{8,10},{9,11},{10,... | collective-permute-start | bytes 1572872 | tf_op jit(solution)/shard_map/ppermute | solution.py:12
  222.5 20.3 %collective-permute-start.7 = (bf16[8,4,128,128]{3,2,1,0:T(8,128)(2,1)S(1)}, bf16[8,4,128,128]{3,2,1,0:T(8,128)(2,1)S(1)}, u32[]{:S(2)}, u32[]{:S(2)}) collective-permute-start(bf16[8,4,128,128]{3,2,1,0:T(8,128)(2,1)S(1)} %bitcast.129), channel_id=1, source_target_pairs={{0,1},{1,0},{2,3},{3,2},{4,5},{5,4},{6,7},{7,6},{8,9},{9,8},{10,11... | collective-permute-start | bytes 3145736 | tf_op jit(solution)/shard_map/ppermute | solution.py:12
  248.3 5.0 %collective-permute-start.9 = (f32[136,128]{1,0:T(8,128)S(1)}, f32[136,128]{1,0:T(8,128)S(1)}, u32[]{:S(2)}, u32[]{:S(2)}) collective-permute-start(f32[136,128]{1,0:T(8,128)S(1)} %pad_maximum_fusion.4), channel_id=1, source_target_pairs={{0,16},{16,0},{1,17},{17,1},{2,18},{18,2},{3,19},{19,3},{4,20},{20... | collective-permute-start | bytes 208904 | tf_op jit(solution)/shard_map/ppermute | solution.py:12
  252.5 35.9 %collective-permute-start.8 = (f32[1,512,128]{2,1,0:T(8,128)S(1)}, f32[1,512,128]{2,1,0:T(8,128)S(1)}, u32[]{:S(2)}, u32[]{:S(2)}) collective-permute-start(f32[1,512,128]{2,1,0:T(8,128)S(1)} %slice_bitcast_fusion.6), channel_id=1, source_target_pairs={{0,16},{16,0},{1,17},{17,1},{2,18},{18,2},{3,19},{19,3},{4,20},{20... | collective-permute-start | bytes 786440 | tf_op jit(solution)/shard_map/ppermute | solution.py:12
  253.3 4.5 %collective-permute-start.10 = (f32[136,128]{1,0:T(8,128)S(1)}, f32[136,128]{1,0:T(8,128)S(1)}, u32[]{:S(2)}, u32[]{:S(2)}) collective-permute-start(f32[136,128]{1,0:T(8,128)S(1)} %fusion.22), channel_id=1, source_target_pairs={{0,1},{1,0},{2,3},{3,2},{4,5},{5,4},{6,7},{7,6},{8,9},{9,8},{10,11... | collective-permute-start | bytes 208904 | tf_op jit(solution)/shard_map/ppermute | solution.py:12
  257.8 4.4 %collective-permute-start.11 = (f32[136,128]{1,0:T(8,128)S(1)}, f32[136,128]{1,0:T(8,128)S(1)}, u32[]{:S(2)}, u32[]{:S(2)}) collective-permute-start(f32[136,128]{1,0:T(8,128)S(1)} %add.75), channel_id=1, source_target_pairs={{0,2},{1,3},{2,0},{3,1},{4,6},{5,7},{6,4},{7,5},{8,10},{9,11},{10,... | collective-permute-start | bytes 208904 | tf_op jit(solution)/shard_map/ppermute | solution.py:12
  262.2 25.2 %collective-permute-start.12 = (f32[136,128]{1,0:T(8,128)S(1)}, f32[136,128]{1,0:T(8,128)S(1)}, u32[]{:S(2)}, u32[]{:S(2)}) collective-permute-start(f32[136,128]{1,0:T(8,128)S(1)} %add.76), channel_id=1, source_target_pairs={{0,4},{1,5},{2,6},{3,7},{4,0},{5,1},{6,2},{7,3},{8,12},{9,13},{10,... | collective-permute-start | bytes 208904 | tf_op jit(solution)/shard_map/ppermute | solution.py:12
  287.5 5.3 %collective-permute-start.13 = (f32[136,128]{1,0:T(8,128)S(1)}, f32[136,128]{1,0:T(8,128)S(1)}, u32[]{:S(2)}, u32[]{:S(2)}) collective-permute-start(f32[136,128]{1,0:T(8,128)S(1)} %add.77), channel_id=1, source_target_pairs={{0,8},{1,9},{2,10},{3,11},{4,12},{5,13},{6,14},{7,15},{8,0},{9,1},... | collective-permute-start | bytes 208904 | tf_op jit(solution)/shard_map/ppermute | solution.py:12
where the time goes:
time: 294 us
  starting transfers between devices  142 us (48%)
  waiting for transfers between devices  123 us (42%)
  Pallas kernels  16.8 us (6%)
  other arithmetic  5.09 us (2%)
    ppermute x14, starting transfers between devices, swap(): return lax.ppermute(x, axis, [(i, i ^ bit) for i in range(n)])  142 us
    ppermute x14, waiting for transfers between devices, swap(): return lax.ppermute(x, axis, [(i, i ^ bit) for i in range(n)])  123 us
    pallas_call x1, Pallas kernels, run_forward(): pl.pallas_call(forward_kernel, out_shape=(jax.ShapeDtypeStruct((row_block...  12.4 us
  transfers between devices with their start and end apart: 14, of which 13 were waited for; matrix products, arithmetic and copies ran while one was open for 0% of the time, Pallas kernels for 0%

commit v1 on v0

v1 whole, which is shorter than its diff:
```python
import functools
import jax
import jax.numpy as jnp
from jax import lax
from jax.experimental import pallas as pl
from jax.experimental.pallas import tpu as pltpu
from jax.sharding import PartitionSpec as P


def swap(x, axis, bit):
    n = lax.axis_size(axis)
    return lax.ppermute(x, axis, [(i, i ^ bit) for i in range(n)])


def bits_of(axis):
    n = lax.axis_size(axis)
    return [1 << k for k in range(n.bit_length() - 1)]


def scatter_sum(x, axis):
    for bit in bits_of(axis):
        pairs = x.reshape((x.shape[0] // 2, 2) + x.shape[1:])
        x = pairs[:, 0] + swap(pairs[:, 1], axis, bit)
    return x[0]


def gather_relative(x, axis):
    x = x[None]
    for bit in reversed(bits_of(axis)):
        x = jnp.stack([x, swap(x, axis, bit)], axis=1)
        x = x.reshape((x.shape[0] * 2,) + x.shape[2:])
    return x


def total_sum(x, axes):
    for axis in axes:
        for bit in bits_of(axis):
            x = x + swap(x, axis, bit)
    return x


GROUP = 8
ROOM = 64
SPARE = 8
FIELD = 1 << 16
UNIT = 2.0**-14


def block_of(code, rows):
    o = code >> 16
    w = (code & (FIELD - 1)).astype(jnp.float32) * UNIT
    left = jnp.where(rows == (o >> 7), w, 0.0).astype(jnp.bfloat16)
    right = jnp.where(rows == (o & 127), 1.0, 0.0).astype(jnp.bfloat16)
    return lax.dot_general(
        left, right, (((1,), (1,)), ((), ())), preferred_element_type=jnp.float32
    ).astype(jnp.bfloat16)


def pack_kernel(meta, pos, codes, labels, out):
    out[...] = jnp.zeros_like(out)
    stride = ROOM + SPARE
    for k in range(labels.shape[0]):
        out[pl.ds(k * stride + ROOM, 1), :] = labels[pl.ds(k, 1), :]

    def turn(i, _):
        for u in range(GROUP):
            s = i * GROUP + u
            out[pl.ds(pos[s], 1), :] = codes[pl.ds(s, 1), :]
        return 0

    lax.fori_loop(0, meta[0], turn, 0)


def build_kernel(meta, order, codes, dense, dbuf, sems):
    turns = meta[0]
    rows = lax.broadcasted_iota(jnp.int32, (128, 128), 0)

    def out_copy(i, slot):
        return pltpu.make_async_copy(
            dbuf.at[slot], dense.at[pl.ds(i * GROUP, GROUP)], sems.at[slot]
        )

    def turn(i, _):
        slot = lax.rem(i, 2)

        @pl.when(i >= 2)
        def _():
            out_copy(i - 2, slot).wait()

        lines = [codes[pl.ds(order[i * GROUP + u], 1), :] for u in range(GROUP)]
        blocks = [block_of(line, rows) for line in lines]
        for u in range(GROUP):
            dbuf[slot, u] = blocks[u]
        out_copy(i, slot).start()
        return 0

    lax.fori_loop(0, turns, turn, 0)

    @pl.when(turns >= 2)
    def _():
        out_copy(turns - 2, lax.rem(turns, 2)).wait()

    @pl.when(turns >= 1)
    def _():
        out_copy(turns - 1, lax.rem(turns + 1, 2)).wait()


def forward_kernel(meta, order, col, owner, codes, panel, totals, dbuf):
    turns = meta[0]
    rows = lax.broadcasted_iota(jnp.int32, (128, 128), 0)
    totals[...] = jnp.zeros_like(totals)

    def build(i, slot):
        lines = [codes[pl.ds(order[i * GROUP + u], 1), :] for u in range(GROUP)]
        blocks = [block_of(line, rows) for line in lines]
        for u in range(GROUP):
            dbuf[slot, :, u * 128 : (u + 1) * 128] = blocks[u]

    def product(i, slot):
        right = jnp.concatenate([panel[col[i * GROUP + u]] for u in range(GROUP)], axis=0)
        return jnp.dot(dbuf[slot], right, preferred_element_type=jnp.float32)

    @pl.when(turns > 0)
    def _():
        build(0, 0)

    def turn(i, _):
        slot = lax.rem(i, 2)
        added = product(i, slot)
        build(i + 1, 1 - slot)
        totals[owner[i]] += added
        return 0

    lax.fori_loop(0, turns, turn, 0)


def tile_kernel(meta, order, dst, col, codes, panel, totals):
    rows = lax.broadcasted_iota(jnp.int32, (128, 128), 0)
    totals[...] = jnp.zeros_like(totals)

    def turn(i, _):
        for u in range(GROUP):
            p = i * GROUP + u
            block = block_of(codes[pl.ds(order[p], 1), :], rows)
            totals[dst[p]] += jnp.dot(block, panel[col[p]], preferred_element_type=jnp.float32)
        return 0

    lax.fori_loop(0, meta[0], turn, 0)


def backward_kernel(meta, src, owner, grad, dense, acc, dbuf, sems):
    turns = meta[0]
    acc[...] = jnp.zeros_like(acc)

    def in_copy(i, slot):
        return pltpu.make_async_copy(
            dense.at[pl.ds(i * GROUP, GROUP)], dbuf.at[slot], sems.at[slot]
        )

    for k in range(2):

        @pl.when(turns > k)
        def _():
            in_copy(k, k).start()

    def turn(i, _):
        slot = lax.rem(i, 3)

        @pl.when(i + 2 < turns)
        def _():
            in_copy(i + 2, lax.rem(i + 2, 3)).start()

        in_copy(i, slot).wait()
        left = jnp.concatenate([grad[src[i * GROUP + u]] for u in range(GROUP)], axis=1)
        right = dbuf[slot].reshape(GROUP * 128, 128)
        acc[owner[i]] += jnp.dot(left, right, preferred_element_type=jnp.float32)
        return 0

    lax.fori_loop(0, turns, turn, 0)


SMEM = pl.BlockSpec(memory_space=pltpu.SMEM)
VMEM = pl.BlockSpec(memory_space=pltpu.VMEM)
HBM = pl.BlockSpec(memory_space=pl.ANY)
PARAMS = pltpu.CompilerParams(vmem_limit_bytes=48 * 1024 * 1024)


def cost(slots, products):
    flops = 2 * slots * products * 128**3
    return pl.CostEstimate(flops=flops, bytes_accessed=slots * 128 * 128 * 2, transcendentals=0)


def run_tile(meta, order, dst, col, codes, panel, row_blocks):
    return pl.pallas_call(
        tile_kernel,
        out_shape=jax.ShapeDtypeStruct((row_blocks, 128, panel.shape[-1]), jnp.float32),
        in_specs=[SMEM] * 4 + [VMEM] * 2,
        out_specs=VMEM,
        compiler_params=PARAMS,
    )(meta, order, dst, col, codes, panel)


def run_pack(meta, pos, codes, labels):
    length = labels.shape[0] * (ROOM + SPARE)
    return pl.pallas_call(
        pack_kernel,
        out_shape=jax.ShapeDtypeStruct((length, 128), jnp.int32),
        in_specs=[SMEM] * 2 + [VMEM] * 2,
        out_specs=VMEM,
        compiler_params=PARAMS,
    )(meta, pos, codes, labels)


def run_build(meta, order, codes):
    return pl.pallas_call(
        build_kernel,
        out_shape=jax.ShapeDtypeStruct((order.shape[0], 128, 128), jnp.bfloat16),
        in_specs=[SMEM] * 2 + [VMEM],
        out_specs=HBM,
        scratch_shapes=[
            pltpu.VMEM((2, GROUP, 128, 128), jnp.bfloat16),
            pltpu.SemaphoreType.DMA((2,)),
        ],
        compiler_params=PARAMS,
        cost_estimate=cost(order.shape[0], 4),
    )(meta, order, codes)


def run_forward(meta, order, col, owner, codes, panel, row_blocks):
    return pl.pallas_call(
        forward_kernel,
        out_shape=jax.ShapeDtypeStruct((row_blocks, 128, panel.shape[-1]), jnp.float32),
        in_specs=[SMEM] * 4 + [VMEM] * 2,
        out_specs=VMEM,
        scratch_shapes=[pltpu.VMEM((2, 128, GROUP * 128), jnp.bfloat16)],
        compiler_params=PARAMS,
        cost_estimate=cost(order.shape[0], 8),
    )(meta, order, col, owner, codes, panel)


def run_backward(meta, src, owner, grad, dense, col_blocks):
    return pl.pallas_call(
        backward_kernel,
        out_shape=jax.ShapeDtypeStruct((col_blocks, grad.shape[1], 128), jnp.float32),
        in_specs=[SMEM] * 3 + [VMEM, HBM],
        out_specs=VMEM,
        scratch_shapes=[
            pltpu.VMEM((3, GROUP, 128, 128), jnp.bfloat16),
            pltpu.SemaphoreType.DMA((3,)),
        ],
        compiler_params=PARAMS,
        cost_estimate=cost(src.shape[0], 4),
    )(meta, src, owner, grad, dense)


def grouped(key, live, keys):
    ids = jnp.arange(key.shape[0], dtype=jnp.int32)
    names = jnp.arange(keys, dtype=jnp.int32)
    key = jnp.where(live, key, keys)
    before = (key[None, :] == key[:, None]) & (ids[None, :] < ids[:, None])
    rank = jnp.sum(before.astype(jnp.int32), axis=1)
    counts = jnp.sum((key[None, :] == names[:, None]).astype(jnp.int32), axis=1)
    filled = (counts + GROUP - 1) // GROUP * GROUP
    base = jnp.sum(jnp.where(names[None, :] < key[:, None], filled[None, :], 0), axis=1)
    pos = jnp.where(live, base + rank, -1)
    ends = jnp.sum(jnp.where(names[None, :] <= names[:, None], filled[None, :], 0), axis=1)
    length = key.shape[0] + keys * GROUP
    first = jnp.arange(length // GROUP, dtype=jnp.int32) * GROUP
    group_key = jnp.sum((ends[None, :] <= first[:, None]).astype(jnp.int32), axis=1)
    return pos, jnp.minimum(group_key, keys - 1), jnp.sum(filled) // GROUP, length


def place(pos, value, length, fill):
    spots = jnp.arange(length, dtype=jnp.int32)
    hit = pos[None, :] == spots[:, None]
    return jnp.sum(jnp.where(hit, value[None, :] - fill, 0), axis=1) + fill


def shards(
    features,
    weight,
    bias,
    cotangent,
    block_count,
    block_rows,
    block_cols,
    edge_offsets,
    edge_weight,
):
    node_dev, width = features.shape
    n_row = lax.axis_size("row")
    n_col = lax.axis_size("col")
    slots = block_rows.shape[2]
    count = block_count[0, 0]
    mine = lax.axis_index("col")
    mine_row = lax.axis_index("row")
    per = node_dev // 128
    row_blocks = per * n_col
    col_blocks = per * n_row
    by_owner = n_row * n_col * node_dev * width * 2 <= 8 * 1024 * 1024

    brow = block_rows[0, 0]
    bcol = block_cols[0, 0]
    ids = jnp.arange(slots, dtype=jnp.int32)
    live = ids < count
    codes = edge_offsets[0, 0] * FIELD + (
        edge_weight[0, 0].astype(jnp.float32) * (1.0 / UNIT)
    ).astype(jnp.int32)
    codes = jnp.pad(codes, ((0, 8), (0, 0)))
    home = brow // per
    turns_plain = ((count + GROUP - 1) // GROUP).reshape(1)

    panel_in = lax.all_gather(features, "row", axis=0, tiled=True)

    def tile_plan(panel):
        order = jnp.where(live, ids, slots)
        dst = jnp.where(live, (home ^ mine) * per + brow % per, 0)
        totals = run_tile(turns_plain, order, dst, bcol, codes, panel, row_blocks)
        return scatter_sum(totals.reshape(n_col, node_dev, width), "col")

    if by_owner:
        same = live[None, :] & (home[None, :] == home[:, None]) & (ids[None, :] < ids[:, None])
        rank = jnp.sum(same.astype(jnp.int32), axis=1)
        over = jnp.any(live & (rank >= ROOM)).astype(jnp.int32)
        fits = live & (rank < ROOM)
        label = 1 + (brow % per) * col_blocks + bcol
        labels = place(jnp.where(fits, home * ROOM + rank, -1), label, n_col * ROOM, 0)
        labels = jnp.concatenate(
            [labels.reshape(n_col, ROOM), jnp.full((n_col, 128 - ROOM), over)], axis=1
        )
        stride = ROOM + SPARE
        pos = jnp.where(fits, home * stride + rank, ROOM + SPARE - 1)
        packed = run_pack(turns_plain, pos, codes, labels)
        came = lax.all_to_all(
            packed.reshape(n_col, stride, 128), "col", split_axis=0, concat_axis=0, tiled=True
        )
        spread = total_sum(jnp.max(came[:, ROOM, ROOM:], axis=0)[None], ("row",))
        any_over = jnp.max(spread) > 0

        projected = jnp.dot(features, weight, preferred_element_type=jnp.float32)
        everywhere = gather_relative(
            gather_relative(projected.astype(jnp.bfloat16), "col"), "row"
        )

        got = came[:, ROOM, :ROOM]
        sources = jnp.arange(n_col, dtype=jnp.int32)[:, None]
        places = jnp.arange(ROOM, dtype=jnp.int32)[None, :]
        row_here = ((got - 1) // col_blocks).reshape(-1)
        col_there = (got - 1) % col_blocks
        col_there = (
            ((col_there // per) ^ mine_row) * n_col + (sources ^ mine)
        ) * per + col_there % per
        pos, owner, turns, length = grouped(row_here, (got > 0).reshape(-1), per)
        line = (sources * stride + places).reshape(-1)
        order = place(pos, line, length + GROUP, ROOM + 1)
        cols = place(pos, col_there.reshape(-1), length + GROUP, 0)
        own = run_forward(
            turns.reshape(1),
            order,
            cols,
            owner,
            came.reshape(n_col * stride, 128),
            everywhere.reshape(-1, 128, width),
            per,
        ).reshape(node_dev, width)

        def slow():
            blocks = [
                lax.dynamic_index_in_dim(everywhere[:, 0], mine_row ^ k, 0, keepdims=False)
                for k in range(n_row)
            ]
            return tile_plan(jnp.stack(blocks).reshape(col_blocks, 128, width))

        own = lax.cond(any_over, slow, lambda: own)
    else:
        panel = jnp.dot(panel_in, weight, preferred_element_type=jnp.float32)
        own = tile_plan(panel.astype(jnp.bfloat16).reshape(col_blocks, 128, width))

    pos, back_owner, back_turns, length = grouped(bcol, live, col_blocks)
    back_order = place(pos, ids, length, slots)
    back_src = place(pos, (home ^ mine) * per + brow % per, length, 0)
    back_turns = back_turns.reshape(1)
    dense = run_build(back_turns, back_order, codes)

    pre = own + bias
    output = jnp.maximum(pre, 0.0).astype(jnp.bfloat16)
    grad_own = jnp.where(pre > 0, cotangent.astype(jnp.float32), 0.0).astype(jnp.bfloat16)
    local_bias = jnp.sum(grad_own.astype(jnp.float32), axis=0)
    turned = jnp.swapaxes(grad_own.reshape(per, 128, width), 1, 2)
    grad = gather_relative(turned, "col").reshape(row_blocks, width, 128)

    acc = run_backward(back_turns, back_src, back_owner, grad, dense, col_blocks)
    back = jnp.swapaxes(acc, 1, 2).reshape(col_blocks * 128, width)
    local_weight = lax.dot_general(
        panel_in,
        back.astype(jnp.bfloat16),
        (((0,), (0,)), ((), ())),
        preferred_element_type=jnp.float32,
    )
    local = jnp.concatenate([local_weight, jnp.tile(local_bias[None], (8, 1))], axis=0)
    total = total_sum(local, ("row", "col"))
    grad_proj = scatter_sum(
        jnp.stack(
            [
                lax.dynamic_slice_in_dim(back, (mine_row ^ k) * node_dev, node_dev, 0)
                for k in range(n_row)
            ]
        ),
        "row",
    ).astype(jnp.bfloat16)
    grad_features = lax.dot_general(
        grad_proj, weight, (((1,), (1,)), ((), ())), preferred_element_type=jnp.float32
    ).astype(jnp.bfloat16)
    scale = (node_dev * n_row * n_col) ** (-0.5)
    return (
        output,
        grad_features,
        total[: weight.shape[0]] * scale,
        total[weight.shape[0]] * scale,
    )


def solution(mesh):
    return jax.shard_map(
        shards,
        mesh=mesh,
        in_specs=(
            P(("row", "col"), None),
            P(),
            P(),
            P(("row", "col"), None),
            P("row", "col"),
            P("row", "col", None),
            P("row", "col", None),
            P("row", "col", None, None),
            P("row", "col", None, None),
        ),
        out_specs=(P(("row", "col"), None), P(("row", "col"), None), P(), P()),
        check_vma=False,
    )
```

time: 294 us -> 213 us (0.72)
  starting transfers between devices: 142 us -> 25.1 us
  Pallas kernels: 16.8 us -> 80.3 us
  waiting for transfers between devices: 123 us -> 73.2 us
  other arithmetic: 5.09 us -> 16.3 us
  between operations: 1.57 us -> 8.24 us
    ppermute x14 -> x16, starting transfers between devices: 142 us -> 18.3 us  [swap(): return lax.ppermute(x, axis, [(i, i ^ bit) for i in range(n)])]
    ppermute x14 -> x16, waiting for transfers between devices: 123 us -> 60.1 us  [swap(): return lax.ppermute(x, axis, [(i, i ^ bit) for i in range(n)])]
    pallas_call x1 -> x3, Pallas kernels: 12.4 us -> 51.5 us  [the longest x1 35.3 us: run_build(): pl.pallas_call(build_kernel, out_shape=jax.ShapeDtypeStruct((order.shape[...]
    pallas_call x1, Pallas kernels: 4.48 us -> 28.8 us  [run_backward(): pl.pallas_call(backward_kernel, out_shape=jax.ShapeDtypeStruct((col_block...]
    all_to_all x0 -> x1, waiting for transfers between devices: none -> 13.1 us  [shards(): lax.all_to_all(packed.reshape(n_col, stride, 128), 'col', split_axis=0, c...]
    all_to_all x0 -> x1, starting transfers between devices: none -> 6.83 us  [shards(): lax.all_to_all(packed.reshape(n_col, stride, 128), 'col', split_axis=0, c...]
    another operation x4 -> x9, other arithmetic: 0.38 us -> 5.89 us  [gather_relative(): x = jnp.stack([x, swap(x, axis, bit)], axis=1)]
    reduce_sum x0 -> x16, other arithmetic: none -> 5.12 us  [the longest x3 1.99 us: place(): return jnp.sum(jnp.where(hit, value[None, :] - fill, 0), axis=1) + fill]
  transfers between devices with their start and end apart: 14 -> 17, of which waited for: 13 -> 13; matrix products, arithmetic and copies ran while one was open for 0% -> 5% of each run, Pallas kernels for 0% -> 18%
where the time goes in v1:
time: 213 us; the launch traced here: 211 us
  Pallas kernels  80.3 us (38%)
  waiting for transfers between devices  73.2 us (34%)
  starting transfers between devices  25.1 us (12%)
  other arithmetic  16.3 us (8%)
  between operations  8.24 us (4%)
  local copies, waits for them, and re-layouts  3.25 us (2%)
  matrix products  2.2 us (1%)
    ppermute x16, waiting for transfers between devices, swap(): return lax.ppermute(x, axis, [(i, i ^ bit) for i in range(n)])  60.1 us
    pallas_call x1, Pallas kernels, run_build(): pl.pallas_call(build_kernel, out_shape=jax.ShapeDtypeStruct((order.shape[...  35.3 us
    pallas_call x1, Pallas kernels, run_backward(): pl.pallas_call(backward_kernel, out_shape=jax.ShapeDtypeStruct((col_block...  28.8 us
    ppermute x16, starting transfers between devices, swap(): return lax.ppermute(x, axis, [(i, i ^ bit) for i in range(n)])  18.3 us
    pallas_call x1, Pallas kernels, run_forward(): pl.pallas_call(forward_kernel, out_shape=jax.ShapeDtypeStruct((row_blocks...  14.1 us
    all_to_all x1, waiting for transfers between devices, shards(): lax.all_to_all(packed.reshape(n_col, stride, 128), 'col', split_axis=0, c...  13.1 us
    all_to_all x1, starting transfers between devices, shards(): lax.all_to_all(packed.reshape(n_col, stride, 128), 'col', split_axis=0, c...  6.83 us
    another operation x9, other arithmetic, gather_relative(): x = jnp.stack([x, swap(x, axis, bit)], axis=1)  5.89 us
  transfers between devices with their start and end apart: 17, of which 13 were waited for; matrix products, arithmetic and copies ran while one was open for 5% of the time, Pallas kernels for 18%

profile of v1, /device:TPU:0, one launch (start us, length us, event | category | flops | bytes accessed | tf_op | source)
XLA Modules:
  0.0 210.6 jit_solution(16724825302121990314)
XLA Ops:
  2.5 4.1 %collective-permute-start.5 = (bf16[1,512,128]{2,1,0:T(8,128)(2,1)S(1)}, bf16[1,512,128]{2,1,0:T(8,128)(2,1)S(1)}, u32[]{:S(2)}, u32[]{:S(2)}) collective-permute-start(bf16[1,512,128]{2,1,0:T(8,128)(2,1)S(1)} %bitcast.161), channel_id=1, source_target_pairs={{0,8},{1,9},{2,10},{3,11},{4,12},{5,13},{6,14},{7,15},{8,0},{9,1},... | collective-permute-start | bytes 393224 | tf_op jit(solution)/shard_map/ppermute | solution.py:12
  9.2 3.6 %collective-permute-done.5 = bf16[1,512,128]{2,1,0:T(8,128)(2,1)S(1)} collective-permute-done((bf16[1,512,128]{2,1,0:T(8,128)(2,1)S(1)}, bf16[1,512,128]{2,1,0:T(8,128)(2,1)S(1)}, u32[]{:S(2)}, u32[]{:S(2)}) %collective-permute-start.5) | collective-permute-done | bytes 131104 | tf_op jit(solution)/shard_map/ppermute | solution.py:12
  14.9 5.6 %collective-permute-done.6 = bf16[2,512,128]{2,1,0:T(8,128)(2,1)S(1)} collective-permute-done((bf16[2,512,128]{2,1,0:T(8,128)(2,1)S(1)}, bf16[2,512,128]{2,1,0:T(8,128)(2,1)S(1)}, u32[]{:S(2)}, u32[]{:S(2)}) %collective-permute-start.6) | collective-permute-done | bytes 262176 | tf_op jit(solution)/shard_map/ppermute | solution.py:12
  20.6 1.3 collective-permute-start.7
  23.6 2.1 shard_map.120
  25.7 6.8 %all-to-all-start = ((s32[16,72,128]{2,1,0:T(8,128)}), s32[16,72,128]{2,1,0:T(8,128)S(1)}, u32[]{:S(2)}, u32[]{:S(2)}) async-start(s32[16,72,128]{2,1,0:T(8,128)} %bitcast.24), calls=%async_computation | async-start | bytes 1179648 | tf_op jit(solution)/shard_map/all_to_all | solution.py:334
  33.0 1.7 collective-permute-start.8
  35.0 13.1 %all-to-all-done = s32[16,72,128]{2,1,0:T(8,128)S(1)} async-done(((s32[16,72,128]{2,1,0:T(8,128)}), s32[16,72,128]{2,1,0:T(8,128)S(1)}, u32[]{:S(2)}, u32[]{:S(2)}) %all-to-all-start) | async-done | bytes 589856 | tf_op jit(solution)/shard_map/all_to_all | solution.py:334
  48.4 14.2 %collective-permute-done.8 = bf16[8,512,128]{2,1,0:T(8,128)(2,1)S(1)} collective-permute-done((bf16[8,512,128]{2,1,0:T(8,128)(2,1)S(1)}, bf16[8,512,128]{2,1,0:T(8,128)(2,1)S(1)}, u32[]{:S(2)}, u32[]{:S(2)}) %collective-permute-start.8) | collective-permute-done | bytes 1048608 | tf_op jit(solution)/shard_map/ppermute | solution.py:12
  70.5 3.9 %pad_maximum_fusion.1 = bf16[1,2,16,512,128]{4,3,2,1,0:T(8,128)(2,1)} fusion(bf16[1,1,16,512,128]{4,3,2,1,0:T(8,128)(2,1)} %bitcast.42, bf16[1,1,16,512,128]{4,3,2,1,0:T(8,128)(2,1)S(1)} %bitcast.145), kind=kLoop, calls=%fused_computation.27 | loop fusion | flops 2097152 | bytes 8388608 | tf_op jit(solution)/shard_map/stack | solution.py:30
  74.4 14.1 %shard_map.121 = f32[4,128,128]{2,1,0:T(8,128)S(1)} custom-call(s32[1]{0:T(128)} %bitcast.26.meta, s32[1064]{0:T(1024)S(1)} %broadcast_add_fusion.order, s32[1064]{0:T(1024)S(1)} %get-tuple-element.44.col, s32[132]{0:T(256)S(1)} %broadcast_minimum_fusion.owner, s32[1152,128]{1,0:T(8,128)S(1)} %bitcast.140, bf16[128,128,128]{2,1,0:T(8,128)(2,1)} %bitcast.43.panel), custom_call_target="tpu_custom_call" | custom-call | flops 35701915648 | bytes 34865152 | tf_op jit(solution)/shard_map/pallas_call | solution.py:230
  90.2 3.5 %collective-permute-start.10 = (bf16[1,4,128,128]{2,3,1,0:T(8,128)(2,1)S(1)}, bf16[1,4,128,128]{2,3,1,0:T(8,128)(2,1)S(1)}, u32[]{:S(2)}, u32[]{:S(2)}) collective-permute-start(bf16[1,4,128,128]{2,3,1,0:T(8,128)(2,1)S(1)} %bitcast.159), channel_id=1, source_target_pairs={{0,8},{1,9},{2,10},{3,11},{4,12},{5,13},{6,14},{7,15},{8,0},{9,1},... | collective-permute-start | bytes 393224 | tf_op jit(solution)/shard_map/ppermute | solution.py:12
  93.7 4.2 %collective-permute-done.10 = bf16[1,4,128,128]{2,3,1,0:T(8,128)(2,1)S(1)} collective-permute-done((bf16[1,4,128,128]{2,3,1,0:T(8,128)(2,1)S(1)}, bf16[1,4,128,128]{2,3,1,0:T(8,128)(2,1)S(1)}, u32[]{:S(2)}, u32[]{:S(2)}) %collective-permute-start.10) | collective-permute-done | bytes 131104 | tf_op jit(solution)/shard_map/ppermute | solution.py:12
  98.1 7.0 %collective-permute-done.11 = bf16[2,4,128,128]{2,3,1,0:T(8,128)(2,1)S(1)} collective-permute-done((bf16[2,4,128,128]{2,3,1,0:T(8,128)(2,1)S(1)}, bf16[2,4,128,128]{2,3,1,0:T(8,128)(2,1)S(1)}, u32[]{:S(2)}, u32[]{:S(2)}) %collective-permute-start.11) | collective-permute-done | bytes 262176 | tf_op jit(solution)/shard_map/ppermute | solution.py:12
  106.6 10.8 %collective-permute-done.12 = bf16[4,4,128,128]{3,2,1,0:T(8,128)(2,1)S(1)} collective-permute-done((bf16[4,4,128,128]{3,2,1,0:T(8,128)(2,1)S(1)}, bf16[4,4,128,128]{3,2,1,0:T(8,128)(2,1)S(1)}, u32[]{:S(2)}, u32[]{:S(2)}) %collective-permute-start.12) | collective-permute-done | bytes 524320 | tf_op jit(solution)/shard_map/ppermute | solution.py:12
  120.4 2.0 all_gather.3
  122.3 35.3 %shard_map.122.dense = bf16[576,128,128]{2,1,0:T(8,128)(2,1)} custom-call(s32[1]{0:T(128)} %bitcast.44.meta, s32[576]{0:T(1024)S(1)} %broadcast_add_fusion.1.order, s32[520,128]{1,0:T(8,128)S(1)} %pad.5.codes), custom_call_target="tpu_custom_call" | custom-call | flops 9663676416 | bytes 18874368 | tf_op jit(solution)/shard_map/pallas_call | solution.py:215
  157.6 1.4 pad_maximum_fusion.3
  159.3 28.8 %shard_map.123 = f32[8,128,128]{2,1,0:T(8,128)S(1)} custom-call(s32[1]{0:T(128)} %bitcast.44.meta, s32[576]{0:T(1024)S(1)} %get-tuple-element.47.src, s32[72]{0:T(128)S(1)} %broadcast_minimum_fusion.1.owner, bf16[64,128,128]{2,1,0:T(8,128)(2,1)S(1)} %bitcast.138, bf16[576,128,128]{2,1,0:T(8,128)(2,1)} %shard_map.122.dense), custom_call_target="tpu_custom_call" | custom-call | flops 9663676416 | bytes 18874368 | tf_op jit(solution)/shard_map/pallas_call | solution.py:242
  190.1 4.3 %collective-permute-done.16 = f32[136,128]{1,0:T(8,128)S(1)} collective-permute-done((f32[136,128]{1,0:T(8,128)S(1)}, f32[136,128]{1,0:T(8,128)S(1)}, u32[]{:S(2)}, u32[]{:S(2)}) %collective-permute-start.16) | collective-permute-done | bytes 69664 | tf_op jit(solution)/shard_map/ppermute | solution.py:12
  194.5 4.3 %collective-permute-done.17 = f32[136,128]{1,0:T(8,128)S(1)} collective-permute-done((f32[136,128]{1,0:T(8,128)S(1)}, f32[136,128]{1,0:T(8,128)S(1)}, u32[]{:S(2)}, u32[]{:S(2)}) %collective-permute-start.17) | collective-permute-done | bytes 69664 | tf_op jit(solution)/shard_map/ppermute | solution.py:12
  199.6 3.6 %collective-permute-done.18 = f32[136,128]{1,0:T(8,128)S(1)} collective-permute-done((f32[136,128]{1,0:T(8,128)S(1)}, f32[136,128]{1,0:T(8,128)S(1)}, u32[]{:S(2)}, u32[]{:S(2)}) %collective-permute-start.18) | collective-permute-done | bytes 69664 | tf_op jit(solution)/shard_map/ppermute | solution.py:12
  203.2 3.9 %collective-permute-start.19 = (f32[136,128]{1,0:T(8,128)S(1)}, f32[136,128]{1,0:T(8,128)S(1)}, u32[]{:S(2)}, u32[]{:S(2)}) collective-permute-start(f32[136,128]{1,0:T(8,128)S(1)} %add.330), channel_id=1, source_target_pairs={{0,8},{1,9},{2,10},{3,11},{4,12},{5,13},{6,14},{7,15},{8,0},{9,1},... | collective-permute-start | bytes 208904 | tf_op jit(solution)/shard_map/ppermute | solution.py:12
  207.9 1.4 collective-permute-done.19
  (105 shorter events, 21.1 us)
Async XLA Ops:
  0.6 0.8 copy-start
  2.5 10.4 %collective-permute-start.5 = (bf16[1,512,128]{2,1,0:T(8,128)(2,1)S(1)}, bf16[1,512,128]{2,1,0:T(8,128)(2,1)S(1)}, u32[]{:S(2)}, u32[]{:S(2)}) collective-permute-start(bf16[1,512,128]{2,1,0:T(8,128)(2,1)S(1)} %bitcast.161), channel_id=1, source_target_pairs={{0,8},{1,9},{2,10},{3,11},{4,12},{5,13},{6,14},{7,15},{8,0},{9,1},... | collective-permute-start | bytes 393224 | tf_op jit(solution)/shard_map/ppermute | solution.py:12
  12.9 7.6 %collective-permute-start.6 = (bf16[2,512,128]{2,1,0:T(8,128)(2,1)S(1)}, bf16[2,512,128]{2,1,0:T(8,128)(2,1)S(1)}, u32[]{:S(2)}, u32[]{:S(2)}) collective-permute-start(bf16[2,512,128]{2,1,0:T(8,128)(2,1)S(1)} %get-tuple-element.66), channel_id=1, source_target_pairs={{0,4},{1,5},{2,6},{3,7},{4,0},{5,1},{6,2},{7,3},{8,12},{9,13},{10,... | collective-permute-start | bytes 786440 | tf_op jit(solution)/shard_map/ppermute | solution.py:12
  20.6 12.3 %collective-permute-start.7 = (bf16[4,512,128]{2,1,0:T(8,128)(2,1)S(1)}, bf16[4,512,128]{2,1,0:T(8,128)(2,1)S(1)}, u32[]{:S(2)}, u32[]{:S(2)}) collective-permute-start(bf16[4,512,128]{2,1,0:T(8,128)(2,1)S(1)} %bitcast.154), channel_id=1, source_target_pairs={{0,2},{1,3},{2,0},{3,1},{4,6},{5,7},{6,4},{7,5},{8,10},{9,11},{10,... | collective-permute-start | bytes 1572872 | tf_op jit(solution)/shard_map/ppermute | solution.py:12
  25.7 22.4 %all-to-all-start = ((s32[16,72,128]{2,1,0:T(8,128)}), s32[16,72,128]{2,1,0:T(8,128)S(1)}, u32[]{:S(2)}, u32[]{:S(2)}) async-start(s32[16,72,128]{2,1,0:T(8,128)} %bitcast.24), calls=%async_computation | async-start | bytes 1179648 | tf_op jit(solution)/shard_map/all_to_all | solution.py:334
  33.0 29.6 %collective-permute-start.8 = (bf16[8,512,128]{2,1,0:T(8,128)(2,1)S(1)}, bf16[8,512,128]{2,1,0:T(8,128)(2,1)S(1)}, u32[]{:S(2)}, u32[]{:S(2)}) collective-permute-start(bf16[8,512,128]{2,1,0:T(8,128)(2,1)S(1)} %bitcast.152), channel_id=1, source_target_pairs={{0,1},{1,0},{2,3},{3,2},{4,5},{5,4},{6,7},{7,6},{8,9},{9,8},{10,11... | collective-permute-start | bytes 3145736 | tf_op jit(solution)/shard_map/ppermute | solution.py:12
  63.0 7.5 %collective-permute-start.9 = (bf16[1,16,512,128]{3,2,1,0:T(8,128)(2,1)S(1)}, bf16[1,16,512,128]{3,2,1,0:T(8,128)(2,1)}, u32[]{:S(2)}, u32[]{:S(2)}) collective-permute-start(bf16[1,16,512,128]{3,2,1,0:T(8,128)(2,1)S(1)} %bitcast.144), channel_id=1, source_target_pairs={{0,16},{16,0},{1,17},{17,1},{2,18},{18,2},{3,19},{19,3},{4,20},{20... | collective-permute-start | bytes 6291464 | tf_op jit(solution)/shard_map/ppermute | solution.py:12
  66.5 2.7 %collective-permute-start.4 = (s32[1,64]{1,0:T(1,128)S(1)}, s32[1,64]{1,0:T(1,128)S(1)}, u32[]{:S(2)}, u32[]{:S(2)}) collective-permute-start(s32[1,64]{1,0:T(1,128)S(1)} %bitcast.174), channel_id=1, source_target_pairs={{0,16},{16,0},{1,17},{17,1},{2,18},{18,2},{3,19},{19,3},{4,20},{20... | collective-permute-start | bytes 776 | tf_op jit(solution)/shard_map/ppermute | solution.py:12
  70.5 3.9 %copy-start.3 = (s32[1,1,512]{2,1,0:T(1,128)S(1)}, s32[1,1,512]{2,1,0:T(1,128)}, u32[]{:S(2)}) copy-start(s32[1,1,512]{2,1,0:T(1,128)} %param.17) | copy-start | bytes 6148
  70.5 3.9 %copy-start.4 = (s32[1,1,512]{2,1,0:T(1,128)S(1)}, s32[1,1,512]{2,1,0:T(1,128)}, u32[]{:S(2)}) copy-start(s32[1,1,512]{2,1,0:T(1,128)} %param.16) | copy-start | bytes 6148
  88.6 0.9 copy-start.2
  88.6 0.9 copy-start.5
  90.2 7.7 %collective-permute-start.10 = (bf16[1,4,128,128]{2,3,1,0:T(8,128)(2,1)S(1)}, bf16[1,4,128,128]{2,3,1,0:T(8,128)(2,1)S(1)}, u32[]{:S(2)}, u32[]{:S(2)}) collective-permute-start(bf16[1,4,128,128]{2,3,1,0:T(8,128)(2,1)S(1)} %bitcast.159), channel_id=1, source_target_pairs={{0,8},{1,9},{2,10},{3,11},{4,12},{5,13},{6,14},{7,15},{8,0},{9,1},... | collective-permute-start | bytes 393224 | tf_op jit(solution)/shard_map/ppermute | solution.py:12
  97.9 7.2 %collective-permute-start.11 = (bf16[2,4,128,128]{2,3,1,0:T(8,128)(2,1)S(1)}, bf16[2,4,128,128]{2,3,1,0:T(8,128)(2,1)S(1)}, u32[]{:S(2)}, u32[]{:S(2)}) collective-permute-start(bf16[2,4,128,128]{2,3,1,0:T(8,128)(2,1)S(1)} %get-tuple-element.64), channel_id=1, source_target_pairs={{0,4},{1,5},{2,6},{3,7},{4,0},{5,1},{6,2},{7,3},{8,12},{9,13},{10,... | collective-permute-start | bytes 786440 | tf_op jit(solution)/shard_map/ppermute | solution.py:12
  105.5 11.9 %collective-permute-start.12 = (bf16[4,4,128,128]{3,2,1,0:T(8,128)(2,1)S(1)}, bf16[4,4,128,128]{3,2,1,0:T(8,128)(2,1)S(1)}, u32[]{:S(2)}, u32[]{:S(2)}) collective-permute-start(bf16[4,4,128,128]{3,2,1,0:T(8,128)(2,1)S(1)} %bitcast.156), channel_id=1, source_target_pairs={{0,2},{1,3},{2,0},{3,1},{4,6},{5,7},{6,4},{7,5},{8,10},{9,11},{10,... | collective-permute-start | bytes 1572872 | tf_op jit(solution)/shard_map/ppermute | solution.py:12
  117.5 2.9 %copy-start.1 = (bf16[512,128]{1,0:T(8,128)(2,1)S(1)}, bf16[512,128]{1,0:T(8,128)(2,1)}, u32[]{:S(2)}) copy-start(bf16[512,128]{1,0:T(8,128)(2,1)} %param.11) | copy-start | bytes 393220
  117.6 40.0 %collective-permute-start.13 = (bf16[8,4,128,128]{3,2,1,0:T(8,128)(2,1)S(1)}, bf16[8,4,128,128]{3,2,1,0:T(8,128)(2,1)}, u32[]{:S(2)}, u32[]{:S(2)}) collective-permute-start(bf16[8,4,128,128]{3,2,1,0:T(8,128)(2,1)S(1)} %bitcast.150), channel_id=1, source_target_pairs={{0,1},{1,0},{2,3},{3,2},{4,5},{5,4},{6,7},{7,6},{8,9},{9,8},{10,11... | collective-permute-start | bytes 3145736 | tf_op jit(solution)/shard_map/ppermute | solution.py:12
  188.7 1.3 collective-permute-start.15
  188.9 18.2 %collective-permute-start.14 = (f32[1,512,128]{2,1,0:T(8,128)S(1)}, f32[1,512,128]{2,1,0:T(8,128)S(1)}, u32[]{:S(2)}, u32[]{:S(2)}) collective-permute-start(f32[1,512,128]{2,1,0:T(8,128)S(1)} %slice_bitcast_fusion.8), channel_id=1, source_target_pairs={{0,16},{16,0},{1,17},{17,1},{2,18},{18,2},{3,19},{19,3},{4,20},{20... | collective-permute-start | bytes 786440 | tf_op jit(solution)/shard_map/ppermute | solution.py:12
  190.0 4.4 %collective-permute-start.16 = (f32[136,128]{1,0:T(8,128)S(1)}, f32[136,128]{1,0:T(8,128)S(1)}, u32[]{:S(2)}, u32[]{:S(2)}) collective-permute-start(f32[136,128]{1,0:T(8,128)S(1)} %fusion.37), channel_id=1, source_target_pairs={{0,1},{1,0},{2,3},{3,2},{4,5},{5,4},{6,7},{7,6},{8,9},{9,8},{10,11... | collective-permute-start | bytes 208904 | tf_op jit(solution)/shard_map/ppermute | solution.py:12
  194.4 4.4 %collective-permute-start.17 = (f32[136,128]{1,0:T(8,128)S(1)}, f32[136,128]{1,0:T(8,128)S(1)}, u32[]{:S(2)}, u32[]{:S(2)}) collective-permute-start(f32[136,128]{1,0:T(8,128)S(1)} %add.328), channel_id=1, source_target_pairs={{0,2},{1,3},{2,0},{3,1},{4,6},{5,7},{6,4},{7,5},{8,10},{9,11},{10,... | collective-permute-start | bytes 208904 | tf_op jit(solution)/shard_map/ppermute | solution.py:12
  198.8 4.4 %collective-permute-start.18 = (f32[136,128]{1,0:T(8,128)S(1)}, f32[136,128]{1,0:T(8,128)S(1)}, u32[]{:S(2)}, u32[]{:S(2)}) collective-permute-start(f32[136,128]{1,0:T(8,128)S(1)} %add.329), channel_id=1, source_target_pairs={{0,4},{1,5},{2,6},{3,7},{4,0},{5,1},{6,2},{7,3},{8,12},{9,13},{10,... | collective-permute-start | bytes 208904 | tf_op jit(solution)/shard_map/ppermute | solution.py:12
  203.2 6.2 %collective-permute-start.19 = (f32[136,128]{1,0:T(8,128)S(1)}, f32[136,128]{1,0:T(8,128)S(1)}, u32[]{:S(2)}, u32[]{:S(2)}) collective-permute-start(f32[136,128]{1,0:T(8,128)S(1)} %add.330), channel_id=1, source_target_pairs={{0,8},{1,9},{2,10},{3,11},{4,12},{5,13},{6,14},{7,15},{8,0},{9,1},... | collective-permute-start | bytes 208904 | tf_op jit(solution)/shard_map/ppermute | solution.py:12

commit v2 on v1

--- a/solution.py
+++ b/solution.py
@@ -1,3 +1,4 @@
+import functools
 import functools
 import jax
 import jax.numpy as jnp
@@ -24,12 +25,35 @@
     return x[0]
 
 
-def gather_relative(x, axis):
-    x = x[None]
-    for bit in reversed(bits_of(axis)):
-        x = jnp.stack([x, swap(x, axis, bit)], axis=1)
-        x = x.reshape((x.shape[0] * 2,) + x.shape[2:])
-    return x
+def part_orders(per):
+    bits = bits_of("col")[::-1]
+    turned = bits[:-2] + bits[-1:] + bits[-2:-1]
+    return [bits, turned] if per % 2 == 0 and len(bits) > 1 else [bits]
+
+
+def gather_pieces(blocks):
+    orders = part_orders(blocks.shape[0])
+    size = blocks.shape[0] // len(orders)
+    held = [blocks[i * size : (i + 1) * size][None] for i in range(len(orders))]
+    for step in range(len(orders[0]) - 1):
+        came = [swap(x, "col", order[step]) for x, order in zip(held, orders)]
+        held = [jnp.concatenate([x, y], axis=0) for x, y in zip(held, came)]
+    came = [swap(x, "col", order[-1]) for x, order in zip(held, orders)]
+    shape = (-1,) + blocks.shape[1:]
+    return [[x.reshape(shape), y.reshape(shape)] for x, y in zip(held, came)]
+
+
+def piece_index(per, far, block, rho=0, n_row=1):
+    orders = part_orders(per)
+    size = per // len(orders)
+    half = lax.axis_size("col") // 2
+    result = 0
+    for i, order in enumerate(orders):
+        spot = sum(((far & bit) > 0).astype(jnp.int32) << t for t, bit in enumerate(order))
+        piece = (i * n_row + rho) * 2 + spot // half
+        here = (piece * half + spot % half) * size + block % size
+        result = jnp.where(block // size == i, here, result)
+    return result
 
 
 def total_sum(x, axes):
@@ -40,6 +64,7 @@
 
 
 GROUP = 8
+DEPTH = 8
 ROOM = 64
 SPARE = 8
 FIELD = 1 << 16
@@ -75,39 +100,51 @@
     turns = meta[0]
     rows = lax.broadcasted_iota(jnp.int32, (128, 128), 0)
 
-    def out_copy(i, slot):
+    def out_copy(i):
+        slot = lax.rem(i, DEPTH)
         return pltpu.make_async_copy(
             dbuf.at[slot], dense.at[pl.ds(i * GROUP, GROUP)], sems.at[slot]
         )
 
     def turn(i, _):
-        slot = lax.rem(i, 2)
-
-        @pl.when(i >= 2)
+        slot = lax.rem(i, DEPTH)
+
+        @pl.when(i >= DEPTH)
         def _():
-            out_copy(i - 2, slot).wait()
+            out_copy(i - DEPTH).wait()
 
         lines = [codes[pl.ds(order[i * GROUP + u], 1), :] for u in range(GROUP)]
         blocks = [block_of(line, rows) for line in lines]
         for u in range(GROUP):
             dbuf[slot, u] = blocks[u]
-        out_copy(i, slot).start()
+        out_copy(i).start()
         return 0
 
     lax.fori_loop(0, turns, turn, 0)
 
-    @pl.when(turns >= 2)
-    def _():
-        out_copy(turns - 2, lax.rem(turns, 2)).wait()
-
-    @pl.when(turns >= 1)
-    def _():
-        out_copy(turns - 1, lax.rem(turns + 1, 2)).wait()
-
-
-def forward_kernel(meta, order, col, owner, codes, panel, totals, dbuf):
+    def finish(i, _):
+        out_copy(i).wait()
+        return 0
+
+    lax.fori_loop(jnp.maximum(turns - DEPTH, 0), turns, finish, 0)
+
+
+def fetch(pieces, into, sems):
+    size = pieces[0].shape[0]
+    copies = [
+        pltpu.make_async_copy(piece, into.at[pl.ds(i * size, size)], sems.at[i])
+        for i, piece in enumerate(pieces)
+    ]
+    for copy in copies:
+        copy.start()
+    return copies
+
+
+def forward_kernel(n, meta, order, col, owner, codes, *refs):
+    pieces, (totals, feat, proj, dbuf, sems) = refs[: 2 * n], refs[2 * n :]
     turns = meta[0]
     rows = lax.broadcasted_iota(jnp.int32, (128, 128), 0)
+    copies = fetch(pieces[:n], feat, sems.at[0]) + fetch(pieces[n:], proj, sems.at[1])
     totals[...] = jnp.zeros_like(totals)
 
     def build(i, slot):
@@ -117,12 +154,18 @@
             dbuf[slot, :, u * 128 : (u + 1) * 128] = blocks[u]
 
     def product(i, slot):
-        right = jnp.concatenate([panel[col[i * GROUP + u]] for u in range(GROUP)], axis=0)
+        spots = [col[i * GROUP + u] for u in range(GROUP)]
+        right = jnp.concatenate(
+            [jnp.concatenate([proj[c], feat[c]], axis=1) for c in spots], axis=0
+        )
         return jnp.dot(dbuf[slot], right, preferred_element_type=jnp.float32)
 
     @pl.when(turns > 0)
     def _():
         build(0, 0)
+
+    for copy in copies:
+        copy.wait()
 
     def turn(i, _):
         slot = lax.rem(i, 2)
@@ -148,31 +191,34 @@
     lax.fori_loop(0, meta[0], turn, 0)
 
 
-def backward_kernel(meta, src, owner, grad, dense, acc, dbuf, sems):
+def backward_kernel(n, meta, src, owner, dense, *refs):
+    pieces, (acc, grad, dbuf, grad_sems, sems) = refs[:n], refs[n:]
     turns = meta[0]
-    acc[...] = jnp.zeros_like(acc)
-
-    def in_copy(i, slot):
+    copies = fetch(pieces, grad, grad_sems)
+
+    def in_copy(i):
+        slot = lax.rem(i, DEPTH)
         return pltpu.make_async_copy(
             dense.at[pl.ds(i * GROUP, GROUP)], dbuf.at[slot], sems.at[slot]
         )
 
-    for k in range(2):
-
-        @pl.when(turns > k)
+    def begin(i, _):
+        in_copy(i).start()
+        return 0
+
+    lax.fori_loop(0, jnp.minimum(turns, DEPTH - 1), begin, 0)
+    acc[...] = jnp.zeros_like(acc)
+    for copy in copies:
+        copy.wait()
+
+    def turn(i, _):
+        @pl.when(i + DEPTH - 1 < turns)
         def _():
-            in_copy(k, k).start()
-
-    def turn(i, _):
-        slot = lax.rem(i, 3)
-
-        @pl.when(i + 2 < turns)
-        def _():
-            in_copy(i + 2, lax.rem(i + 2, 3)).start()
-
-        in_copy(i, slot).wait()
+            in_copy(i + DEPTH - 1).start()
+
+        in_copy(i).wait()
         left = jnp.concatenate([grad[src[i * GROUP + u]] for u in range(GROUP)], axis=1)
-        right = dbuf[slot].reshape(GROUP * 128, 128)
+        right = dbuf[lax.rem(i, DEPTH)].reshape(GROUP * 128, 128)
         acc[owner[i]] += jnp.dot(left, right, preferred_element_type=jnp.float32)
         return 0
 
@@ -218,39 +264,50 @@
         in_specs=[SMEM] * 2 + [VMEM],
         out_specs=HBM,
         scratch_shapes=[
-            pltpu.VMEM((2, GROUP, 128, 128), jnp.bfloat16),
-            pltpu.SemaphoreType.DMA((2,)),
+            pltpu.VMEM((DEPTH, GROUP, 128, 128), jnp.bfloat16),
+            pltpu.SemaphoreType.DMA((DEPTH,)),
         ],
         compiler_params=PARAMS,
         cost_estimate=cost(order.shape[0], 4),
     )(meta, order, codes)
 
 
-def run_forward(meta, order, col, owner, codes, panel, row_blocks):
+def run_forward(meta, order, col, owner, codes, feat, proj, row_blocks):
+    n = len(feat)
+    size, _, width = feat[0].shape
     return pl.pallas_call(
-        forward_kernel,
-        out_shape=jax.ShapeDtypeStruct((row_blocks, 128, panel.shape[-1]), jnp.float32),
-        in_specs=[SMEM] * 4 + [VMEM] * 2,
+        functools.partial(forward_kernel, n),
+        out_shape=jax.ShapeDtypeStruct((row_blocks, 128, 2 * width), jnp.float32),
+        in_specs=[SMEM] * 4 + [VMEM] + [HBM] * (2 * n),
         out_specs=VMEM,
-        scratch_shapes=[pltpu.VMEM((2, 128, GROUP * 128), jnp.bfloat16)],
+        scratch_shapes=[
+            pltpu.VMEM((n * size, 128, width), jnp.bfloat16),
+            pltpu.VMEM((n * size, 128, width), jnp.bfloat16),
+            pltpu.VMEM((2, 128, GROUP * 128), jnp.bfloat16),
+            pltpu.SemaphoreType.DMA((2, n)),
+        ],
         compiler_params=PARAMS,
         cost_estimate=cost(order.shape[0], 8),
-    )(meta, order, col, owner, codes, panel)
-
-
-def run_backward(meta, src, owner, grad, dense, col_blocks):
+    )(meta, order, col, owner, codes, *feat, *proj)
+
+
+def run_backward(meta, src, owner, pieces, dense, col_blocks):
+    n = len(pieces)
+    size, width, _ = pieces[0].shape
     return pl.pallas_call(
-        backward_kernel,
-        out_shape=jax.ShapeDtypeStruct((col_blocks, grad.shape[1], 128), jnp.float32),
-        in_specs=[SMEM] * 3 + [VMEM, HBM],
+        functools.partial(backward_kernel, n),
+        out_shape=jax.ShapeDtypeStruct((col_blocks, width, 128), jnp.float32),
+        in_specs=[SMEM] * 3 + [HBM] * (n + 1),
         out_specs=VMEM,
         scratch_shapes=[
-            pltpu.VMEM((3, GROUP, 128, 128), jnp.bfloat16),
-            pltpu.SemaphoreType.DMA((3,)),
+            pltpu.VMEM((n * size, width, 128), jnp.bfloat16),
+            pltpu.VMEM((DEPTH, GROUP, 128, 128), jnp.bfloat16),
+            pltpu.SemaphoreType.DMA((n,)),
+            pltpu.SemaphoreType.DMA((DEPTH,)),
         ],
         compiler_params=PARAMS,
         cost_estimate=cost(src.shape[0], 4),
-    )(meta, src, owner, grad, dense)
+    )(meta, src, owner, dense, *pieces)
 
 
 def grouped(key, live, keys):
@@ -310,13 +367,14 @@
     home = brow // per
     turns_plain = ((count + GROUP - 1) // GROUP).reshape(1)
 
-    panel_in = lax.all_gather(features, "row", axis=0, tiled=True)
-
-    def tile_plan(panel):
+    def tile_plan():
+        wide = lax.all_gather(features, "row", axis=0, tiled=True)
+        low = jnp.dot(wide, weight, preferred_element_type=jnp.float32).astype(jnp.bfloat16)
+        panel = jnp.concatenate([low, wide], axis=1).reshape(col_blocks, 128, 2 * width)
         order = jnp.where(live, ids, slots)
         dst = jnp.where(live, (home ^ mine) * per + brow % per, 0)
         totals = run_tile(turns_plain, order, dst, bcol, codes, panel, row_blocks)
-        return scatter_sum(totals.reshape(n_col, node_dev, width), "col")
+        return scatter_sum(totals.reshape(n_col, node_dev, 2 * width), "col")
 
     if by_owner:
         same = live[None, :] & (home[None, :] == home[:, None]) & (ids[None, :] < ids[:, None])
@@ -337,19 +395,27 @@
         spread = total_sum(jnp.max(came[:, ROOM, ROOM:], axis=0)[None], ("row",))
         any_over = jnp.max(spread) > 0
 
-        projected = jnp.dot(features, weight, preferred_element_type=jnp.float32)
-        everywhere = gather_relative(
-            gather_relative(projected.astype(jnp.bfloat16), "col"), "row"
-        )
+        feat = []
+        for pair in gather_pieces(features.reshape(per, 128, width)):
+            rows = [pair]
+            for bit in bits_of("row"):
+                rows = rows + [[swap(x, "row", bit) for x in pair] for pair in rows]
+            feat += [x for pair in rows for x in pair]
+        proj = [
+            jnp.dot(x.reshape(-1, width), weight, preferred_element_type=jnp.float32)
+            .astype(jnp.bfloat16)
+            .reshape(x.shape)
+            for x in feat
+        ]
 
         got = came[:, ROOM, :ROOM]
         sources = jnp.arange(n_col, dtype=jnp.int32)[:, None]
         places = jnp.arange(ROOM, dtype=jnp.int32)[None, :]
         row_here = ((got - 1) // col_blocks).reshape(-1)
         col_there = (got - 1) % col_blocks
-        col_there = (
-            ((col_there // per) ^ mine_row) * n_col + (sources ^ mine)
-        ) * per + col_there % per
+        col_there = piece_index(
+            per, sources ^ mine, col_there % per, (col_there // per) ^ mine_row, n_row
+        )
         pos, owner, turns, length = grouped(row_here, (got > 0).reshape(-1), per)
         line = (sources * stride + places).reshape(-1)
         order = place(pos, line, length + GROUP, ROOM + 1)
@@ -360,45 +426,37 @@
             cols,
             owner,
             came.reshape(n_col * stride, 128),
-            everywhere.reshape(-1, 128, width),
+            feat,
+            proj,
             per,
-        ).reshape(node_dev, width)
-
-        def slow():
-            blocks = [
-                lax.dynamic_index_in_dim(everywhere[:, 0], mine_row ^ k, 0, keepdims=False)
-                for k in range(n_row)
-            ]
-            return tile_plan(jnp.stack(blocks).reshape(col_blocks, 128, width))
-
-        own = lax.cond(any_over, slow, lambda: own)
+        ).reshape(node_dev, 2 * width)
+        own = lax.cond(any_over, tile_plan, lambda: own)
     else:
-        panel = jnp.dot(panel_in, weight, preferred_element_type=jnp.float32)
-        own = tile_plan(panel.astype(jnp.bfloat16).reshape(col_blocks, 128, width))
+        own = tile_plan()
 
     pos, back_owner, back_turns, length = grouped(bcol, live, col_blocks)
     back_order = place(pos, ids, length, slots)
-    back_src = place(pos, (home ^ mine) * per + brow % per, length, 0)
+    back_src = place(pos, piece_index(per, home ^ mine, brow % per), length, 0)
     back_turns = back_turns.reshape(1)
     dense = run_build(back_turns, back_order, codes)
 
-    pre = own + bias
+    pre = own[:, :width] + bias
     output = jnp.maximum(pre, 0.0).astype(jnp.bfloat16)
     grad_own = jnp.where(pre > 0, cotangent.astype(jnp.float32), 0.0).astype(jnp.bfloat16)
     local_bias = jnp.sum(grad_own.astype(jnp.float32), axis=0)
     turned = jnp.swapaxes(grad_own.reshape(per, 128, width), 1, 2)
-    grad = gather_relative(turned, "col").reshape(row_blocks, width, 128)
-
-    acc = run_backward(back_turns, back_src, back_owner, grad, dense, col_blocks)
-    back = jnp.swapaxes(acc, 1, 2).reshape(col_blocks * 128, width)
+    grad = [x for pair in gather_pieces(turned) for x in pair]
     local_weight = lax.dot_general(
-        panel_in,
-        back.astype(jnp.bfloat16),
+        own[:, width:].astype(jnp.bfloat16),
+        grad_own,
         (((0,), (0,)), ((), ())),
         preferred_element_type=jnp.float32,
     )
     local = jnp.concatenate([local_weight, jnp.tile(local_bias[None], (8, 1))], axis=0)
     total = total_sum(local, ("row", "col"))
+
+    acc = run_backward(back_turns, back_src, back_owner, grad, dense, col_blocks)
+    back = jnp.swapaxes(acc, 1, 2).reshape(col_blocks * 128, width)
     grad_proj = scatter_sum(
         jnp.stack(
             [

time: 213 us -> 177 us (0.83)
  the two profiles are of different devices: /device:TPU:0 before, /device:TPU:23 now
where the time goes in v2:
time: 177 us; the launch traced here: 176 us
  Pallas kernels  58.4 us (33%)
  starting transfers between devices  43 us (24%)
  waiting for transfers between devices  33.5 us (19%)
  other arithmetic  13.6 us (8%)
  matrix products  12.7 us (7%)
  between operations  8.31 us (5%)
  local copies, waits for them, and re-layouts  6.02 us (3%)
    ppermute x27, starting transfers between devices, swap(): return lax.ppermute(x, axis, [(i, i ^ bit) for i in range(n)])  37 us
    ppermute x27, waiting for transfers between devices, swap(): return lax.ppermute(x, axis, [(i, i ^ bit) for i in range(n)])  33.5 us
    pallas_call x1, Pallas kernels, run_build(): pl.pallas_call(build_kernel, out_shape=jax.ShapeDtypeStruct((order.shape[...  22.2 us
    pallas_call x1, Pallas kernels, run_forward(): pl.pallas_call(functools.partial(forward_kernel, n), out_shape=jax.ShapeD...  17.5 us
    pallas_call x1, Pallas kernels, run_backward(): pl.pallas_call(functools.partial(backward_kernel, n), out_shape=jax.Shape...  16.7 us
    dot_general x8, matrix products, shards(): jnp.dot(x.reshape(-1, width), weight, preferred_element_type=jnp.float32)  10.7 us
    all_to_all x1, starting transfers between devices, shards(): lax.all_to_all(packed.reshape(n_col, stride, 128), 'col', split_axis=0, c...  5.99 us
    unnamed x16, local copies, waits for them, and re-layouts  3.84 us
  transfers between devices with their start and end apart: 28, of which 12 were waited for; matrix products, arithmetic and copies ran while one was open for 11% of the time, Pallas kernels for 13%

profile of v2, /device:TPU:23, one launch (start us, length us, event | category | flops | bytes accessed | tf_op | source)
XLA Modules:
  0.0 175.8 jit_solution(16615673074931379117)
XLA Ops:
  6.2 2.1 %shard_map.120 = s32[1152,128]{1,0:T(8,128)} custom-call(s32[1]{0:T(128)} %bitcast.16.meta, s32[512]{0:T(512)S(1)} %get-tuple-element.116.pos, s32[520,128]{1,0:T(8,128)S(1)} %pad.5.codes, s32[16,128]{1,0:T(8,128)S(1)} %concatenate.53.labels), custom_call_target="tpu_custom_call" | custom-call | tf_op jit(solution)/shard_map/pallas_call | solution.py:251
  8.3 6.0 %all-to-all-start = ((s32[16,72,128]{2,1,0:T(8,128)}), s32[16,72,128]{2,1,0:T(8,128)}, u32[]{:S(2)}, u32[]{:S(2)}) async-start(s32[16,72,128]{2,1,0:T(8,128)} %bitcast.20), calls=%async_computation | async-start | bytes 1179648 | tf_op jit(solution)/shard_map/all_to_all | solution.py:392
  15.5 2.1 %collective-permute-start.5 = (bf16[1,2,128,128]{3,2,1,0:T(8,128)(2,1)S(1)}, bf16[1,2,128,128]{3,2,1,0:T(8,128)(2,1)S(1)}, u32[]{:S(2)}, u32[]{:S(2)}) collective-permute-start(bf16[1,2,128,128]{3,2,1,0:T(8,128)(2,1)S(1)} %bitcast.169), channel_id=1, source_target_pairs={{0,8},{1,9},{2,10},{3,11},{4,12},{5,13},{6,14},{7,15},{8,0},{9,1},... | collective-permute-start | bytes 196616 | tf_op jit(solution)/shard_map/ppermute | solution.py:13
  20.7 22.2 %shard_map.122.dense = bf16[576,128,128]{2,1,0:T(8,128)(2,1)} custom-call(s32[1]{0:T(128)} %bitcast.46.meta, s32[576]{0:T(1024)S(1)} %broadcast_add_fusion.1.order, s32[520,128]{1,0:T(8,128)S(1)} %pad.5.codes), custom_call_target="tpu_custom_call" | custom-call | flops 9663676416 | bytes 18874368 | tf_op jit(solution)/shard_map/pallas_call | solution.py:261
  44.6 2.2 %collective-permute-done.12 = bf16[2,2,128,128]{3,2,1,0:T(8,128)(2,1)S(1)} collective-permute-done((bf16[2,2,128,128]{3,2,1,0:T(8,128)(2,1)S(1)}, bf16[2,2,128,128]{3,2,1,0:T(8,128)(2,1)S(1)}, u32[]{:S(2)}, u32[]{:S(2)}) %collective-permute-start.12) | collective-permute-done | bytes 131104 | tf_op jit(solution)/shard_map/ppermute | solution.py:13
  48.8 3.3 %collective-permute-done.13 = bf16[4,2,128,128]{3,2,1,0:T(8,128)(2,1)S(1)} collective-permute-done((bf16[4,2,128,128]{3,2,1,0:T(8,128)(2,1)S(1)}, bf16[4,2,128,128]{3,2,1,0:T(8,128)(2,1)S(1)}, u32[]{:S(2)}, u32[]{:S(2)}) %collective-permute-start.13) | collective-permute-done | bytes 262176 | tf_op jit(solution)/shard_map/ppermute | solution.py:13
  52.2 2.0 %collective-permute-done.7 = bf16[4,2,128,128]{3,2,1,0:T(8,128)(2,1)S(1)} collective-permute-done((bf16[4,2,128,128]{3,2,1,0:T(8,128)(2,1)S(1)}, bf16[4,2,128,128]{3,2,1,0:T(8,128)(2,1)S(1)}, u32[]{:S(2)}, u32[]{:S(2)}) %collective-permute-start.7) | collective-permute-done | bytes 262176 | tf_op jit(solution)/shard_map/ppermute | solution.py:13
  55.0 6.8 %collective-permute-start.15 = (bf16[16,128,128]{2,1,0:T(8,128)(2,1)S(1)}, bf16[16,128,128]{2,1,0:T(8,128)(2,1)S(1)}, u32[]{:S(2)}, u32[]{:S(2)}) collective-permute-start(bf16[16,128,128]{2,1,0:T(8,128)(2,1)S(1)} %bitcast.139), channel_id=1, source_target_pairs={{0,16},{16,0},{1,17},{17,1},{2,18},{18,2},{3,19},{19,3},{4,20},{20... | collective-permute-start | bytes 1572872 | tf_op jit(solution)/shard_map/ppermute | solution.py:13
  66.1 3.2 %collective-permute-start.16 = (bf16[16,128,128]{2,1,0:T(8,128)(2,1)S(1)}, bf16[16,128,128]{2,1,0:T(8,128)(2,1)}, u32[]{:S(2)}, u32[]{:S(2)}) collective-permute-start(bf16[16,128,128]{2,1,0:T(8,128)(2,1)S(1)} %bitcast.145), channel_id=1, source_target_pairs={{0,16},{16,0},{1,17},{17,1},{2,18},{18,2},{3,19},{19,3},{4,20},{20... | collective-permute-start | bytes 1572872 | tf_op jit(solution)/shard_map/ppermute | solution.py:13
  83.6 2.1 %convolution_convert_fusion.1 = bf16[2048,128]{1,0:T(8,128)(2,1)} fusion(bf16[2048,128]{1,0:T(8,128)(2,1)} %bitcast.44, bf16[128,128]{1,0:T(8,128)(2,1)S(1)} %copy-done.4), kind=kOutput, calls=%fused_computation.29 | convolution fusion | flops 67371008 | bytes 1081344 | tf_op jit(solution)/shard_map/dot_general | solution.py:405
  85.7 2.1 %convolution_convert_fusion.5 = bf16[2048,128]{1,0:T(8,128)(2,1)} fusion(bf16[2048,128]{1,0:T(8,128)(2,1)} %bitcast.36, bf16[128,128]{1,0:T(8,128)(2,1)S(1)} %copy-done.4), kind=kOutput, calls=%fused_computation.33 | convolution fusion | flops 67371008 | bytes 1081344 | tf_op jit(solution)/shard_map/dot_general | solution.py:405
  90.9 17.5 %shard_map.121 = f32[4,128,256]{2,1,0:T(8,128)} custom-call(s32[1]{0:T(128)} %bitcast.22.meta, s32[1064]{0:T(1024)S(1)} %broadcast_add_fusion.order, s32[1064]{0:T(1024)S(1)} %get-tuple-element.92.col, s32[132]{0:T(256)S(1)} %broadcast_minimum_fusion.owner, s32[1152,128]{1,0:T(8,128)} %bitcast.23.codes, bf16[16,128,128]{2,1,0:T(8,128)(2,1)S(1)} %bitcast.144, ...), custom_call_target="tpu_custom_call" | custom-call | flops 35701915648 | bytes 34865152 | tf_op jit(solution)/shard_map/pallas_call | solution.py:278
  112.4 2.4 %collective-permute-start.17 = (bf16[1,2,128,128]{3,2,1,0:T(8,128)(2,1)S(1)}, bf16[1,2,128,128]{3,2,1,0:T(8,128)(2,1)S(1)}, u32[]{:S(2)}, u32[]{:S(2)}) collective-permute-start(bf16[1,2,128,128]{3,2,1,0:T(8,128)(2,1)S(1)} %get-tuple-element.110), channel_id=1, source_target_pairs={{0,8},{1,9},{2,10},{3,11},{4,12},{5,13},{6,14},{7,15},{8,0},{9,1},... | collective-permute-start | bytes 196616 | tf_op jit(solution)/shard_map/ppermute | solution.py:13
  118.5 2.9 %collective-permute-done.22 = bf16[2,2,128,128]{3,2,1,0:T(8,128)(2,1)S(1)} collective-permute-done((bf16[2,2,128,128]{3,2,1,0:T(8,128)(2,1)S(1)}, bf16[2,2,128,128]{3,2,1,0:T(8,128)(2,1)S(1)}, u32[]{:S(2)}, u32[]{:S(2)}) %collective-permute-start.22) | collective-permute-done | bytes 131104 | tf_op jit(solution)/shard_map/ppermute | solution.py:13
  121.4 2.5 %collective-permute-start.23 = (bf16[4,2,128,128]{3,2,1,0:T(8,128)(2,1)S(1)}, bf16[4,2,128,128]{3,2,1,0:T(8,128)(2,1)S(1)}, u32[]{:S(2)}, u32[]{:S(2)}) collective-permute-start(bf16[4,2,128,128]{3,2,1,0:T(8,128)(2,1)S(1)} %pad_maximum_fusion.8), channel_id=1, source_target_pairs={{0,1},{1,0},{2,3},{3,2},{4,5},{5,4},{6,7},{7,6},{8,9},{9,8},{10,11... | collective-permute-start | bytes 786440 | tf_op jit(solution)/shard_map/ppermute | solution.py:13
  125.4 1.8 %collective-permute-start.27 = (f32[136,128]{1,0:T(8,128)S(1)}, f32[136,128]{1,0:T(8,128)S(1)}, u32[]{:S(2)}, u32[]{:S(2)}) collective-permute-start(f32[136,128]{1,0:T(8,128)S(1)} %fusion.51), channel_id=1, source_target_pairs={{0,1},{1,0},{2,3},{3,2},{4,5},{5,4},{6,7},{7,6},{8,9},{9,8},{10,11... | collective-permute-start | bytes 208904 | tf_op jit(solution)/shard_map/ppermute | solution.py:13
  127.2 1.9 %collective-permute-done.23 = bf16[4,2,128,128]{3,2,1,0:T(8,128)(2,1)S(1)} collective-permute-done((bf16[4,2,128,128]{3,2,1,0:T(8,128)(2,1)S(1)}, bf16[4,2,128,128]{3,2,1,0:T(8,128)(2,1)S(1)}, u32[]{:S(2)}, u32[]{:S(2)}) %collective-permute-start.23) | collective-permute-done | bytes 262176 | tf_op jit(solution)/shard_map/ppermute | solution.py:13
  129.2 3.1 %collective-permute-start.24 = (bf16[8,2,128,128]{3,2,1,0:T(8,128)(2,1)S(1)}, bf16[8,2,128,128]{3,2,1,0:T(8,128)(2,1)S(1)}, u32[]{:S(2)}, u32[]{:S(2)}) collective-permute-start(bf16[8,2,128,128]{3,2,1,0:T(8,128)(2,1)S(1)} %pad_maximum_fusion.4), channel_id=1, source_target_pairs={{0,2},{1,3},{2,0},{3,1},{4,6},{5,7},{6,4},{7,5},{8,10},{9,11},{10,... | collective-permute-start | bytes 1572872 | tf_op jit(solution)/shard_map/ppermute | solution.py:13
  132.3 2.0 %collective-permute-start.20 = (bf16[8,2,128,128]{3,2,1,0:T(8,128)(2,1)S(1)}, bf16[8,2,128,128]{3,2,1,0:T(8,128)(2,1)S(1)}, u32[]{:S(2)}, u32[]{:S(2)}) collective-permute-start(bf16[8,2,128,128]{3,2,1,0:T(8,128)(2,1)S(1)} %pad_maximum_fusion.3), channel_id=1, source_target_pairs={{0,1},{1,0},{2,3},{3,2},{4,5},{5,4},{6,7},{7,6},{8,9},{9,8},{10,11... | collective-permute-start | bytes 1572872 | tf_op jit(solution)/shard_map/ppermute | solution.py:13
  135.4 10.4 %collective-permute-done.28 = f32[136,128]{1,0:T(8,128)S(1)} collective-permute-done((f32[136,128]{1,0:T(8,128)S(1)}, f32[136,128]{1,0:T(8,128)S(1)}, u32[]{:S(2)}, u32[]{:S(2)}) %collective-permute-start.28) | collective-permute-done | bytes 69664 | tf_op jit(solution)/shard_map/ppermute | solution.py:13
  146.7 2.3 %collective-permute-done.29 = f32[136,128]{1,0:T(8,128)S(1)} collective-permute-done((f32[136,128]{1,0:T(8,128)S(1)}, f32[136,128]{1,0:T(8,128)S(1)}, u32[]{:S(2)}, u32[]{:S(2)}) %collective-permute-start.29) | collective-permute-done | bytes 69664 | tf_op jit(solution)/shard_map/ppermute | solution.py:13
  149.1 4.1 %collective-permute-done.30 = f32[136,128]{1,0:T(8,128)S(1)} collective-permute-done((f32[136,128]{1,0:T(8,128)S(1)}, f32[136,128]{1,0:T(8,128)S(1)}, u32[]{:S(2)}, u32[]{:S(2)}) %collective-permute-start.30) | collective-permute-done | bytes 69664 | tf_op jit(solution)/shard_map/ppermute | solution.py:13
  153.3 16.7 %shard_map.123 = f32[8,128,128]{2,1,0:T(8,128)S(1)} custom-call(s32[1]{0:T(128)} %bitcast.46.meta, s32[576]{0:T(1024)S(1)} %get-tuple-element.95.src, s32[72]{0:T(128)S(1)} %broadcast_minimum_fusion.1.owner, bf16[576,128,128]{2,1,0:T(8,128)(2,1)} %shard_map.122.dense, bf16[16,128,128]{2,1,0:T(8,128)(2,1)S(1)} %bitcast.157, ...), custom_call_target="tpu_custom_call" | custom-call | flops 9663676416 | bytes 18874368 | tf_op jit(solution)/shard_map/pallas_call | solution.py:297
  170.3 3.4 %collective-permute-start.25 = (f32[1,512,128]{2,1,0:T(8,128)S(1)}, f32[1,512,128]{2,1,0:T(8,128)S(1)}, u32[]{:S(2)}, u32[]{:S(2)}) collective-permute-start(f32[1,512,128]{2,1,0:T(8,128)S(1)} %slice_bitcast_fusion.8), channel_id=1, source_target_pairs={{0,16},{16,0},{1,17},{17,1},{2,18},{18,2},{3,19},{19,3},{4,20},{20... | collective-permute-start | bytes 786440 | tf_op jit(solution)/shard_map/ppermute | solution.py:13
  (144 shorter events, 42.3 us)
Async XLA Ops:
  8.3 66.2 %all-to-all-start = ((s32[16,72,128]{2,1,0:T(8,128)}), s32[16,72,128]{2,1,0:T(8,128)}, u32[]{:S(2)}, u32[]{:S(2)}) async-start(s32[16,72,128]{2,1,0:T(8,128)} %bitcast.20), calls=%async_computation | async-start | bytes 1179648 | tf_op jit(solution)/shard_map/all_to_all | solution.py:392
  15.2 27.7 %collective-permute-start.11 = (bf16[1,2,128,128]{3,2,1,0:T(8,128)(2,1)S(1)}, bf16[1,2,128,128]{3,2,1,0:T(8,128)(2,1)S(1)}, u32[]{:S(2)}, u32[]{:S(2)}) collective-permute-start(bf16[1,2,128,128]{3,2,1,0:T(8,128)(2,1)S(1)} %bitcast.173), channel_id=1, source_target_pairs={{0,8},{1,9},{2,10},{3,11},{4,12},{5,13},{6,14},{7,15},{8,0},{9,1},... | collective-permute-start | bytes 196616 | tf_op jit(solution)/shard_map/ppermute | solution.py:13
  15.5 27.4 %collective-permute-start.5 = (bf16[1,2,128,128]{3,2,1,0:T(8,128)(2,1)S(1)}, bf16[1,2,128,128]{3,2,1,0:T(8,128)(2,1)S(1)}, u32[]{:S(2)}, u32[]{:S(2)}) collective-permute-start(bf16[1,2,128,128]{3,2,1,0:T(8,128)(2,1)S(1)} %bitcast.169), channel_id=1, source_target_pairs={{0,8},{1,9},{2,10},{3,11},{4,12},{5,13},{6,14},{7,15},{8,0},{9,1},... | collective-permute-start | bytes 196616 | tf_op jit(solution)/shard_map/ppermute | solution.py:13
  43.0 5.6 %collective-permute-start.6 = (bf16[2,2,128,128]{3,2,1,0:T(8,128)(2,1)S(1)}, bf16[2,2,128,128]{3,2,1,0:T(8,128)(2,1)S(1)}, u32[]{:S(2)}, u32[]{:S(2)}) collective-permute-start(bf16[2,2,128,128]{3,2,1,0:T(8,128)(2,1)S(1)} %pad_maximum_fusion.9), channel_id=1, source_target_pairs={{0,4},{1,5},{2,6},{3,7},{4,0},{5,1},{6,2},{7,3},{8,12},{9,13},{10,... | collective-permute-start | bytes 393224 | tf_op jit(solution)/shard_map/ppermute | solution.py:13
  46.8 5.3 %collective-permute-start.13 = (bf16[4,2,128,128]{3,2,1,0:T(8,128)(2,1)S(1)}, bf16[4,2,128,128]{3,2,1,0:T(8,128)(2,1)S(1)}, u32[]{:S(2)}, u32[]{:S(2)}) collective-permute-start(bf16[4,2,128,128]{3,2,1,0:T(8,128)(2,1)S(1)} %pad_maximum_fusion.6), channel_id=1, source_target_pairs={{0,1},{1,0},{2,3},{3,2},{4,5},{5,4},{6,7},{7,6},{8,9},{9,8},{10,11... | collective-permute-start | bytes 786440 | tf_op jit(solution)/shard_map/ppermute | solution.py:13
  48.7 5.6 %collective-permute-start.7 = (bf16[4,2,128,128]{3,2,1,0:T(8,128)(2,1)S(1)}, bf16[4,2,128,128]{3,2,1,0:T(8,128)(2,1)S(1)}, u32[]{:S(2)}, u32[]{:S(2)}) collective-permute-start(bf16[4,2,128,128]{3,2,1,0:T(8,128)(2,1)S(1)} %pad_maximum_fusion.5), channel_id=1, source_target_pairs={{0,2},{1,3},{2,0},{3,1},{4,6},{5,7},{6,4},{7,5},{8,10},{9,11},{10,... | collective-permute-start | bytes 786440 | tf_op jit(solution)/shard_map/ppermute | solution.py:13
  52.1 14.0 %collective-permute-start.14 = (bf16[8,2,128,128]{3,2,1,0:T(8,128)(2,1)S(1)}, bf16[8,2,128,128]{3,2,1,0:T(8,128)(2,1)S(1)}, u32[]{:S(2)}, u32[]{:S(2)}) collective-permute-start(bf16[8,2,128,128]{3,2,1,0:T(8,128)(2,1)S(1)} %pad_maximum_fusion.2), channel_id=1, source_target_pairs={{0,2},{1,3},{2,0},{3,1},{4,6},{5,7},{6,4},{7,5},{8,10},{9,11},{10,... | collective-permute-start | bytes 1572872 | tf_op jit(solution)/shard_map/ppermute | solution.py:13
  54.3 15.0 %collective-permute-start.8 = (bf16[8,2,128,128]{3,2,1,0:T(8,128)(2,1)S(1)}, bf16[8,2,128,128]{3,2,1,0:T(8,128)(2,1)S(1)}, u32[]{:S(2)}, u32[]{:S(2)}) collective-permute-start(bf16[8,2,128,128]{3,2,1,0:T(8,128)(2,1)S(1)} %pad_maximum_fusion.1), channel_id=1, source_target_pairs={{0,1},{1,0},{2,3},{3,2},{4,5},{5,4},{6,7},{7,6},{8,9},{9,8},{10,11... | collective-permute-start | bytes 1572872 | tf_op jit(solution)/shard_map/ppermute | solution.py:13
  55.0 15.3 %collective-permute-start.15 = (bf16[16,128,128]{2,1,0:T(8,128)(2,1)S(1)}, bf16[16,128,128]{2,1,0:T(8,128)(2,1)S(1)}, u32[]{:S(2)}, u32[]{:S(2)}) collective-permute-start(bf16[16,128,128]{2,1,0:T(8,128)(2,1)S(1)} %bitcast.139), channel_id=1, source_target_pairs={{0,16},{16,0},{1,17},{17,1},{2,18},{18,2},{3,19},{19,3},{4,20},{20... | collective-permute-start | bytes 1572872 | tf_op jit(solution)/shard_map/ppermute | solution.py:13
  62.4 8.9 %collective-permute-start.9 = (bf16[16,128,128]{2,1,0:T(8,128)(2,1)S(1)}, bf16[16,128,128]{2,1,0:T(8,128)(2,1)S(1)}, u32[]{:S(2)}, u32[]{:S(2)}) collective-permute-start(bf16[16,128,128]{2,1,0:T(8,128)(2,1)S(1)} %bitcast.142), channel_id=1, source_target_pairs={{0,16},{16,0},{1,17},{17,1},{2,18},{18,2},{3,19},{19,3},{4,20},{20... | collective-permute-start | bytes 1572872 | tf_op jit(solution)/shard_map/ppermute | solution.py:13
  66.1 17.4 %collective-permute-start.16 = (bf16[16,128,128]{2,1,0:T(8,128)(2,1)S(1)}, bf16[16,128,128]{2,1,0:T(8,128)(2,1)}, u32[]{:S(2)}, u32[]{:S(2)}) collective-permute-start(bf16[16,128,128]{2,1,0:T(8,128)(2,1)S(1)} %bitcast.145), channel_id=1, source_target_pairs={{0,16},{16,0},{1,17},{17,1},{2,18},{18,2},{3,19},{19,3},{4,20},{20... | collective-permute-start | bytes 1572872 | tf_op jit(solution)/shard_map/ppermute | solution.py:13
  69.4 16.3 %collective-permute-start.10 = (bf16[16,128,128]{2,1,0:T(8,128)(2,1)S(1)}, bf16[16,128,128]{2,1,0:T(8,128)(2,1)}, u32[]{:S(2)}, u32[]{:S(2)}) collective-permute-start(bf16[16,128,128]{2,1,0:T(8,128)(2,1)S(1)} %bitcast.148), channel_id=1, source_target_pairs={{0,16},{16,0},{1,17},{17,1},{2,18},{18,2},{3,19},{19,3},{4,20},{20... | collective-permute-start | bytes 1572872 | tf_op jit(solution)/shard_map/ppermute | solution.py:13
  111.1 4.7 %collective-permute-start.21 = (bf16[1,2,128,128]{3,2,1,0:T(8,128)(2,1)S(1)}, bf16[1,2,128,128]{3,2,1,0:T(8,128)(2,1)S(1)}, u32[]{:S(2)}, u32[]{:S(2)}) collective-permute-start(bf16[1,2,128,128]{3,2,1,0:T(8,128)(2,1)S(1)} %get-tuple-element.109), channel_id=1, source_target_pairs={{0,8},{1,9},{2,10},{3,11},{4,12},{5,13},{6,14},{7,15},{8,0},{9,1},... | collective-permute-start | bytes 196616 | tf_op jit(solution)/shard_map/ppermute | solution.py:13
  112.4 4.9 %collective-permute-start.17 = (bf16[1,2,128,128]{3,2,1,0:T(8,128)(2,1)S(1)}, bf16[1,2,128,128]{3,2,1,0:T(8,128)(2,1)S(1)}, u32[]{:S(2)}, u32[]{:S(2)}) collective-permute-start(bf16[1,2,128,128]{3,2,1,0:T(8,128)(2,1)S(1)} %get-tuple-element.110), channel_id=1, source_target_pairs={{0,8},{1,9},{2,10},{3,11},{4,12},{5,13},{6,14},{7,15},{8,0},{9,1},... | collective-permute-start | bytes 196616 | tf_op jit(solution)/shard_map/ppermute | solution.py:13
  115.9 5.5 %collective-permute-start.22 = (bf16[2,2,128,128]{3,2,1,0:T(8,128)(2,1)S(1)}, bf16[2,2,128,128]{3,2,1,0:T(8,128)(2,1)S(1)}, u32[]{:S(2)}, u32[]{:S(2)}) collective-permute-start(bf16[2,2,128,128]{3,2,1,0:T(8,128)(2,1)S(1)} %pad_maximum_fusion.12), channel_id=1, source_target_pairs={{0,4},{1,5},{2,6},{3,7},{4,0},{5,1},{6,2},{7,3},{8,12},{9,13},{10,... | collective-permute-start | bytes 393224 | tf_op jit(solution)/shard_map/ppermute | solution.py:13
  117.3 6.6 %collective-permute-start.18 = (bf16[2,2,128,128]{3,2,1,0:T(8,128)(2,1)S(1)}, bf16[2,2,128,128]{3,2,1,0:T(8,128)(2,1)S(1)}, u32[]{:S(2)}, u32[]{:S(2)}) collective-permute-start(bf16[2,2,128,128]{3,2,1,0:T(8,128)(2,1)S(1)} %pad_maximum_fusion.11), channel_id=1, source_target_pairs={{0,4},{1,5},{2,6},{3,7},{4,0},{5,1},{6,2},{7,3},{8,12},{9,13},{10,... | collective-permute-start | bytes 393224 | tf_op jit(solution)/shard_map/ppermute | solution.py:13
  118.4 7.0 %collective-permute-start.26 = (f32[136,128]{1,0:T(8,128)S(1)}, f32[136,128]{1,0:T(8,128)S(1)}, u32[]{:S(2)}, u32[]{:S(2)}) collective-permute-start(f32[136,128]{1,0:T(8,128)S(1)} %pad_maximum_fusion.13), channel_id=1, source_target_pairs={{0,16},{16,0},{1,17},{17,1},{2,18},{18,2},{3,19},{19,3},{4,20},{20... | collective-permute-start | bytes 208904 | tf_op jit(solution)/shard_map/ppermute | solution.py:13
  121.4 7.7 %collective-permute-start.23 = (bf16[4,2,128,128]{3,2,1,0:T(8,128)(2,1)S(1)}, bf16[4,2,128,128]{3,2,1,0:T(8,128)(2,1)S(1)}, u32[]{:S(2)}, u32[]{:S(2)}) collective-permute-start(bf16[4,2,128,128]{3,2,1,0:T(8,128)(2,1)S(1)} %pad_maximum_fusion.8), channel_id=1, source_target_pairs={{0,1},{1,0},{2,3},{3,2},{4,5},{5,4},{6,7},{7,6},{8,9},{9,8},{10,11... | collective-permute-start | bytes 786440 | tf_op jit(solution)/shard_map/ppermute | solution.py:13
  124.0 8.3 %collective-permute-start.19 = (bf16[4,2,128,128]{3,2,1,0:T(8,128)(2,1)S(1)}, bf16[4,2,128,128]{3,2,1,0:T(8,128)(2,1)S(1)}, u32[]{:S(2)}, u32[]{:S(2)}) collective-permute-start(bf16[4,2,128,128]{3,2,1,0:T(8,128)(2,1)S(1)} %pad_maximum_fusion.7), channel_id=1, source_target_pairs={{0,2},{1,3},{2,0},{3,1},{4,6},{5,7},{6,4},{7,5},{8,10},{9,11},{10,... | collective-permute-start | bytes 786440 | tf_op jit(solution)/shard_map/ppermute | solution.py:13
  125.4 9.0 %collective-permute-start.27 = (f32[136,128]{1,0:T(8,128)S(1)}, f32[136,128]{1,0:T(8,128)S(1)}, u32[]{:S(2)}, u32[]{:S(2)}) collective-permute-start(f32[136,128]{1,0:T(8,128)S(1)} %fusion.51), channel_id=1, source_target_pairs={{0,1},{1,0},{2,3},{3,2},{4,5},{5,4},{6,7},{7,6},{8,9},{9,8},{10,11... | collective-permute-start | bytes 208904 | tf_op jit(solution)/shard_map/ppermute | solution.py:13
  129.2 24.1 %collective-permute-start.24 = (bf16[8,2,128,128]{3,2,1,0:T(8,128)(2,1)S(1)}, bf16[8,2,128,128]{3,2,1,0:T(8,128)(2,1)S(1)}, u32[]{:S(2)}, u32[]{:S(2)}) collective-permute-start(bf16[8,2,128,128]{3,2,1,0:T(8,128)(2,1)S(1)} %pad_maximum_fusion.4), channel_id=1, source_target_pairs={{0,2},{1,3},{2,0},{3,1},{4,6},{5,7},{6,4},{7,5},{8,10},{9,11},{10,... | collective-permute-start | bytes 1572872 | tf_op jit(solution)/shard_map/ppermute | solution.py:13
  132.3 20.9 %collective-permute-start.20 = (bf16[8,2,128,128]{3,2,1,0:T(8,128)(2,1)S(1)}, bf16[8,2,128,128]{3,2,1,0:T(8,128)(2,1)S(1)}, u32[]{:S(2)}, u32[]{:S(2)}) collective-permute-start(bf16[8,2,128,128]{3,2,1,0:T(8,128)(2,1)S(1)} %pad_maximum_fusion.3), channel_id=1, source_target_pairs={{0,1},{1,0},{2,3},{3,2},{4,5},{5,4},{6,7},{7,6},{8,9},{9,8},{10,11... | collective-permute-start | bytes 1572872 | tf_op jit(solution)/shard_map/ppermute | solution.py:13
  134.4 11.3 %collective-permute-start.28 = (f32[136,128]{1,0:T(8,128)S(1)}, f32[136,128]{1,0:T(8,128)S(1)}, u32[]{:S(2)}, u32[]{:S(2)}) collective-permute-start(f32[136,128]{1,0:T(8,128)S(1)} %add.621), channel_id=1, source_target_pairs={{0,2},{1,3},{2,0},{3,1},{4,6},{5,7},{6,4},{7,5},{8,10},{9,11},{10,... | collective-permute-start | bytes 208904 | tf_op jit(solution)/shard_map/ppermute | solution.py:13
  170.3 4.6 %collective-permute-start.25 = (f32[1,512,128]{2,1,0:T(8,128)S(1)}, f32[1,512,128]{2,1,0:T(8,128)S(1)}, u32[]{:S(2)}, u32[]{:S(2)}) collective-permute-start(f32[1,512,128]{2,1,0:T(8,128)S(1)} %slice_bitcast_fusion.8), channel_id=1, source_target_pairs={{0,16},{16,0},{1,17},{17,1},{2,18},{18,2},{3,19},{19,3},{4,20},{20... | collective-permute-start | bytes 786440 | tf_op jit(solution)/shard_map/ppermute | solution.py:13
  (12 other events, 110.3 us)

commit v3 on v2

--- a/solution.py
+++ b/solution.py
@@ -31,13 +31,15 @@
     return [bits, turned] if per % 2 == 0 and len(bits) > 1 else [bits]
 
 
-def gather_pieces(blocks):
+def gather_pieces(blocks, beside=None):
     orders = part_orders(blocks.shape[0])
     size = blocks.shape[0] // len(orders)
     held = [blocks[i * size : (i + 1) * size][None] for i in range(len(orders))]
     for step in range(len(orders[0]) - 1):
         came = [swap(x, "col", order[step]) for x, order in zip(held, orders)]
         held = [jnp.concatenate([x, y], axis=0) for x, y in zip(held, came)]
+        if beside is not None:
+            beside(step, held)
     came = [swap(x, "col", order[-1]) for x, order in zip(held, orders)]
     shape = (-1,) + blocks.shape[1:]
     return [[x.reshape(shape), y.reshape(shape)] for x, y in zip(held, came)]
@@ -56,11 +58,8 @@
     return result
 
 
-def total_sum(x, axes):
-    for axis in axes:
-        for bit in bits_of(axis):
-            x = x + swap(x, axis, bit)
-    return x
+def total_steps():
+    return [("row", bit) for bit in bits_of("row")] + [("col", bit) for bit in bits_of("col")[::-1]]
 
 
 GROUP = 8
@@ -81,7 +80,7 @@
     ).astype(jnp.bfloat16)
 
 
-def pack_kernel(meta, pos, codes, labels, out):
+def pack_kernel(meta, pos, codes, labels, after, out):
     out[...] = jnp.zeros_like(out)
     stride = ROOM + SPARE
     for k in range(labels.shape[0]):
@@ -96,8 +95,9 @@
     lax.fori_loop(0, meta[0], turn, 0)
 
 
-def build_kernel(meta, order, codes, dense, dbuf, sems):
-    turns = meta[0]
+def build_kernel(meta, order, codes, *refs):
+    dense, dbuf, sems = refs[-3:]
+    start, turns = meta[0], meta[1]
     rows = lax.broadcasted_iota(jnp.int32, (128, 128), 0)
 
     def out_copy(i):
@@ -109,7 +109,7 @@
     def turn(i, _):
         slot = lax.rem(i, DEPTH)
 
-        @pl.when(i >= DEPTH)
+        @pl.when(i >= start + DEPTH)
         def _():
             out_copy(i - DEPTH).wait()
 
@@ -120,13 +120,13 @@
         out_copy(i).start()
         return 0
 
-    lax.fori_loop(0, turns, turn, 0)
+    lax.fori_loop(start, turns, turn, 0)
 
     def finish(i, _):
         out_copy(i).wait()
         return 0
 
-    lax.fori_loop(jnp.maximum(turns - DEPTH, 0), turns, finish, 0)
+    lax.fori_loop(jnp.maximum(turns - DEPTH, start), turns, finish, 0)
 
 
 def fetch(pieces, into, sems):
@@ -140,11 +140,13 @@
     return copies
 
 
-def forward_kernel(n, meta, order, col, owner, codes, *refs):
-    pieces, (totals, feat, proj, dbuf, sems) = refs[: 2 * n], refs[2 * n :]
+def forward_kernel(n, meta, order, col, owner, codes, weight, *refs):
+    pieces, (totals, feat, proj, dbuf, sems) = refs[:n], refs[n:]
     turns = meta[0]
     rows = lax.broadcasted_iota(jnp.int32, (128, 128), 0)
-    copies = fetch(pieces[:n], feat, sems.at[0]) + fetch(pieces[n:], proj, sems.at[1])
+    copies = fetch(pieces, feat, sems)
+    size, _, width = pieces[0].shape
+    batch = 4 if size % 4 == 0 else 1
     totals[...] = jnp.zeros_like(totals)
 
     def build(i, slot):
@@ -164,8 +166,16 @@
     def _():
         build(0, 0)
 
-    for copy in copies:
+    def project(t, _):
+        spot = pl.ds(t * batch, batch)
+        held = feat[spot].reshape(batch * 128, width)
+        low = jnp.dot(held, weight[...], preferred_element_type=jnp.float32)
+        proj[spot] = low.astype(jnp.bfloat16).reshape(batch, 128, width)
+        return 0
+
+    for i, copy in enumerate(copies):
         copy.wait()
+        lax.fori_loop(i * size // batch, (i + 1) * size // batch, project, 0)
 
     def turn(i, _):
         slot = lax.rem(i, 2)
@@ -246,49 +256,51 @@
     )(meta, order, dst, col, codes, panel)
 
 
-def run_pack(meta, pos, codes, labels):
+def run_pack(meta, pos, codes, labels, after):
     length = labels.shape[0] * (ROOM + SPARE)
     return pl.pallas_call(
         pack_kernel,
         out_shape=jax.ShapeDtypeStruct((length, 128), jnp.int32),
-        in_specs=[SMEM] * 2 + [VMEM] * 2,
+        in_specs=[SMEM] * 2 + [VMEM] * 2 + [HBM],
         out_specs=VMEM,
         compiler_params=PARAMS,
-    )(meta, pos, codes, labels)
-
-
-def run_build(meta, order, codes):
+    )(meta, pos, codes, labels, after)
+
+
+def run_build(meta, order, codes, after, dense):
+    others = after if dense is None else after + [dense]
     return pl.pallas_call(
         build_kernel,
         out_shape=jax.ShapeDtypeStruct((order.shape[0], 128, 128), jnp.bfloat16),
-        in_specs=[SMEM] * 2 + [VMEM],
+        in_specs=[SMEM] * 2 + [VMEM] + [HBM] * len(others),
         out_specs=HBM,
         scratch_shapes=[
             pltpu.VMEM((DEPTH, GROUP, 128, 128), jnp.bfloat16),
             pltpu.SemaphoreType.DMA((DEPTH,)),
         ],
+        input_output_aliases={} if dense is None else {2 + len(others): 0},
         compiler_params=PARAMS,
-        cost_estimate=cost(order.shape[0], 4),
-    )(meta, order, codes)
-
-
-def run_forward(meta, order, col, owner, codes, feat, proj, row_blocks):
+        cost_estimate=cost(order.shape[0], 2),
+    )(meta, order, codes, *others)
+
+
+def run_forward(meta, order, col, owner, codes, weight, feat, row_blocks):
     n = len(feat)
     size, _, width = feat[0].shape
     return pl.pallas_call(
         functools.partial(forward_kernel, n),
         out_shape=jax.ShapeDtypeStruct((row_blocks, 128, 2 * width), jnp.float32),
-        in_specs=[SMEM] * 4 + [VMEM] + [HBM] * (2 * n),
+        in_specs=[SMEM] * 4 + [VMEM] * 2 + [HBM] * n,
         out_specs=VMEM,
         scratch_shapes=[
             pltpu.VMEM((n * size, 128, width), jnp.bfloat16),
             pltpu.VMEM((n * size, 128, width), jnp.bfloat16),
             pltpu.VMEM((2, 128, GROUP * 128), jnp.bfloat16),
-            pltpu.SemaphoreType.DMA((2, n)),
+            pltpu.SemaphoreType.DMA((n,)),
         ],
         compiler_params=PARAMS,
         cost_estimate=cost(order.shape[0], 8),
-    )(meta, order, col, owner, codes, *feat, *proj)
+    )(meta, order, col, owner, codes, weight, *feat)
 
 
 def run_backward(meta, src, owner, pieces, dense, col_blocks):
@@ -388,25 +400,30 @@
         )
         stride = ROOM + SPARE
         pos = jnp.where(fits, home * stride + rank, ROOM + SPARE - 1)
-        packed = run_pack(turns_plain, pos, codes, labels)
-        came = lax.all_to_all(
-            packed.reshape(n_col, stride, 128), "col", split_axis=0, concat_axis=0, tiled=True
-        )
-        spread = total_sum(jnp.max(came[:, ROOM, ROOM:], axis=0)[None], ("row",))
-        any_over = jnp.max(spread) > 0
+        state = {}
+
+        def exchange(step, held):
+            if step == 0:
+                packed = run_pack(turns_plain, pos, codes, labels, held[0])
+                state["came"] = lax.all_to_all(
+                    packed.reshape(n_col, stride, 128),
+                    "col",
+                    split_axis=0,
+                    concat_axis=0,
+                    tiled=True,
+                )
 
         feat = []
-        for pair in gather_pieces(features.reshape(per, 128, width)):
+        for pair in gather_pieces(features.reshape(per, 128, width), exchange):
             rows = [pair]
             for bit in bits_of("row"):
                 rows = rows + [[swap(x, "row", bit) for x in pair] for pair in rows]
             feat += [x for pair in rows for x in pair]
-        proj = [
-            jnp.dot(x.reshape(-1, width), weight, preferred_element_type=jnp.float32)
-            .astype(jnp.bfloat16)
-            .reshape(x.shape)
-            for x in feat
-        ]
+        came = state["came"]
+        spread = jnp.max(came[:, ROOM, ROOM:], axis=0)[None]
+        for bit in bits_of("row"):
+            spread = spread + swap(spread, "row", bit)
+        any_over = jnp.max(spread) > 0
 
         got = came[:, ROOM, :ROOM]
         sources = jnp.arange(n_col, dtype=jnp.int32)[:, None]
@@ -426,8 +443,8 @@
             cols,
             owner,
             came.reshape(n_col * stride, 128),
+            weight,
             feat,
-            proj,
             per,
         ).reshape(node_dev, 2 * width)
         own = lax.cond(any_over, tile_plan, lambda: own)
@@ -437,15 +454,20 @@
     pos, back_owner, back_turns, length = grouped(bcol, live, col_blocks)
     back_order = place(pos, ids, length, slots)
     back_src = place(pos, piece_index(per, home ^ mine, brow % per), length, 0)
-    back_turns = back_turns.reshape(1)
-    dense = run_build(back_turns, back_order, codes)
+    parts = [0, 1, 2, 4]
+    state = {"dense": None}
+
+    def build(step, held):
+        if step + 1 < len(parts):
+            span = jnp.stack([back_turns * part // 4 for part in parts[step : step + 2]])
+            state["dense"] = run_build(span, back_order, codes, held, state["dense"])
 
     pre = own[:, :width] + bias
     output = jnp.maximum(pre, 0.0).astype(jnp.bfloat16)
     grad_own = jnp.where(pre > 0, cotangent.astype(jnp.float32), 0.0).astype(jnp.bfloat16)
     local_bias = jnp.sum(grad_own.astype(jnp.float32), axis=0)
     turned = jnp.swapaxes(grad_own.reshape(per, 128, width), 1, 2)
-    grad = [x for pair in gather_pieces(turned) for x in pair]
+    grad = [x for pair in gather_pieces(turned, build) for x in pair]
     local_weight = lax.dot_general(
         own[:, width:].astype(jnp.bfloat16),
         grad_own,
@@ -453,9 +475,14 @@
         preferred_element_type=jnp.float32,
     )
     local = jnp.concatenate([local_weight, jnp.tile(local_bias[None], (8, 1))], axis=0)
-    total = total_sum(local, ("row", "col"))
-
-    acc = run_backward(back_turns, back_src, back_owner, grad, dense, col_blocks)
+    steps = total_steps()
+    for axis, bit in steps[:-1]:
+        local = local + swap(local, axis, bit)
+    acc = run_backward(
+        back_turns.reshape(1), back_src, back_owner, grad, state["dense"], col_blocks
+    )
+    acc, local = lax.optimization_barrier((acc, local))
+    total = local + swap(local, *steps[-1])
     back = jnp.swapaxes(acc, 1, 2).reshape(col_blocks * 128, width)
     grad_proj = scatter_sum(
         jnp.stack(

time: 177 us -> 163 us (0.921)
  the two profiles are of different devices: /device:TPU:23 before, /device:TPU:18 now
where the time goes in v3:
time: 163 us; the launch traced here: 161 us
  Pallas kernels  65.5 us (40%)
  starting transfers between devices  33.2 us (20%)
  waiting for transfers between devices  28.2 us (17%)
  other arithmetic  17.8 us (11%)
  between operations  8.3 us (5%)
  local copies, waits for them, and re-layouts  6.02 us (4%)
  matrix products  2.04 us (1%)
    ppermute x27, waiting for transfers between devices, swap(): return lax.ppermute(x, axis, [(i, i ^ bit) for i in range(n)])  28.1 us
    ppermute x27, starting transfers between devices, swap(): return lax.ppermute(x, axis, [(i, i ^ bit) for i in range(n)])  26.5 us
    pallas_call x3, Pallas kernels, run_build(): pl.pallas_call(build_kernel, out_shape=jax.ShapeDtypeStruct((order.shape[...  25.2 us
    pallas_call x1, Pallas kernels, run_forward(): pl.pallas_call(functools.partial(forward_kernel, n), out_shape=jax.ShapeD...  21.3 us
    pallas_call x1, Pallas kernels, run_backward(): pl.pallas_call(functools.partial(backward_kernel, n), out_shape=jax.Shape...  17 us
    all_to_all x1, starting transfers between devices, exchange(): lax.all_to_all(packed.reshape(n_col, stride, 128), 'col', split_axis=0, c...  6.76 us
  transfers between devices with their start and end apart: 28, of which 7 were waited for; matrix products, arithmetic and copies ran while one was open for 13% of the time, Pallas kernels for 17%

profile of v3, /device:TPU:18, one launch (start us, length us, event | category | flops | bytes accessed | tf_op | source)
XLA Modules:
  0.0 161.1 jit_solution(14465608185339169980)
XLA Ops:
  1.9 2.6 %collective-permute-start.11 = (bf16[1,2,128,128]{3,2,1,0:T(8,128)(2,1)S(1)}, bf16[1,2,128,128]{3,2,1,0:T(8,128)(2,1)S(1)}, u32[]{:S(2)}, u32[]{:S(2)}) collective-permute-start(bf16[1,2,128,128]{3,2,1,0:T(8,128)(2,1)S(1)} %bitcast.133), channel_id=1, source_target_pairs={{0,8},{1,9},{2,10},{3,11},{4,12},{5,13},{6,14},{7,15},{8,0},{9,1},... | collective-permute-start | bytes 196616 | tf_op jit(solution)/shard_map/ppermute | solution.py:13
  10.5 1.6 %collective-permute-start.6 = (bf16[2,2,128,128]{3,2,1,0:T(8,128)(2,1)S(1)}, bf16[2,2,128,128]{3,2,1,0:T(8,128)(2,1)S(1)}, u32[]{:S(2)}, u32[]{:S(2)}) collective-permute-start(bf16[2,2,128,128]{3,2,1,0:T(8,128)(2,1)S(1)} %pad_maximum_fusion.9.after), channel_id=1, source_target_pairs={{0,4},{1,5},{2,6},{3,7},{4,0},{5,1},{6,2},{7,3},{8,12},{9,13},{10,... | collective-permute-start | bytes 393224 | tf_op jit(solution)/shard_map/ppermute | solution.py:13
  16.1 2.1 %shard_map.120 = s32[1152,128]{1,0:T(8,128)} custom-call(s32[1]{0:T(128)} %bitcast.16.meta, s32[512]{0:T(512)S(1)} %get-tuple-element.120.pos, s32[520,128]{1,0:T(8,128)S(1)} %pad.5.codes, s32[16,128]{1,0:T(8,128)S(1)} %concatenate.53.labels, bf16[2,2,128,128]{3,2,1,0:T(8,128)(2,1)S(1)} %pad_maximum_fusion.9.after), custom_call_target="tpu_custom_call" | custom-call | tf_op jit(solution)/shard_map/pallas_call | solution.py:261
  18.1 6.8 %all-to-all-start = ((s32[16,72,128]{2,1,0:T(8,128)}), s32[16,72,128]{2,1,0:T(8,128)S(1)}, u32[]{:S(2)}, u32[]{:S(2)}) async-start(s32[16,72,128]{2,1,0:T(8,128)} %bitcast.21), calls=%async_computation | async-start | bytes 1179648 | tf_op jit(solution)/shard_map/all_to_all | solution.py:408
  24.9 1.5 collective-permute-start.7
  30.9 6.2 %collective-permute-done.7 = bf16[4,2,128,128]{3,2,1,0:T(8,128)(2,1)S(1)} collective-permute-done((bf16[4,2,128,128]{3,2,1,0:T(8,128)(2,1)S(1)}, bf16[4,2,128,128]{3,2,1,0:T(8,128)(2,1)S(1)}, u32[]{:S(2)}, u32[]{:S(2)}) %collective-permute-start.7) | collective-permute-done | bytes 262176 | tf_op jit(solution)/shard_map/ppermute | solution.py:13
  37.2 1.9 %collective-permute-done.13 = bf16[4,2,128,128]{3,2,1,0:T(8,128)(2,1)S(1)} collective-permute-done((bf16[4,2,128,128]{3,2,1,0:T(8,128)(2,1)S(1)}, bf16[4,2,128,128]{3,2,1,0:T(8,128)(2,1)S(1)}, u32[]{:S(2)}, u32[]{:S(2)}) %collective-permute-start.13) | collective-permute-done | bytes 262176 | tf_op jit(solution)/shard_map/ppermute | solution.py:13
  39.8 9.8 %collective-permute-done.8 = bf16[8,2,128,128]{3,2,1,0:T(8,128)(2,1)S(1)} collective-permute-done((bf16[8,2,128,128]{3,2,1,0:T(8,128)(2,1)S(1)}, bf16[8,2,128,128]{3,2,1,0:T(8,128)(2,1)S(1)}, u32[]{:S(2)}, u32[]{:S(2)}) %collective-permute-start.8) | collective-permute-done | bytes 524320 | tf_op jit(solution)/shard_map/ppermute | solution.py:13
  51.0 1.4 select_select_fusion
  58.8 2.0 %select_reduce_fusion = (s32[1064]{0:T(1024)S(1)}, s32[1064]{0:T(1024)S(1)}) fusion(s32[1024]{0:T(1024)} %get-tuple-element.117, s32[1024]{0:T(1024)S(1)} %add_select_fusion.7, s32[1024]{0:T(1024)S(1)} %sub.113), kind=kLoop, calls=%fused_computation.23 | loop fusion | flops 5445552 | bytes 20800 | tf_op jit(solution)/shard_map/reduce_sum | solution.py:345
  60.9 1.3 add_reduce_fusion.1
  62.9 21.3 %shard_map.121 = f32[4,128,256]{2,1,0:T(8,128)} custom-call(s32[1]{0:T(128)} %bitcast.23.meta, s32[1064]{0:T(1024)S(1)} %broadcast_add_fusion.order, s32[1064]{0:T(1024)S(1)} %get-tuple-element.96.col, s32[132]{0:T(256)S(1)} %broadcast_minimum_fusion.owner, s32[1152,128]{1,0:T(8,128)S(1)} %bitcast.113, bf16[128,128]{1,0:T(8,128)(2,1)S(1)} %copy-done.2, ...), custom_call_target="tpu_custom_call" | custom-call | flops 35701915648 | bytes 34865152 | tf_op jit(solution)/shard_map/pallas_call | solution.py:290
  85.1 1.7 %convert_reduce_fusion.3 = (f32[128]{0:T(128)S(1)}, bf16[512,128]{1,0:T(8,128)(2,1)S(1)}, bf16[512,128]{1,0:T(8,128)(2,1)}) fusion(bf16[512,128]{1,0:T(8,128)(2,1)S(1)} %copy-done.1, f32[128]{0:T(128)S(1)} %copy-done.4, f32[512,256]{1,0:T(8,128)} %get-tuple-element.131), kind=kLoop, calls=%fused_computation.57 | loop fusion | flops 589696 | bytes 656384 | tf_op jit(solution)/shard_map/reduce_sum | solution.py:468
  88.8 2.3 %collective-permute-start.25 = (f32[136,128]{1,0:T(8,128)S(1)}, f32[136,128]{1,0:T(8,128)S(1)}, u32[]{:S(2)}, u32[]{:S(2)}) collective-permute-start(f32[136,128]{1,0:T(8,128)S(1)} %pad_maximum_fusion.13), channel_id=1, source_target_pairs={{0,16},{16,0},{1,17},{17,1},{2,18},{18,2},{3,19},{19,3},{4,20},{20... | collective-permute-start | bytes 208904 | tf_op jit(solution)/shard_map/ppermute | solution.py:13
  93.7 5.5 %collective-permute-start.21 = (bf16[2,2,128,128]{3,2,1,0:T(8,128)(2,1)S(1)}, bf16[2,2,128,128]{3,2,1,0:T(8,128)(2,1)S(1)}, u32[]{:S(2)}, u32[]{:S(2)}) collective-permute-start(bf16[2,2,128,128]{3,2,1,0:T(8,128)(2,1)S(1)} %pad_maximum_fusion.12.refs_1_), channel_id=1, source_target_pairs={{0,4},{1,5},{2,6},{3,7},{4,0},{5,1},{6,2},{7,3},{8,12},{9,13},{10,... | collective-permute-start | bytes 393224 | tf_op jit(solution)/shard_map/ppermute | solution.py:13
  101.2 4.9 %collective-permute-done.26 = f32[136,128]{1,0:T(8,128)S(1)} collective-permute-done((f32[136,128]{1,0:T(8,128)S(1)}, f32[136,128]{1,0:T(8,128)S(1)}, u32[]{:S(2)}, u32[]{:S(2)}) %collective-permute-start.26) | collective-permute-done | bytes 69664 | tf_op jit(solution)/shard_map/ppermute | solution.py:13
  106.1 1.8 %collective-permute-start.27 = (f32[136,128]{1,0:T(8,128)S(1)}, f32[136,128]{1,0:T(8,128)S(1)}, u32[]{:S(2)}, u32[]{:S(2)}) collective-permute-start(f32[136,128]{1,0:T(8,128)S(1)} %add.622), channel_id=1, source_target_pairs={{0,4},{1,5},{2,6},{3,7},{4,0},{5,1},{6,2},{7,3},{8,12},{9,13},{10,... | collective-permute-start | bytes 208904 | tf_op jit(solution)/shard_map/ppermute | solution.py:13
  108.3 1.4 collective-permute-start.19
  109.7 6.6 %shard_map.122.refs_2_ = bf16[576,128,128]{2,1,0:T(8,128)(2,1)} custom-call(s32[2]{0:T(128)S(1)} %pad_add_fusion.2.meta, s32[576]{0:T(1024)S(1)} %broadcast_add_fusion.1.order, s32[520,128]{1,0:T(8,128)S(1)} %pad.5.codes, bf16[2,2,128,128]{3,2,1,0:T(8,128)(2,1)S(1)} %pad_maximum_fusion.11.refs_0_, bf16[2,2,128,128]{3,2,1,0:T(8,128)(2,1)S(1)} %pad_maximum_fusion.12.refs_1_), custom_call_target="tpu_custom_call" | custom-call | flops 4831838208 | bytes 18874368 | tf_op jit(solution)/shard_map/pallas_call | solution.py:272
  116.9 1.7 %collective-permute-start.24 = (bf16[8,2,128,128]{3,2,1,0:T(8,128)(2,1)S(1)}, bf16[8,2,128,128]{3,2,1,0:T(8,128)(2,1)S(1)}, u32[]{:S(2)}, u32[]{:S(2)}) collective-permute-start(bf16[8,2,128,128]{3,2,1,0:T(8,128)(2,1)S(1)} %pad_maximum_fusion.4.refs_1_), channel_id=1, source_target_pairs={{0,2},{1,3},{2,0},{3,1},{4,6},{5,7},{6,4},{7,5},{8,10},{9,11},{10,... | collective-permute-start | bytes 1572872 | tf_op jit(solution)/shard_map/ppermute | solution.py:13
  119.1 6.6 %shard_map.123.refs_2_ = bf16[576,128,128]{2,1,0:T(8,128)(2,1)} custom-call(s32[2]{0:T(128)S(1)} %pad_add_fusion.1.meta, s32[576]{0:T(1024)S(1)} %broadcast_add_fusion.1.order, s32[520,128]{1,0:T(8,128)S(1)} %pad.5.codes, bf16[4,2,128,128]{3,2,1,0:T(8,128)(2,1)S(1)} %pad_maximum_fusion.7.refs_0_, ...), custom_call_target="tpu_custom_call", output_to_operand_aliasing={{}: (5, {})} | custom-call | flops 4831838208 | bytes 18874368 | tf_op jit(solution)/shard_map/pallas_call | solution.py:272
  125.8 11.9 %shard_map.124.dense = bf16[576,128,128]{2,1,0:T(8,128)(2,1)} custom-call(s32[2]{0:T(128)S(1)} %pad_add_fusion.meta, s32[576]{0:T(1024)S(1)} %broadcast_add_fusion.1.order, s32[520,128]{1,0:T(8,128)S(1)} %pad.5.codes, bf16[8,2,128,128]{3,2,1,0:T(8,128)(2,1)S(1)} %pad_maximum_fusion.3.refs_0_, ...), custom_call_target="tpu_custom_call", output_to_operand_aliasing={{}: (5, {})} | custom-call | flops 4831838208 | bytes 18874368 | tf_op jit(solution)/shard_map/pallas_call | solution.py:272
  137.7 17.0 %shard_map.125 = f32[8,128,128]{2,1,0:T(8,128)S(1)} custom-call(s32[1]{0:T(128)} %bitcast.30.meta, s32[576]{0:T(1024)S(1)} %get-tuple-element.99.src, s32[72]{0:T(128)S(1)} %broadcast_minimum_fusion.1.owner, bf16[576,128,128]{2,1,0:T(8,128)(2,1)} %shard_map.124.dense, bf16[16,128,128]{2,1,0:T(8,128)(2,1)S(1)} %bitcast.111, ...), custom_call_target="tpu_custom_call" | custom-call | flops 9663676416 | bytes 18874368 | tf_op jit(solution)/shard_map/pallas_call | solution.py:309
  155.2 3.9 %collective-permute-done.30 = f32[136,128]{1,0:T(8,128)S(1)} collective-permute-done((f32[136,128]{1,0:T(8,128)S(1)}, f32[136,128]{1,0:T(8,128)S(1)}, u32[]{:S(2)}, u32[]{:S(2)}) %collective-permute-start.30) | collective-permute-done | bytes 69664 | tf_op jit(solution)/shard_map/ppermute | solution.py:13
  (133 shorter events, 29.1 us)
Async XLA Ops:
  1.5 8.9 %collective-permute-start.4 = (bf16[1,2,128,128]{3,2,1,0:T(8,128)(2,1)S(1)}, bf16[1,2,128,128]{3,2,1,0:T(8,128)(2,1)S(1)}, u32[]{:S(2)}, u32[]{:S(2)}) collective-permute-start(bf16[1,2,128,128]{3,2,1,0:T(8,128)(2,1)S(1)} %bitcast.137), channel_id=1, source_target_pairs={{0,8},{1,9},{2,10},{3,11},{4,12},{5,13},{6,14},{7,15},{8,0},{9,1},... | collective-permute-start | bytes 196616 | tf_op jit(solution)/shard_map/ppermute | solution.py:13
  1.9 10.2 %collective-permute-start.11 = (bf16[1,2,128,128]{3,2,1,0:T(8,128)(2,1)S(1)}, bf16[1,2,128,128]{3,2,1,0:T(8,128)(2,1)S(1)}, u32[]{:S(2)}, u32[]{:S(2)}) collective-permute-start(bf16[1,2,128,128]{3,2,1,0:T(8,128)(2,1)S(1)} %bitcast.133), channel_id=1, source_target_pairs={{0,8},{1,9},{2,10},{3,11},{4,12},{5,13},{6,14},{7,15},{8,0},{9,1},... | collective-permute-start | bytes 196616 | tf_op jit(solution)/shard_map/ppermute | solution.py:13
  10.5 14.4 %collective-permute-start.6 = (bf16[2,2,128,128]{3,2,1,0:T(8,128)(2,1)S(1)}, bf16[2,2,128,128]{3,2,1,0:T(8,128)(2,1)S(1)}, u32[]{:S(2)}, u32[]{:S(2)}) collective-permute-start(bf16[2,2,128,128]{3,2,1,0:T(8,128)(2,1)S(1)} %pad_maximum_fusion.9.after), channel_id=1, source_target_pairs={{0,4},{1,5},{2,6},{3,7},{4,0},{5,1},{6,2},{7,3},{8,12},{9,13},{10,... | collective-permute-start | bytes 393224 | tf_op jit(solution)/shard_map/ppermute | solution.py:13
  12.1 14.3 %collective-permute-start.12 = (bf16[2,2,128,128]{3,2,1,0:T(8,128)(2,1)S(1)}, bf16[2,2,128,128]{3,2,1,0:T(8,128)(2,1)S(1)}, u32[]{:S(2)}, u32[]{:S(2)}) collective-permute-start(bf16[2,2,128,128]{3,2,1,0:T(8,128)(2,1)S(1)} %pad_maximum_fusion.10), channel_id=1, source_target_pairs={{0,4},{1,5},{2,6},{3,7},{4,0},{5,1},{6,2},{7,3},{8,12},{9,13},{10,... | collective-permute-start | bytes 393224 | tf_op jit(solution)/shard_map/ppermute | solution.py:13
  18.1 32.0 %all-to-all-start = ((s32[16,72,128]{2,1,0:T(8,128)}), s32[16,72,128]{2,1,0:T(8,128)S(1)}, u32[]{:S(2)}, u32[]{:S(2)}) async-start(s32[16,72,128]{2,1,0:T(8,128)} %bitcast.21), calls=%async_computation | async-start | bytes 1179648 | tf_op jit(solution)/shard_map/all_to_all | solution.py:408
  24.9 12.1 %collective-permute-start.7 = (bf16[4,2,128,128]{3,2,1,0:T(8,128)(2,1)S(1)}, bf16[4,2,128,128]{3,2,1,0:T(8,128)(2,1)S(1)}, u32[]{:S(2)}, u32[]{:S(2)}) collective-permute-start(bf16[4,2,128,128]{3,2,1,0:T(8,128)(2,1)S(1)} %pad_maximum_fusion.5), channel_id=1, source_target_pairs={{0,2},{1,3},{2,0},{3,1},{4,6},{5,7},{6,4},{7,5},{8,10},{9,11},{10,... | collective-permute-start | bytes 786440 | tf_op jit(solution)/shard_map/ppermute | solution.py:13
  26.5 12.5 %collective-permute-start.13 = (bf16[4,2,128,128]{3,2,1,0:T(8,128)(2,1)S(1)}, bf16[4,2,128,128]{3,2,1,0:T(8,128)(2,1)S(1)}, u32[]{:S(2)}, u32[]{:S(2)}) collective-permute-start(bf16[4,2,128,128]{3,2,1,0:T(8,128)(2,1)S(1)} %pad_maximum_fusion.6), channel_id=1, source_target_pairs={{0,1},{1,0},{2,3},{3,2},{4,5},{5,4},{6,7},{7,6},{8,9},{9,8},{10,11... | collective-permute-start | bytes 786440 | tf_op jit(solution)/shard_map/ppermute | solution.py:13
  37.1 12.5 %collective-permute-start.8 = (bf16[8,2,128,128]{3,2,1,0:T(8,128)(2,1)S(1)}, bf16[8,2,128,128]{3,2,1,0:T(8,128)(2,1)S(1)}, u32[]{:S(2)}, u32[]{:S(2)}) collective-permute-start(bf16[8,2,128,128]{3,2,1,0:T(8,128)(2,1)S(1)} %pad_maximum_fusion.1), channel_id=1, source_target_pairs={{0,1},{1,0},{2,3},{3,2},{4,5},{5,4},{6,7},{7,6},{8,9},{9,8},{10,11... | collective-permute-start | bytes 1572872 | tf_op jit(solution)/shard_map/ppermute | solution.py:13
  39.1 10.7 %collective-permute-start.14 = (bf16[8,2,128,128]{3,2,1,0:T(8,128)(2,1)S(1)}, bf16[8,2,128,128]{3,2,1,0:T(8,128)(2,1)S(1)}, u32[]{:S(2)}, u32[]{:S(2)}) collective-permute-start(bf16[8,2,128,128]{3,2,1,0:T(8,128)(2,1)S(1)} %pad_maximum_fusion.2), channel_id=1, source_target_pairs={{0,2},{1,3},{2,0},{3,1},{4,6},{5,7},{6,4},{7,5},{8,10},{9,11},{10,... | collective-permute-start | bytes 1572872 | tf_op jit(solution)/shard_map/ppermute | solution.py:13
  39.3 23.6 %collective-permute-start.9 = (bf16[16,128,128]{2,1,0:T(8,128)(2,1)S(1)}, bf16[16,128,128]{2,1,0:T(8,128)(2,1)S(1)}, u32[]{:S(2)}, u32[]{:S(2)}) collective-permute-start(bf16[16,128,128]{2,1,0:T(8,128)(2,1)S(1)} %bitcast.114), channel_id=1, source_target_pairs={{0,16},{16,0},{1,17},{17,1},{2,18},{18,2},{3,19},{19,3},{4,20},{20... | collective-permute-start | bytes 1572872 | tf_op jit(solution)/shard_map/ppermute | solution.py:13
  39.3 23.5 %collective-permute-start.15 = (bf16[16,128,128]{2,1,0:T(8,128)(2,1)S(1)}, bf16[16,128,128]{2,1,0:T(8,128)(2,1)}, u32[]{:S(2)}, u32[]{:S(2)}) collective-permute-start(bf16[16,128,128]{2,1,0:T(8,128)(2,1)S(1)} %bitcast.116), channel_id=1, source_target_pairs={{0,16},{16,0},{1,17},{17,1},{2,18},{18,2},{3,19},{19,3},{4,20},{20... | collective-permute-start | bytes 1572872 | tf_op jit(solution)/shard_map/ppermute | solution.py:13
  49.6 13.3 %collective-permute-start.10 = (bf16[16,128,128]{2,1,0:T(8,128)(2,1)S(1)}, bf16[16,128,128]{2,1,0:T(8,128)(2,1)}, u32[]{:S(2)}, u32[]{:S(2)}) collective-permute-start(bf16[16,128,128]{2,1,0:T(8,128)(2,1)S(1)} %bitcast.119), channel_id=1, source_target_pairs={{0,16},{16,0},{1,17},{17,1},{2,18},{18,2},{3,19},{19,3},{4,20},{20... | collective-permute-start | bytes 1572872 | tf_op jit(solution)/shard_map/ppermute | solution.py:13
  49.8 13.1 %collective-permute-start.16 = (bf16[16,128,128]{2,1,0:T(8,128)(2,1)S(1)}, bf16[16,128,128]{2,1,0:T(8,128)(2,1)}, u32[]{:S(2)}, u32[]{:S(2)}) collective-permute-start(bf16[16,128,128]{2,1,0:T(8,128)(2,1)S(1)} %bitcast.121), channel_id=1, source_target_pairs={{0,16},{16,0},{1,17},{17,1},{2,18},{18,2},{3,19},{19,3},{4,20},{20... | collective-permute-start | bytes 1572872 | tf_op jit(solution)/shard_map/ppermute | solution.py:13
  88.8 11.6 %collective-permute-start.25 = (f32[136,128]{1,0:T(8,128)S(1)}, f32[136,128]{1,0:T(8,128)S(1)}, u32[]{:S(2)}, u32[]{:S(2)}) collective-permute-start(f32[136,128]{1,0:T(8,128)S(1)} %pad_maximum_fusion.13), channel_id=1, source_target_pairs={{0,16},{16,0},{1,17},{17,1},{2,18},{18,2},{3,19},{19,3},{4,20},{20... | collective-permute-start | bytes 208904 | tf_op jit(solution)/shard_map/ppermute | solution.py:13
  91.1 8.1 %collective-permute-start.17 = (bf16[1,2,128,128]{3,2,1,0:T(8,128)(2,1)S(1)}, bf16[1,2,128,128]{3,2,1,0:T(8,128)(2,1)S(1)}, u32[]{:S(2)}, u32[]{:S(2)}) collective-permute-start(bf16[1,2,128,128]{3,2,1,0:T(8,128)(2,1)S(1)} %get-tuple-element.114), channel_id=1, source_target_pairs={{0,8},{1,9},{2,10},{3,11},{4,12},{5,13},{6,14},{7,15},{8,0},{9,1},... | collective-permute-start | bytes 196616 | tf_op jit(solution)/shard_map/ppermute | solution.py:13
  93.7 14.2 %collective-permute-start.21 = (bf16[2,2,128,128]{3,2,1,0:T(8,128)(2,1)S(1)}, bf16[2,2,128,128]{3,2,1,0:T(8,128)(2,1)S(1)}, u32[]{:S(2)}, u32[]{:S(2)}) collective-permute-start(bf16[2,2,128,128]{3,2,1,0:T(8,128)(2,1)S(1)} %pad_maximum_fusion.12.refs_1_), channel_id=1, source_target_pairs={{0,4},{1,5},{2,6},{3,7},{4,0},{5,1},{6,2},{7,3},{8,12},{9,13},{10,... | collective-permute-start | bytes 393224 | tf_op jit(solution)/shard_map/ppermute | solution.py:13
  99.2 9.0 %collective-permute-start.18 = (bf16[2,2,128,128]{3,2,1,0:T(8,128)(2,1)S(1)}, bf16[2,2,128,128]{3,2,1,0:T(8,128)(2,1)S(1)}, u32[]{:S(2)}, u32[]{:S(2)}) collective-permute-start(bf16[2,2,128,128]{3,2,1,0:T(8,128)(2,1)S(1)} %pad_maximum_fusion.11.refs_0_), channel_id=1, source_target_pairs={{0,4},{1,5},{2,6},{3,7},{4,0},{5,1},{6,2},{7,3},{8,12},{9,13},{10,... | collective-permute-start | bytes 393224 | tf_op jit(solution)/shard_map/ppermute | solution.py:13
  100.3 5.8 %collective-permute-start.26 = (f32[136,128]{1,0:T(8,128)S(1)}, f32[136,128]{1,0:T(8,128)S(1)}, u32[]{:S(2)}, u32[]{:S(2)}) collective-permute-start(f32[136,128]{1,0:T(8,128)S(1)} %fusion.51), channel_id=1, source_target_pairs={{0,8},{1,9},{2,10},{3,11},{4,12},{5,13},{6,14},{7,15},{8,0},{9,1},... | collective-permute-start | bytes 208904 | tf_op jit(solution)/shard_map/ppermute | solution.py:13
  106.1 10.2 %collective-permute-start.27 = (f32[136,128]{1,0:T(8,128)S(1)}, f32[136,128]{1,0:T(8,128)S(1)}, u32[]{:S(2)}, u32[]{:S(2)}) collective-permute-start(f32[136,128]{1,0:T(8,128)S(1)} %add.622), channel_id=1, source_target_pairs={{0,4},{1,5},{2,6},{3,7},{4,0},{5,1},{6,2},{7,3},{8,12},{9,13},{10,... | collective-permute-start | bytes 208904 | tf_op jit(solution)/shard_map/ppermute | solution.py:13
  107.9 8.9 %collective-permute-start.22 = (bf16[4,2,128,128]{3,2,1,0:T(8,128)(2,1)S(1)}, bf16[4,2,128,128]{3,2,1,0:T(8,128)(2,1)S(1)}, u32[]{:S(2)}, u32[]{:S(2)}) collective-permute-start(bf16[4,2,128,128]{3,2,1,0:T(8,128)(2,1)S(1)} %pad_maximum_fusion.8.refs_1_), channel_id=1, source_target_pairs={{0,1},{1,0},{2,3},{3,2},{4,5},{5,4},{6,7},{7,6},{8,9},{9,8},{10,11... | collective-permute-start | bytes 786440 | tf_op jit(solution)/shard_map/ppermute | solution.py:13
  108.3 10.3 %collective-permute-start.19 = (bf16[4,2,128,128]{3,2,1,0:T(8,128)(2,1)S(1)}, bf16[4,2,128,128]{3,2,1,0:T(8,128)(2,1)S(1)}, u32[]{:S(2)}, u32[]{:S(2)}) collective-permute-start(bf16[4,2,128,128]{3,2,1,0:T(8,128)(2,1)S(1)} %pad_maximum_fusion.7.refs_0_), channel_id=1, source_target_pairs={{0,2},{1,3},{2,0},{3,1},{4,6},{5,7},{6,4},{7,5},{8,10},{9,11},{10,... | collective-permute-start | bytes 786440 | tf_op jit(solution)/shard_map/ppermute | solution.py:13
  116.4 9.4 %collective-permute-start.28 = (f32[136,128]{1,0:T(8,128)S(1)}, f32[136,128]{1,0:T(8,128)S(1)}, u32[]{:S(2)}, u32[]{:S(2)}) collective-permute-start(f32[136,128]{1,0:T(8,128)S(1)} %add.623), channel_id=1, source_target_pairs={{0,2},{1,3},{2,0},{3,1},{4,6},{5,7},{6,4},{7,5},{8,10},{9,11},{10,... | collective-permute-start | bytes 208904 | tf_op jit(solution)/shard_map/ppermute | solution.py:13
  116.9 20.8 %collective-permute-start.24 = (bf16[8,2,128,128]{3,2,1,0:T(8,128)(2,1)S(1)}, bf16[8,2,128,128]{3,2,1,0:T(8,128)(2,1)S(1)}, u32[]{:S(2)}, u32[]{:S(2)}) collective-permute-start(bf16[8,2,128,128]{3,2,1,0:T(8,128)(2,1)S(1)} %pad_maximum_fusion.4.refs_1_), channel_id=1, source_target_pairs={{0,2},{1,3},{2,0},{3,1},{4,6},{5,7},{6,4},{7,5},{8,10},{9,11},{10,... | collective-permute-start | bytes 1572872 | tf_op jit(solution)/shard_map/ppermute | solution.py:13
  118.7 19.1 %collective-permute-start.23 = (bf16[8,2,128,128]{3,2,1,0:T(8,128)(2,1)S(1)}, bf16[8,2,128,128]{3,2,1,0:T(8,128)(2,1)S(1)}, u32[]{:S(2)}, u32[]{:S(2)}) collective-permute-start(bf16[8,2,128,128]{3,2,1,0:T(8,128)(2,1)S(1)} %pad_maximum_fusion.3.refs_0_), channel_id=1, source_target_pairs={{0,1},{1,0},{2,3},{3,2},{4,5},{5,4},{6,7},{7,6},{8,9},{9,8},{10,11... | collective-permute-start | bytes 1572872 | tf_op jit(solution)/shard_map/ppermute | solution.py:13
  (8 other events, 85.4 us)

commit v4 on v3

--- a/solution.py
+++ b/solution.py
@@ -31,15 +31,14 @@
     return [bits, turned] if per % 2 == 0 and len(bits) > 1 else [bits]
 
 
-def gather_pieces(blocks, beside=None):
+def gather_pieces(blocks, beside):
     orders = part_orders(blocks.shape[0])
     size = blocks.shape[0] // len(orders)
     held = [blocks[i * size : (i + 1) * size][None] for i in range(len(orders))]
     for step in range(len(orders[0]) - 1):
         came = [swap(x, "col", order[step]) for x, order in zip(held, orders)]
         held = [jnp.concatenate([x, y], axis=0) for x, y in zip(held, came)]
-        if beside is not None:
-            beside(step, held)
+        held = beside(step, held)
     came = [swap(x, "col", order[-1]) for x, order in zip(held, orders)]
     shape = (-1,) + blocks.shape[1:]
     return [[x.reshape(shape), y.reshape(shape)] for x, y in zip(held, came)]
@@ -59,7 +58,16 @@
 
 
 def total_steps():
-    return [("row", bit) for bit in bits_of("row")] + [("col", bit) for bit in bits_of("col")[::-1]]
+    bits = bits_of("col")[::-1]
+    steps = [("row", [bit]) for bit in bits_of("row")]
+    return steps + [("col", bits[i : i + 2]) for i in range(0, len(bits), 2)]
+
+
+def total_step(x, axis, bits):
+    if len(bits) == 1:
+        return x + swap(x, axis, bits[0])
+    near, far, both = [swap(x, axis, bit) for bit in (bits[0], bits[1], bits[0] ^ bits[1])]
+    return (x + near) + (far + both)
 
 
 GROUP = 8
@@ -70,11 +78,22 @@
 UNIT = 2.0**-14
 
 
+def tile_rows():
+    shape = (8, 16, 128)
+    rows = 16 * lax.broadcasted_iota(jnp.int32, shape, 0) + lax.broadcasted_iota(jnp.int32, shape, 1)
+    return rows.astype(jnp.float32).astype(jnp.bfloat16)
+
+
 def block_of(code, rows):
+    def tile(x):
+        return jnp.broadcast_to(x.astype(jnp.float32), (16, 128)).astype(jnp.bfloat16)[None]
+
     o = code >> 16
-    w = (code & (FIELD - 1)).astype(jnp.float32) * UNIT
-    left = jnp.where(rows == (o >> 7), w, 0.0).astype(jnp.bfloat16)
-    right = jnp.where(rows == (o & 127), 1.0, 0.0).astype(jnp.bfloat16)
+    zero = jnp.zeros((), jnp.bfloat16)
+    one = jnp.ones((), jnp.bfloat16)
+    w = tile((code & (FIELD - 1)).astype(jnp.float32) * UNIT)
+    left = jnp.where(rows == tile(o >> 7), w, zero).reshape(128, 128)
+    right = jnp.where(rows == tile(o & 127), one, zero).reshape(128, 128)
     return lax.dot_general(
         left, right, (((1,), (1,)), ((), ())), preferred_element_type=jnp.float32
     ).astype(jnp.bfloat16)
@@ -98,7 +117,7 @@
 def build_kernel(meta, order, codes, *refs):
     dense, dbuf, sems = refs[-3:]
     start, turns = meta[0], meta[1]
-    rows = lax.broadcasted_iota(jnp.int32, (128, 128), 0)
+    rows = tile_rows()
 
     def out_copy(i):
         slot = lax.rem(i, DEPTH)
@@ -143,7 +162,7 @@
 def forward_kernel(n, meta, order, col, owner, codes, weight, *refs):
     pieces, (totals, feat, proj, dbuf, sems) = refs[:n], refs[n:]
     turns = meta[0]
-    rows = lax.broadcasted_iota(jnp.int32, (128, 128), 0)
+    rows = tile_rows()
     copies = fetch(pieces, feat, sems)
     size, _, width = pieces[0].shape
     batch = 4 if size % 4 == 0 else 1
@@ -188,7 +207,7 @@
 
 
 def tile_kernel(meta, order, dst, col, codes, panel, totals):
-    rows = lax.broadcasted_iota(jnp.int32, (128, 128), 0)
+    rows = tile_rows()
     totals[...] = jnp.zeros_like(totals)
 
     def turn(i, _):
@@ -238,7 +257,8 @@
 SMEM = pl.BlockSpec(memory_space=pltpu.SMEM)
 VMEM = pl.BlockSpec(memory_space=pltpu.VMEM)
 HBM = pl.BlockSpec(memory_space=pl.ANY)
-PARAMS = pltpu.CompilerParams(vmem_limit_bytes=48 * 1024 * 1024)
+PARAMS = pltpu.CompilerParams(vmem_limit_bytes=16 * 1024 * 1024)
+WIDE_PARAMS = pltpu.CompilerParams(vmem_limit_bytes=48 * 1024 * 1024)
 
 
 def cost(slots, products):
@@ -252,7 +272,7 @@
         out_shape=jax.ShapeDtypeStruct((row_blocks, 128, panel.shape[-1]), jnp.float32),
         in_specs=[SMEM] * 4 + [VMEM] * 2,
         out_specs=VMEM,
-        compiler_params=PARAMS,
+        compiler_params=WIDE_PARAMS,
     )(meta, order, dst, col, codes, panel)
 
 
@@ -412,13 +432,9 @@
                     concat_axis=0,
                     tiled=True,
                 )
-
-        feat = []
-        for pair in gather_pieces(features.reshape(per, 128, width), exchange):
-            rows = [pair]
-            for bit in bits_of("row"):
-                rows = rows + [[swap(x, "row", bit) for x in pair] for pair in rows]
-            feat += [x for pair in rows for x in pair]
+            return held
+
+        pairs = gather_pieces(features.reshape(per, 128, width), exchange)
         came = state["came"]
         spread = jnp.max(came[:, ROOM, ROOM:], axis=0)[None]
         for bit in bits_of("row"):
@@ -437,6 +453,15 @@
         line = (sources * stride + places).reshape(-1)
         order = place(pos, line, length + GROUP, ROOM + 1)
         cols = place(pos, col_there.reshape(-1), length + GROUP, 0)
+        last, order, cols, owner, turns = lax.optimization_barrier(
+            ([pair[1] for pair in pairs], order, cols, owner, turns)
+        )
+        feat = []
+        for pair in [[pair[0], x] for pair, x in zip(pairs, last)]:
+            rows = [pair]
+            for bit in bits_of("row"):
+                rows = rows + [[swap(x, "row", bit) for x in pair] for pair in rows]
+            feat += [x for pair in rows for x in pair]
         own = run_forward(
             turns.reshape(1),
             order,
@@ -467,22 +492,34 @@
     grad_own = jnp.where(pre > 0, cotangent.astype(jnp.float32), 0.0).astype(jnp.bfloat16)
     local_bias = jnp.sum(grad_own.astype(jnp.float32), axis=0)
     turned = jnp.swapaxes(grad_own.reshape(per, 128, width), 1, 2)
-    grad = [x for pair in gather_pieces(turned, build) for x in pair]
     local_weight = lax.dot_general(
         own[:, width:].astype(jnp.bfloat16),
         grad_own,
         (((0,), (0,)), ((), ())),
         preferred_element_type=jnp.float32,
     )
-    local = jnp.concatenate([local_weight, jnp.tile(local_bias[None], (8, 1))], axis=0)
+    total = jnp.concatenate([local_weight, jnp.tile(local_bias[None], (8, 1))], axis=0)
     steps = total_steps()
-    for axis, bit in steps[:-1]:
-        local = local + swap(local, axis, bit)
+    for step in steps[: n_row.bit_length() - 1]:
+        total = total_step(total, *step)
+    steps = steps[n_row.bit_length() - 1 :]
+
+    def beside(step, held):
+        build(step, held)
+        if step == 1:
+            later, state["total"] = lax.optimization_barrier((held, state["total"]))
+            for one in steps[:-1]:
+                state["total"] = total_step(state["total"], *one)
+            return later
+        return held
+
+    state["total"] = total
+    grad = [x for pair in gather_pieces(turned, beside) for x in pair]
+    grad, total = lax.optimization_barrier((grad, state["total"]))
+    total = total_step(total, *steps[-1])
     acc = run_backward(
         back_turns.reshape(1), back_src, back_owner, grad, state["dense"], col_blocks
     )
-    acc, local = lax.optimization_barrier((acc, local))
-    total = local + swap(local, *steps[-1])
     back = jnp.swapaxes(acc, 1, 2).reshape(col_blocks * 128, width)
     grad_proj = scatter_sum(
         jnp.stack(

time: 163 us -> 156 us (0.957)
  the two profiles are of different devices: /device:TPU:18 before, /device:TPU:11 now
where the time goes in v4:
time: 156 us; the launch traced here: 154 us
  starting transfers between devices  59.3 us (38%)
  Pallas kernels  42.5 us (27%)
  other arithmetic  19.5 us (12%)
  waiting for transfers between devices  17.8 us (11%)
  between operations  8.21 us (5%)
  local copies, waits for them, and re-layouts  4.34 us (3%)
  matrix products  2.04 us (1%)
    ppermute x29, starting transfers between devices, swap(): return lax.ppermute(x, axis, [(i, i ^ bit) for i in range(n)])  52.7 us
    ppermute x29, waiting for transfers between devices, swap(): return lax.ppermute(x, axis, [(i, i ^ bit) for i in range(n)])  17.8 us
    pallas_call x1, Pallas kernels, run_forward(): pl.pallas_call(functools.partial(forward_kernel, n), out_shape=jax.ShapeD...  17.3 us
    pallas_call x3, Pallas kernels, run_build(): pl.pallas_call(build_kernel, out_shape=jax.ShapeDtypeStruct((order.shape[...  14 us
    pallas_call x1, Pallas kernels, run_backward(): pl.pallas_call(functools.partial(backward_kernel, n), out_shape=jax.Shape...  9.47 us
    all_to_all x1, starting transfers between devices, exchange(): lax.all_to_all(packed.reshape(n_col, stride, 128), 'col', split_axis=0, c...  6.61 us
    reduce_sum x3, other arithmetic, place(): return jnp.sum(jnp.where(hit, value[None, :] - fill, 0), axis=1) + fill  3.39 us
  transfers between devices with their start and end apart: 30, of which 8 were waited for; matrix products, arithmetic and copies ran while one was open for 13% of the time, Pallas kernels for 16%

profile of v4, /device:TPU:11, one launch (start us, length us, event | category | flops | bytes accessed | tf_op | source)
XLA Modules:
  0.0 153.7 jit_solution(17853029069099216098)
XLA Ops:
  1.5 2.4 %collective-permute-start.4 = (bf16[1,2,128,128]{3,2,1,0:T(8,128)(2,1)S(1)}, bf16[1,2,128,128]{3,2,1,0:T(8,128)(2,1)S(1)}, u32[]{:S(2)}, u32[]{:S(2)}) collective-permute-start(bf16[1,2,128,128]{3,2,1,0:T(8,128)(2,1)S(1)} %bitcast.137), channel_id=1, source_target_pairs={{0,8},{1,9},{2,10},{3,11},{4,12},{5,13},{6,14},{7,15},{8,0},{9,1},... | collective-permute-start | bytes 196616 | tf_op jit(solution)/shard_map/ppermute | solution.py:13
  11.1 1.7 %shard_map.120 = s32[1152,128]{1,0:T(8,128)} custom-call(s32[1]{0:T(128)} %bitcast.16.meta, s32[512]{0:T(512)S(1)} %get-tuple-element.144.pos, s32[520,128]{1,0:T(8,128)S(1)} %pad.5.codes, s32[16,128]{1,0:T(8,128)S(1)} %concatenate.51.labels, bf16[2,2,128,128]{3,2,1,0:T(8,128)(2,1)S(1)} %pad_maximum_fusion.7.after), custom_call_target="tpu_custom_call" | custom-call | tf_op jit(solution)/shard_map/pallas_call | solution.py:281
  12.8 6.6 %all-to-all-start = ((s32[16,72,128]{2,1,0:T(8,128)}), s32[16,72,128]{2,1,0:T(8,128)S(1)}, u32[]{:S(2)}, u32[]{:S(2)}) async-start(s32[16,72,128]{2,1,0:T(8,128)} %bitcast.21), calls=%async_computation | async-start | bytes 1179648 | tf_op jit(solution)/shard_map/all_to_all | solution.py:428
  24.5 7.2 %collective-permute-done.6 = bf16[2,2,128,128]{3,2,1,0:T(8,128)(2,1)S(1)} collective-permute-done((bf16[2,2,128,128]{3,2,1,0:T(8,128)(2,1)S(1)}, bf16[2,2,128,128]{3,2,1,0:T(8,128)(2,1)S(1)}, u32[]{:S(2)}, u32[]{:S(2)}) %collective-permute-start.6) | collective-permute-done | bytes 131104 | tf_op jit(solution)/shard_map/ppermute | solution.py:13
  33.0 1.5 collective-permute-done.10
  37.8 2.4 %collective-permute-done.11 = bf16[4,2,128,128]{3,2,1,0:T(8,128)(2,1)S(1)} collective-permute-done((bf16[4,2,128,128]{3,2,1,0:T(8,128)(2,1)S(1)}, bf16[4,2,128,128]{3,2,1,0:T(8,128)(2,1)S(1)}, u32[]{:S(2)}, u32[]{:S(2)}) %collective-permute-start.11) | collective-permute-done | bytes 262176 | tf_op jit(solution)/shard_map/ppermute | solution.py:13
  40.2 1.4 collective-permute-start.12
  41.6 6.0 %collective-permute-start.13 = (bf16[16,128,128]{2,1,0:T(8,128)(2,1)S(1)}, bf16[16,128,128]{2,1,0:T(8,128)(2,1)S(1)}, u32[]{:S(2)}, u32[]{:S(2)}) collective-permute-start(bf16[16,128,128]{2,1,0:T(8,128)(2,1)S(1)} %bitcast.114), channel_id=1, source_target_pairs={{0,16},{16,0},{1,17},{17,1},{2,18},{18,2},{3,19},{19,3},{4,20},{20... | collective-permute-start | bytes 1572872 | tf_op jit(solution)/shard_map/ppermute | solution.py:13
  55.6 2.0 %select_reduce_fusion = (s32[1064]{0:T(1024)S(1)}, s32[1064]{0:T(1024)S(1)}) fusion(s32[1024]{0:T(1024)} %get-tuple-element.142, s32[1024]{0:T(1024)S(1)} %add_select_fusion.7, s32[1024]{0:T(1024)S(1)} %sub.112), kind=kLoop, calls=%fused_computation.23 | loop fusion | flops 5445552 | bytes 20800 | tf_op jit(solution)/shard_map/reduce_sum | solution.py:365
  62.8 17.3 %shard_map.121 = f32[4,128,256]{2,1,0:T(8,128)} custom-call(s32[1]{0:T(128)} %bitcast.26.meta, s32[1064]{0:T(1024)S(1)} %broadcast_add_fusion.order, s32[1064]{0:T(1024)S(1)} %get-tuple-element.56.col, s32[132]{0:T(256)S(1)} %broadcast_minimum_fusion.owner, s32[1152,128]{1,0:T(8,128)S(1)} %bitcast.113, bf16[128,128]{1,0:T(8,128)(2,1)S(1)} %copy-done.2, ...), custom_call_target="tpu_custom_call" | custom-call | flops 35701915648 | bytes 34865152 | tf_op jit(solution)/shard_map/pallas_call | solution.py:310
  81.1 1.7 %convert_reduce_fusion.3 = (f32[128]{0:T(128)S(1)}, bf16[512,128]{1,0:T(8,128)(2,1)S(1)}, bf16[512,128]{1,0:T(8,128)(2,1)}) fusion(bf16[512,128]{1,0:T(8,128)(2,1)S(1)} %copy-done.1, f32[128]{0:T(128)S(1)} %copy-done.5, f32[512,256]{1,0:T(8,128)} %get-tuple-element.157), kind=kLoop, calls=%fused_computation.55 | loop fusion | flops 589696 | bytes 656384 | tf_op jit(solution)/shard_map/reduce_sum | solution.py:493
  86.5 2.8 %collective-permute-start.21 = (f32[136,128]{1,0:T(8,128)S(1)}, f32[136,128]{1,0:T(8,128)S(1)}, u32[]{:S(2)}, u32[]{:S(2)}) collective-permute-start(f32[136,128]{1,0:T(8,128)S(1)} %pad_maximum_fusion.11), channel_id=1, source_target_pairs={{0,16},{16,0},{1,17},{17,1},{2,18},{18,2},{3,19},{19,3},{4,20},{20... | collective-permute-start | bytes 208904 | tf_op jit(solution)/shard_map/ppermute | solution.py:13
  89.4 2.0 %collective-permute-start.18 = (bf16[2,2,128,128]{3,2,1,0:T(8,128)(2,1)S(1)}, bf16[2,2,128,128]{3,2,1,0:T(8,128)(2,1)S(1)}, u32[]{:S(2)}, u32[]{:S(2)}) collective-permute-start(bf16[2,2,128,128]{3,2,1,0:T(8,128)(2,1)S(1)} %pad_maximum_fusion.9.refs_0_), channel_id=1, source_target_pairs={{0,4},{1,5},{2,6},{3,7},{4,0},{5,1},{6,2},{7,3},{8,12},{9,13},{10,... | collective-permute-start | bytes 393224 | tf_op jit(solution)/shard_map/ppermute | solution.py:13
  92.6 3.4 %shard_map.122.refs_2_ = bf16[576,128,128]{2,1,0:T(8,128)(2,1)S(1)} custom-call(s32[2]{0:T(128)S(1)} %pad_add_fusion.2.meta, s32[576]{0:T(1024)S(1)} %broadcast_add_fusion.1.order, s32[520,128]{1,0:T(8,128)S(1)} %pad.5.codes, bf16[2,2,128,128]{3,2,1,0:T(8,128)(2,1)S(1)} %pad_maximum_fusion.9.refs_0_, bf16[2,2,128,128]{3,2,1,0:T(8,128)(2,1)S(1)} %pad_maximum_fusion.10.refs_1_), custom_call_target="tpu_custom_call" | custom-call | flops 4831838208 | bytes 18874368 | tf_op jit(solution)/shard_map/pallas_call | solution.py:292
  96.1 2.1 %collective-permute-done.20 = bf16[2,2,128,128]{3,2,1,0:T(8,128)(2,1)S(1)} collective-permute-done((bf16[2,2,128,128]{3,2,1,0:T(8,128)(2,1)S(1)}, bf16[2,2,128,128]{3,2,1,0:T(8,128)(2,1)S(1)}, u32[]{:S(2)}, u32[]{:S(2)}) %collective-permute-start.20) | collective-permute-done | bytes 131104 | tf_op jit(solution)/shard_map/ppermute | solution.py:13
  98.4 3.5 %collective-permute-start.26 = (f32[136,128]{1,0:T(8,128)S(1)}, f32[136,128]{1,0:T(8,128)S(1)}, u32[]{:S(2)}, u32[]{:S(2)}) collective-permute-start(f32[136,128]{1,0:T(8,128)S(1)} %fusion.51), channel_id=1, source_target_pairs={{0,8},{1,9},{2,10},{3,11},{4,12},{5,13},{6,14},{7,15},{8,0},{9,1},... | collective-permute-start | bytes 208904 | tf_op jit(solution)/shard_map/ppermute | solution.py:13
  101.9 1.6 %collective-permute-start.23 = (bf16[4,2,128,128]{3,2,1,0:T(8,128)(2,1)S(1)}, bf16[4,2,128,128]{3,2,1,0:T(8,128)(2,1)S(1)}, u32[]{:S(2)}, u32[]{:S(2)}) collective-permute-start(bf16[4,2,128,128]{3,2,1,0:T(8,128)(2,1)S(1)} %pad_maximum_fusion.6.refs_1_), channel_id=1, source_target_pairs={{0,1},{1,0},{2,3},{3,2},{4,5},{5,4},{6,7},{7,6},{8,9},{9,8},{10,11... | collective-permute-start | bytes 786440 | tf_op jit(solution)/shard_map/ppermute | solution.py:13
  103.5 3.8 %shard_map.123.refs_2_ = bf16[576,128,128]{2,1,0:T(8,128)(2,1)S(1)} custom-call(s32[2]{0:T(128)S(1)} %get-tuple-element.156.meta, s32[576]{0:T(1024)S(1)} %broadcast_add_fusion.1.order, s32[520,128]{1,0:T(8,128)S(1)} %pad.5.codes, bf16[4,2,128,128]{3,2,1,0:T(8,128)(2,1)S(1)} %pad_maximum_fusion.5.refs_0_, ...), custom_call_target="tpu_custom_call", output_to_operand_aliasing={{}: (5, {})} | custom-call | flops 4831838208 | bytes 18874368 | tf_op jit(solution)/shard_map/pallas_call | solution.py:292
  107.4 1.8 %collective-permute-start.24 = (bf16[8,2,128,128]{3,2,1,0:T(8,128)(2,1)S(1)}, bf16[8,2,128,128]{3,2,1,0:T(8,128)(2,1)S(1)}, u32[]{:S(2)}, u32[]{:S(2)}) collective-permute-start(bf16[8,2,128,128]{3,2,1,0:T(8,128)(2,1)S(1)} %constant_dynamic-update-slice_fusion.refs_0_), channel_id=1, source_target_pairs={{0,1},{1,0},{2,3},{3,2},{4,5},{5,4},{6,7},{7,6},{8,9},{9,8},{10,11... | collective-permute-start | bytes 1572872 | tf_op jit(solution)/shard_map/ppermute | solution.py:13
  109.3 6.8 %shard_map.124.dense = bf16[576,128,128]{2,1,0:T(8,128)(2,1)S(1)} custom-call(s32[2]{0:T(128)S(1)} %get-tuple-element.155.meta, s32[576]{0:T(1024)S(1)} %broadcast_add_fusion.1.order, s32[520,128]{1,0:T(8,128)S(1)} %pad.5.codes, bf16[8,2,128,128]{3,2,1,0:T(8,128)(2,1)S(1)} %constant_dynamic-update-slice_fusion.refs_0_, ...), custom_call_target="tpu_custom_call", output_to_operand_aliasing={{}: (5, {})} | custom-call | flops 4831838208 | bytes 18874368 | tf_op jit(solution)/shard_map/pallas_call | solution.py:292
  116.1 2.9 %collective-permute-done.24 = bf16[8,2,128,128]{3,2,1,0:T(8,128)(2,1)S(1)} collective-permute-done((bf16[8,2,128,128]{3,2,1,0:T(8,128)(2,1)S(1)}, bf16[8,2,128,128]{3,2,1,0:T(8,128)(2,1)S(1)}, u32[]{:S(2)}, u32[]{:S(2)}) %collective-permute-start.24) | collective-permute-done | bytes 524320 | tf_op jit(solution)/shard_map/ppermute | solution.py:13
  119.2 4.0 %collective-permute-start.32 = (f32[136,128]{1,0:T(8,128)S(1)}, f32[136,128]{1,0:T(8,128)S(1)}, u32[]{:S(2)}, u32[]{:S(2)}) collective-permute-start(f32[136,128]{1,0:T(8,128)S(1)} %add_add_fusion.1), channel_id=1, source_target_pairs={{0,3},{1,2},{2,1},{3,0},{4,7},{5,6},{6,5},{7,4},{8,11},{9,10},{10,... | collective-permute-start | bytes 208904 | tf_op jit(solution)/shard_map/ppermute | solution.py:13
  123.2 9.5 %shard_map.125 = f32[8,128,128]{2,1,0:T(8,128)S(1)} custom-call(s32[1]{0:T(128)} %bitcast.30.meta, s32[576]{0:T(1024)S(1)} %get-tuple-element.123.src, s32[72]{0:T(128)S(1)} %broadcast_minimum_fusion.1.owner, bf16[576,128,128]{2,1,0:T(8,128)(2,1)S(1)} %shard_map.124.dense, bf16[16,128,128]{2,1,0:T(8,128)(2,1)S(1)} %bitcast.112, ...), custom_call_target="tpu_custom_call" | custom-call | flops 9663676416 | bytes 18874368 | tf_op jit(solution)/shard_map/pallas_call | solution.py:329
  133.0 18.6 %collective-permute-start.29 = (f32[1,512,128]{2,1,0:T(8,128)S(1)}, f32[1,512,128]{2,1,0:T(8,128)S(1)}, u32[]{:S(2)}, u32[]{:S(2)}) collective-permute-start(f32[1,512,128]{2,1,0:T(8,128)S(1)} %slice_bitcast_fusion.8), channel_id=1, source_target_pairs={{0,16},{16,0},{1,17},{17,1},{2,18},{18,2},{3,19},{19,3},{4,20},{20... | collective-permute-start | bytes 786440 | tf_op jit(solution)/shard_map/ppermute | solution.py:13
  (138 shorter events, 32.5 us)
Async XLA Ops:
  1.5 9.5 %collective-permute-start.4 = (bf16[1,2,128,128]{3,2,1,0:T(8,128)(2,1)S(1)}, bf16[1,2,128,128]{3,2,1,0:T(8,128)(2,1)S(1)}, u32[]{:S(2)}, u32[]{:S(2)}) collective-permute-start(bf16[1,2,128,128]{3,2,1,0:T(8,128)(2,1)S(1)} %bitcast.137), channel_id=1, source_target_pairs={{0,8},{1,9},{2,10},{3,11},{4,12},{5,13},{6,14},{7,15},{8,0},{9,1},... | collective-permute-start | bytes 196616 | tf_op jit(solution)/shard_map/ppermute | solution.py:13
  3.9 15.9 %collective-permute-start.9 = (bf16[1,2,128,128]{3,2,1,0:T(8,128)(2,1)S(1)}, bf16[1,2,128,128]{3,2,1,0:T(8,128)(2,1)S(1)}, u32[]{:S(2)}, u32[]{:S(2)}) collective-permute-start(bf16[1,2,128,128]{3,2,1,0:T(8,128)(2,1)S(1)} %bitcast.133), channel_id=1, source_target_pairs={{0,8},{1,9},{2,10},{3,11},{4,12},{5,13},{6,14},{7,15},{8,0},{9,1},... | collective-permute-start | bytes 196616 | tf_op jit(solution)/shard_map/ppermute | solution.py:13
  12.8 34.8 %all-to-all-start = ((s32[16,72,128]{2,1,0:T(8,128)}), s32[16,72,128]{2,1,0:T(8,128)S(1)}, u32[]{:S(2)}, u32[]{:S(2)}) async-start(s32[16,72,128]{2,1,0:T(8,128)} %bitcast.21), calls=%async_computation | async-start | bytes 1179648 | tf_op jit(solution)/shard_map/all_to_all | solution.py:428
  19.5 12.3 %collective-permute-start.6 = (bf16[2,2,128,128]{3,2,1,0:T(8,128)(2,1)S(1)}, bf16[2,2,128,128]{3,2,1,0:T(8,128)(2,1)S(1)}, u32[]{:S(2)}, u32[]{:S(2)}) collective-permute-start(bf16[2,2,128,128]{3,2,1,0:T(8,128)(2,1)S(1)} %pad_maximum_fusion.7.after), channel_id=1, source_target_pairs={{0,4},{1,5},{2,6},{3,7},{4,0},{5,1},{6,2},{7,3},{8,12},{9,13},{10,... | collective-permute-start | bytes 393224 | tf_op jit(solution)/shard_map/ppermute | solution.py:13
  19.8 14.7 %collective-permute-start.10 = (bf16[2,2,128,128]{3,2,1,0:T(8,128)(2,1)S(1)}, bf16[2,2,128,128]{3,2,1,0:T(8,128)(2,1)S(1)}, u32[]{:S(2)}, u32[]{:S(2)}) collective-permute-start(bf16[2,2,128,128]{3,2,1,0:T(8,128)(2,1)S(1)} %pad_maximum_fusion.8), channel_id=1, source_target_pairs={{0,4},{1,5},{2,6},{3,7},{4,0},{5,1},{6,2},{7,3},{8,12},{9,13},{10,... | collective-permute-start | bytes 393224 | tf_op jit(solution)/shard_map/ppermute | solution.py:13
  31.8 5.6 %collective-permute-start.7 = (bf16[4,2,128,128]{3,2,1,0:T(8,128)(2,1)S(1)}, bf16[4,2,128,128]{3,2,1,0:T(8,128)(2,1)S(1)}, u32[]{:S(2)}, u32[]{:S(2)}) collective-permute-start(bf16[4,2,128,128]{3,2,1,0:T(8,128)(2,1)S(1)} %pad_maximum_fusion.3), channel_id=1, source_target_pairs={{0,2},{1,3},{2,0},{3,1},{4,6},{5,7},{6,4},{7,5},{8,10},{9,11},{10,... | collective-permute-start | bytes 786440 | tf_op jit(solution)/shard_map/ppermute | solution.py:13
  37.4 20.2 %collective-permute-start.8 = (bf16[8,2,128,128]{3,2,1,0:T(8,128)(2,1)S(1)}, bf16[8,2,128,128]{3,2,1,0:T(8,128)(2,1)S(1)}, u32[]{:S(2)}, u32[]{:S(2)}) collective-permute-start(bf16[8,2,128,128]{3,2,1,0:T(8,128)(2,1)S(1)} %pad_maximum_fusion.1), channel_id=1, source_target_pairs={{0,1},{1,0},{2,3},{3,2},{4,5},{5,4},{6,7},{7,6},{8,9},{9,8},{10,11... | collective-permute-start | bytes 1572872 | tf_op jit(solution)/shard_map/ppermute | solution.py:13
  40.2 17.4 %collective-permute-start.12 = (bf16[8,2,128,128]{3,2,1,0:T(8,128)(2,1)S(1)}, bf16[8,2,128,128]{3,2,1,0:T(8,128)(2,1)S(1)}, u32[]{:S(2)}, u32[]{:S(2)}) collective-permute-start(bf16[8,2,128,128]{3,2,1,0:T(8,128)(2,1)S(1)} %pad_maximum_fusion.2), channel_id=1, source_target_pairs={{0,2},{1,3},{2,0},{3,1},{4,6},{5,7},{6,4},{7,5},{8,10},{9,11},{10,... | collective-permute-start | bytes 1572872 | tf_op jit(solution)/shard_map/ppermute | solution.py:13
  41.6 21.2 %collective-permute-start.13 = (bf16[16,128,128]{2,1,0:T(8,128)(2,1)S(1)}, bf16[16,128,128]{2,1,0:T(8,128)(2,1)S(1)}, u32[]{:S(2)}, u32[]{:S(2)}) collective-permute-start(bf16[16,128,128]{2,1,0:T(8,128)(2,1)S(1)} %bitcast.114), channel_id=1, source_target_pairs={{0,16},{16,0},{1,17},{17,1},{2,18},{18,2},{3,19},{19,3},{4,20},{20... | collective-permute-start | bytes 1572872 | tf_op jit(solution)/shard_map/ppermute | solution.py:13
  47.6 15.2 %collective-permute-start.15 = (bf16[16,128,128]{2,1,0:T(8,128)(2,1)S(1)}, bf16[16,128,128]{2,1,0:T(8,128)(2,1)}, u32[]{:S(2)}, u32[]{:S(2)}) collective-permute-start(bf16[16,128,128]{2,1,0:T(8,128)(2,1)S(1)} %bitcast.116), channel_id=1, source_target_pairs={{0,16},{16,0},{1,17},{17,1},{2,18},{18,2},{3,19},{19,3},{4,20},{20... | collective-permute-start | bytes 1572872 | tf_op jit(solution)/shard_map/ppermute | solution.py:13
  85.4 6.0 %collective-permute-start.19 = (bf16[1,2,128,128]{3,2,1,0:T(8,128)(2,1)S(1)}, bf16[1,2,128,128]{3,2,1,0:T(8,128)(2,1)S(1)}, u32[]{:S(2)}, u32[]{:S(2)}) collective-permute-start(bf16[1,2,128,128]{3,2,1,0:T(8,128)(2,1)S(1)} %get-tuple-element.137), channel_id=1, source_target_pairs={{0,8},{1,9},{2,10},{3,11},{4,12},{5,13},{6,14},{7,15},{8,0},{9,1},... | collective-permute-start | bytes 196616 | tf_op jit(solution)/shard_map/ppermute | solution.py:13
  86.5 9.5 %collective-permute-start.21 = (f32[136,128]{1,0:T(8,128)S(1)}, f32[136,128]{1,0:T(8,128)S(1)}, u32[]{:S(2)}, u32[]{:S(2)}) collective-permute-start(f32[136,128]{1,0:T(8,128)S(1)} %pad_maximum_fusion.11), channel_id=1, source_target_pairs={{0,16},{16,0},{1,17},{17,1},{2,18},{18,2},{3,19},{19,3},{4,20},{20... | collective-permute-start | bytes 208904 | tf_op jit(solution)/shard_map/ppermute | solution.py:13
  89.4 6.7 %collective-permute-start.18 = (bf16[2,2,128,128]{3,2,1,0:T(8,128)(2,1)S(1)}, bf16[2,2,128,128]{3,2,1,0:T(8,128)(2,1)S(1)}, u32[]{:S(2)}, u32[]{:S(2)}) collective-permute-start(bf16[2,2,128,128]{3,2,1,0:T(8,128)(2,1)S(1)} %pad_maximum_fusion.9.refs_0_), channel_id=1, source_target_pairs={{0,4},{1,5},{2,6},{3,7},{4,0},{5,1},{6,2},{7,3},{8,12},{9,13},{10,... | collective-permute-start | bytes 393224 | tf_op jit(solution)/shard_map/ppermute | solution.py:13
  91.4 6.8 %collective-permute-start.20 = (bf16[2,2,128,128]{3,2,1,0:T(8,128)(2,1)S(1)}, bf16[2,2,128,128]{3,2,1,0:T(8,128)(2,1)S(1)}, u32[]{:S(2)}, u32[]{:S(2)}) collective-permute-start(bf16[2,2,128,128]{3,2,1,0:T(8,128)(2,1)S(1)} %pad_maximum_fusion.10.refs_1_), channel_id=1, source_target_pairs={{0,4},{1,5},{2,6},{3,7},{4,0},{5,1},{6,2},{7,3},{8,12},{9,13},{10,... | collective-permute-start | bytes 393224 | tf_op jit(solution)/shard_map/ppermute | solution.py:13
  98.3 11.0 %collective-permute-start.27 = (f32[136,128]{1,0:T(8,128)S(1)}, f32[136,128]{1,0:T(8,128)S(1)}, u32[]{:S(2)}, u32[]{:S(2)}) collective-permute-start(f32[136,128]{1,0:T(8,128)S(1)} %fusion.51), channel_id=1, source_target_pairs={{0,4},{1,5},{2,6},{3,7},{4,0},{5,1},{6,2},{7,3},{8,12},{9,13},{10,... | collective-permute-start | bytes 208904 | tf_op jit(solution)/shard_map/ppermute | solution.py:13
  98.4 10.9 %collective-permute-start.28 = (f32[136,128]{1,0:T(8,128)S(1)}, f32[136,128]{1,0:T(8,128)S(1)}, u32[]{:S(2)}, u32[]{:S(2)}) collective-permute-start(f32[136,128]{1,0:T(8,128)S(1)} %fusion.51), channel_id=1, source_target_pairs={{0,12},{1,13},{2,14},{3,15},{4,8},{5,9},{6,10},{7,11},{8,4},{9,5},... | collective-permute-start | bytes 208904 | tf_op jit(solution)/shard_map/ppermute | solution.py:13
  98.4 10.8 %collective-permute-start.26 = (f32[136,128]{1,0:T(8,128)S(1)}, f32[136,128]{1,0:T(8,128)S(1)}, u32[]{:S(2)}, u32[]{:S(2)}) collective-permute-start(f32[136,128]{1,0:T(8,128)S(1)} %fusion.51), channel_id=1, source_target_pairs={{0,8},{1,9},{2,10},{3,11},{4,12},{5,13},{6,14},{7,15},{8,0},{9,1},... | collective-permute-start | bytes 208904 | tf_op jit(solution)/shard_map/ppermute | solution.py:13
  101.9 7.2 %collective-permute-start.23 = (bf16[4,2,128,128]{3,2,1,0:T(8,128)(2,1)S(1)}, bf16[4,2,128,128]{3,2,1,0:T(8,128)(2,1)S(1)}, u32[]{:S(2)}, u32[]{:S(2)}) collective-permute-start(bf16[4,2,128,128]{3,2,1,0:T(8,128)(2,1)S(1)} %pad_maximum_fusion.6.refs_1_), channel_id=1, source_target_pairs={{0,1},{1,0},{2,3},{3,2},{4,5},{5,4},{6,7},{7,6},{8,9},{9,8},{10,11... | collective-permute-start | bytes 786440 | tf_op jit(solution)/shard_map/ppermute | solution.py:13
  107.4 11.6 %collective-permute-start.24 = (bf16[8,2,128,128]{3,2,1,0:T(8,128)(2,1)S(1)}, bf16[8,2,128,128]{3,2,1,0:T(8,128)(2,1)S(1)}, u32[]{:S(2)}, u32[]{:S(2)}) collective-permute-start(bf16[8,2,128,128]{3,2,1,0:T(8,128)(2,1)S(1)} %constant_dynamic-update-slice_fusion.refs_0_), channel_id=1, source_target_pairs={{0,1},{1,0},{2,3},{3,2},{4,5},{5,4},{6,7},{7,6},{8,9},{9,8},{10,11... | collective-permute-start | bytes 1572872 | tf_op jit(solution)/shard_map/ppermute | solution.py:13
  109.2 9.9 %collective-permute-start.25 = (bf16[8,2,128,128]{3,2,1,0:T(8,128)(2,1)S(1)}, bf16[8,2,128,128]{3,2,1,0:T(8,128)(2,1)S(1)}, u32[]{:S(2)}, u32[]{:S(2)}) collective-permute-start(bf16[8,2,128,128]{3,2,1,0:T(8,128)(2,1)S(1)} %constant_dynamic-update-slice_fusion.2.refs_1_), channel_id=1, source_target_pairs={{0,2},{1,3},{2,0},{3,1},{4,6},{5,7},{6,4},{7,5},{8,10},{9,11},{10,... | collective-permute-start | bytes 1572872 | tf_op jit(solution)/shard_map/ppermute | solution.py:13
  119.1 32.6 %collective-permute-start.31 = (f32[136,128]{1,0:T(8,128)S(1)}, f32[136,128]{1,0:T(8,128)S(1)}, u32[]{:S(2)}, u32[]{:S(2)}) collective-permute-start(f32[136,128]{1,0:T(8,128)S(1)} %add_add_fusion.1), channel_id=1, source_target_pairs={{0,1},{1,0},{2,3},{3,2},{4,5},{5,4},{6,7},{7,6},{8,9},{9,8},{10,11... | collective-permute-start | bytes 208904 | tf_op jit(solution)/shard_map/ppermute | solution.py:13
  119.2 32.4 %collective-permute-start.32 = (f32[136,128]{1,0:T(8,128)S(1)}, f32[136,128]{1,0:T(8,128)S(1)}, u32[]{:S(2)}, u32[]{:S(2)}) collective-permute-start(f32[136,128]{1,0:T(8,128)S(1)} %add_add_fusion.1), channel_id=1, source_target_pairs={{0,3},{1,2},{2,1},{3,0},{4,7},{5,6},{6,5},{7,4},{8,11},{9,10},{10,... | collective-permute-start | bytes 208904 | tf_op jit(solution)/shard_map/ppermute | solution.py:13
  123.2 28.4 %collective-permute-start.30 = (f32[136,128]{1,0:T(8,128)S(1)}, f32[136,128]{1,0:T(8,128)S(1)}, u32[]{:S(2)}, u32[]{:S(2)}) collective-permute-start(f32[136,128]{1,0:T(8,128)S(1)} %add_add_fusion.1), channel_id=1, source_target_pairs={{0,2},{1,3},{2,0},{3,1},{4,6},{5,7},{6,4},{7,5},{8,10},{9,11},{10,... | collective-permute-start | bytes 208904 | tf_op jit(solution)/shard_map/ppermute | solution.py:13
  133.0 19.8 %collective-permute-start.29 = (f32[1,512,128]{2,1,0:T(8,128)S(1)}, f32[1,512,128]{2,1,0:T(8,128)S(1)}, u32[]{:S(2)}, u32[]{:S(2)}) collective-permute-start(f32[1,512,128]{2,1,0:T(8,128)S(1)} %slice_bitcast_fusion.8), channel_id=1, source_target_pairs={{0,16},{16,0},{1,17},{17,1},{2,18},{18,2},{3,19},{19,3},{4,20},{20... | collective-permute-start | bytes 786440 | tf_op jit(solution)/shard_map/ppermute | solution.py:13
  (11 other events, 106.5 us)
